TPU v7x, 32 devices: a whole 2x2x4 slice. The times are simulated.
32 devices in a mesh: dp: 4 (over z), seq: 4 (over x, core), head: 2 (over y).
Axes of the slice: x: 2, y: 2, z: 4, core: 2. Of those that a mesh axis runs over, the one named last changes fastest.
Arguments:
- queries: bfloat16 [4, 1440, 512], P('dp', 'seq', 'head'), may hold values from -40 to 40
- key_rows: bfloat16 [4, 1440, 256], P('dp', 'seq', 'head'), may hold values from -6 to 6
- value_rows: bfloat16 [4, 1440, 256], P('dp', 'seq', 'head'), may hold values from -6 to 6
- grad_out: bfloat16 [4, 1440, 512], P('dp', 'seq', 'head'), may hold values from -6 to 6
- doc_lengths: int32 [4, 4], P('dp'), may hold values from 2 to 1080, as said below
- dest_index: int32 [4, 1440], P('dp', 'seq'), may hold values from 0 to 3, as said below
Outputs:
- attended: bfloat16 [4, 1440, 512], P('dp', 'seq', 'head')
- query_grad: bfloat16 [4, 1440, 512], P('dp', 'seq', 'head')
- key_grad: bfloat16 [4, 1440, 256], P('dp', 'seq', 'head')
- value_grad: bfloat16 [4, 1440, 256], P('dp', 'seq', 'head')
Inputs may be any that keep to these rules, and one draw needn't show every extreme that they name: `dest_index`: within each loader sequence and each shard of 360 positions, every value 0 to 3 appears exactly 360 / 4 times. `doc_lengths`: each row holds 4 lengths that sum to 1440; the largest is exactly 1080.
All inputs are finite; a program needn't handle non-finite values.
Results may differ from a plain program's by a relative error of at most 0.0095.
Values may be sent and summed in bfloat16 or wider, within the bound.
No kernel may reach another device: no remote copies, remote signals or barrier semaphores. Data moves between devices by JAX's collectives and lax.ppermute only.
A program may use at most 64 MiB of HBM per device.

v0:
```python
import jax
import jax.numpy as jnp
from jax import lax
from jax.sharding import PartitionSpec as P

HEAD_DIM = 128
WINDOW = 1024


score_scale = 168.0 ** (-0.5)
neg_large = -1e30


def document_ids(lengths, positions):
    boundary = jnp.cumsum(lengths, dtype=jnp.int32)
    return jnp.sum((positions[:, None] >= boundary[None, :]).astype(jnp.int32), axis=1)


def local(queries, key_rows, value_rows, grad_out, doc_lengths, dest_index):
    row_count = queries.shape[1]
    peer_count = lax.axis_size("dp")
    group_rows = row_count // peer_count
    span_count = lax.axis_size("seq")
    shard_index = lax.axis_index("seq")
    query_cols = queries.shape[2]
    key_cols = key_rows.shape[2]
    local_rows = jnp.arange(row_count, dtype=jnp.int32)
    send_order = jnp.argsort(dest_index[0] * row_count + local_rows)
    back_order = jnp.argsort(send_order)

    def outgoing(values):
        return values[0][send_order].reshape(peer_count, group_rows, values.shape[2])

    def homeward(values):
        return values.reshape(peer_count, group_rows, values.shape[1])

    def settle(values):
        return values.reshape(row_count, values.shape[2])[back_order][None]

    arrived = (
        lax.all_to_all(outgoing(queries), "dp", split_axis=0, concat_axis=0, tiled=True),
        lax.all_to_all(outgoing(key_rows), "dp", split_axis=0, concat_axis=0, tiled=True),
        lax.all_to_all(outgoing(value_rows), "dp", split_axis=0, concat_axis=0, tiled=True),
        lax.all_to_all(outgoing(grad_out), "dp", split_axis=0, concat_axis=0, tiled=True),
    )
    query_here = arrived[0].reshape(row_count, query_cols)
    key_here = arrived[1].reshape(row_count, key_cols)
    value_here = arrived[2].reshape(row_count, key_cols)
    grad_here = arrived[3].reshape(row_count, query_cols)
    reach_back = min(span_count - 1, (WINDOW + row_count - 2) // row_count)
    context_rows = (reach_back + 1) * row_count
    lead_rows = reach_back * row_count
    skip_rows = max(0, lead_rows - (WINDOW - 1))
    used_rows = context_rows - skip_rows
    full_keys, full_values = (
        lax.all_gather(key_here, "seq", axis=0, tiled=True),
        lax.all_gather(value_here, "seq", axis=0, tiled=True),
    )
    blank_rows = jnp.zeros((lead_rows, key_cols), jnp.bfloat16)
    ctx_keys = lax.dynamic_slice_in_dim(
        jnp.concatenate([blank_rows, full_keys], axis=0),
        shard_index * row_count + skip_rows,
        used_rows,
        0,
    )
    ctx_values = lax.dynamic_slice_in_dim(
        jnp.concatenate([blank_rows, full_values], axis=0),
        shard_index * row_count + skip_rows,
        used_rows,
        0,
    )
    seq_length = row_count * span_count
    all_docs = document_ids(doc_lengths[0], jnp.arange(seq_length, dtype=jnp.int32))
    padded_docs = jnp.concatenate([jnp.full((lead_rows,), -1, jnp.int32), all_docs])
    query_docs = lax.dynamic_slice_in_dim(all_docs, shard_index * row_count, row_count, 0)
    key_docs = lax.dynamic_slice_in_dim(
        padded_docs, shard_index * row_count + skip_rows, used_rows, 0
    )
    distance = (lead_rows - skip_rows + local_rows)[:, None] - jnp.arange(
        used_rows, dtype=jnp.int32
    )[None, :]
    allowed = (query_docs[:, None] == key_docs[None, :]) & (distance >= 0) & (distance < WINDOW)
    query_three = query_here.reshape(row_count, 2, HEAD_DIM)
    key_group = ctx_keys
    value_group = ctx_values
    scores = (
        jnp.einsum("qhd,kd->hqk", query_three, key_group, preferred_element_type=jnp.float32)
        * score_scale
    )
    scores = jnp.where(allowed[None], scores, neg_large)
    row_peak = jnp.max(scores, axis=2, keepdims=True)
    weights = jnp.where(allowed[None], jnp.exp(scores - row_peak), 0.0)
    prob_rows = weights / jnp.sum(weights, axis=2, keepdims=True)
    prob_low = prob_rows.astype(jnp.bfloat16)
    mixed_rows = jnp.einsum(
        "hqk,kd->qhd", prob_low, value_group, preferred_element_type=jnp.float32
    )
    head_outs = mixed_rows.astype(jnp.bfloat16).reshape(row_count, 2 * HEAD_DIM)
    saved_terms = (query_three, key_group, value_group, prob_rows, prob_low)
    query_three, key_group, value_group, prob_rows, prob_low = saved_terms
    grad_three = grad_here.reshape(row_count, 2, HEAD_DIM)
    value_parts = [
        jnp.einsum("hqk,qhd->kd", prob_low, grad_three, preferred_element_type=jnp.float32)
    ]
    prob_grad = jnp.einsum(
        "qhd,kd->hqk", grad_three, value_group, preferred_element_type=jnp.float32
    )
    center = jnp.sum(prob_rows * prob_grad, axis=2, keepdims=True)
    dscore = (prob_rows * (prob_grad - center) * score_scale).astype(jnp.bfloat16)
    query_grads = (
        jnp.einsum("hqk,kd->qhd", dscore, key_group, preferred_element_type=jnp.float32)
        .astype(jnp.bfloat16)
        .reshape(row_count, 2 * HEAD_DIM)
    )
    key_parts = [jnp.einsum("hqk,qhd->kd", dscore, query_three, preferred_element_type=jnp.float32)]
    front_zeros = jnp.zeros((skip_rows, key_cols), jnp.float32)
    key_low = lax.optimization_barrier(
        jnp.concatenate([front_zeros] + key_parts, axis=0).astype(jnp.bfloat16)
    )
    value_low = lax.optimization_barrier(
        jnp.concatenate([front_zeros] + value_parts, axis=0).astype(jnp.bfloat16)
    )
    zero_rows = jnp.zeros((lead_rows + seq_length, key_cols), jnp.float32)

    def spread(portion):
        placed = lax.dynamic_update_slice_in_dim(
            zero_rows, portion.astype(jnp.float32), shard_index * row_count, 0
        )
        return placed[lead_rows:]

    key_sum, value_sum = (
        lax.psum_scatter(
            spread(key_low).astype(jnp.bfloat16), "seq", scatter_dimension=0, tiled=True
        ).astype(jnp.float32),
        lax.psum_scatter(
            spread(value_low).astype(jnp.bfloat16), "seq", scatter_dimension=0, tiled=True
        ).astype(jnp.float32),
    )
    key_grad = key_sum.astype(jnp.bfloat16)
    value_grad = value_sum.astype(jnp.bfloat16)
    home_rows = (
        lax.all_to_all(homeward(head_outs), "dp", split_axis=0, concat_axis=0, tiled=True),
        lax.all_to_all(homeward(query_grads), "dp", split_axis=0, concat_axis=0, tiled=True),
        lax.all_to_all(homeward(key_grad), "dp", split_axis=0, concat_axis=0, tiled=True),
        lax.all_to_all(homeward(value_grad), "dp", split_axis=0, concat_axis=0, tiled=True),
    )
    return (settle(home_rows[0]), settle(home_rows[1]), settle(home_rows[2]), settle(home_rows[3]))


def solution(mesh):
    return jax.shard_map(
        local,
        mesh=mesh,
        in_specs=(
            P("dp", "seq", "head"),
            P("dp", "seq", "head"),
            P("dp", "seq", "head"),
            P("dp", "seq", "head"),
            P("dp", None),
            P("dp", "seq"),
        ),
        out_specs=(
            P("dp", "seq", "head"),
            P("dp", "seq", "head"),
            P("dp", "seq", "head"),
            P("dp", "seq", "head"),
        ),
        check_vma=False,
    )
```

profile of v0, /device:TPU:0, one launch (start us, length us, event | category | flops | bytes accessed | tf_op | source)
XLA Modules:
  0.0 147.9 jit_solution(16045399902807172635)
XLA Ops:
  8.0 3.8 %sort.31 = (s32[360]{0:T(512)}, s32[360]{0:T(512)S(1)}) sort(s32[360]{0:T(512)S(1)} %iota_add_fusion.1, s32[360]{0:T(512)S(1)} %iota.29), dimensions={0}, to_apply=%region_0.0 | sort | flops 3240 | bytes 5760 | tf_op jit(solution)/shard_map/jit(argsort)/sort | solution.py:28
  11.7 2.1 %gather_fusion = bf16[360,128]{1,0:T(8,128)(2,1)S(1)} fusion(bf16[360,128]{1,0:T(8,128)(2,1)} %bitcast.75, s32[1024]{0:T(1024)S(1)} %pad_clamp_fusion.1), kind=kCustom, calls=%fused_computation | custom fusion | bytes 185760 | tf_op jit(solution)/shard_map/gather | solution.py:32
  14.5 6.3 %all-to-all-start = ((bf16[4,90,128]{2,1,0:T(8,128)(2,1)}), bf16[4,90,128]{2,1,0:T(8,128)(2,1)S(1)}, u32[]{:S(2)}, u32[]{:S(2)}) async-start(bf16[4,90,128]{2,1,0:T(8,128)(2,1)} %reshape.127), calls=%async_computation | async-start | bytes 196608 | tf_op jit(solution)/shard_map/all_to_all | solution.py:43
  21.7 2.1 %gather_fusion.1 = bf16[360,128]{1,0:T(8,128)(2,1)S(1)} fusion(bf16[360,128]{1,0:T(8,128)(2,1)} %bitcast.76, s32[1024]{0:T(1024)S(1)} %pad_clamp_fusion.1), kind=kCustom, calls=%fused_computation.1 | custom fusion | bytes 185760 | tf_op jit(solution)/shard_map/gather | solution.py:32
  24.6 2.0 %all-to-all-done = bf16[4,90,128]{2,1,0:T(8,128)(2,1)S(1)} async-done(((bf16[4,90,128]{2,1,0:T(8,128)(2,1)}), bf16[4,90,128]{2,1,0:T(8,128)(2,1)S(1)}, u32[]{:S(2)}, u32[]{:S(2)}) %all-to-all-start) | async-done | bytes 92192 | tf_op jit(solution)/shard_map/all_to_all | solution.py:43
  26.6 3.3 %all-to-all-start.1 = ((bf16[4,90,128]{2,1,0:T(8,128)(2,1)}), bf16[4,90,128]{2,1,0:T(8,128)(2,1)S(1)}, u32[]{:S(2)}, u32[]{:S(2)}) async-start(bf16[4,90,128]{2,1,0:T(8,128)(2,1)} %reshape.131), calls=%async_computation.1 | async-start | bytes 196608 | tf_op jit(solution)/shard_map/all_to_all | solution.py:42
  30.8 2.0 %gather_fusion.2 = bf16[360,256]{1,0:T(8,128)(2,1)S(1)} fusion(bf16[360,256]{1,0:T(8,128)(2,1)S(1)} %bitcast.73, s32[1024]{0:T(1024)S(1)} %pad_clamp_fusion.1), kind=kCustom, calls=%fused_computation.2 | custom fusion | bytes 370080 | tf_op jit(solution)/shard_map/gather | solution.py:32
  33.5 2.0 %gather_fusion.4 = bf16[360,256]{1,0:T(8,128)(2,1)S(1)} fusion(bf16[360,256]{1,0:T(8,128)(2,1)S(1)} %bitcast.74, s32[1024]{0:T(1024)S(1)} %pad_clamp_fusion.1), kind=kCustom, calls=%fused_computation.4 | custom fusion | bytes 370080 | tf_op jit(solution)/shard_map/gather | solution.py:32
  36.4 5.1 %all-to-all-start.4 = ((bf16[4,90,256]{2,1,0:T(8,128)(2,1)}), bf16[4,90,256]{2,1,0:T(8,128)(2,1)S(1)}, u32[]{:S(2)}, u32[]{:S(2)}) async-start(bf16[4,90,256]{2,1,0:T(8,128)(2,1)} %reshape.135), calls=%async_computation.4 | async-start | bytes 393216 | tf_op jit(solution)/shard_map/all_to_all | solution.py:44
  41.5 6.3 %all_gather.6 = bf16[1440,128]{1,0:T(8,128)(2,1)S(1)} all-gather(bf16[360,128]{1,0:T(8,128)(2,1)S(1)} %reshape.128), channel_id=1, replica_groups=mesh['dp'=4,'seq'=4,'head'=2] {'seq'}, dimensions={0}, use_global_device_ids=true | all-gather | bytes 460800 | tf_op jit(solution)/shard_map/all_gather | solution.py:57
  47.8 6.4 %all_gather.7 = bf16[1440,128]{1,0:T(8,128)(2,1)S(1)} all-gather(bf16[360,128]{1,0:T(8,128)(2,1)S(1)} %reshape.132), channel_id=1, replica_groups=mesh['dp'=4,'seq'=4,'head'=2] {'seq'}, dimensions={0}, use_global_device_ids=true | all-gather | bytes 460800 | tf_op jit(solution)/shard_map/all_gather | solution.py:56
  54.2 5.1 %all-to-all-start.2 = ((bf16[4,90,256]{2,1,0:T(8,128)(2,1)}), bf16[4,90,256]{2,1,0:T(8,128)(2,1)S(1)}, u32[]{:S(2)}, u32[]{:S(2)}) async-start(bf16[4,90,256]{2,1,0:T(8,128)(2,1)} %reshape.133), calls=%async_computation.2 | async-start | bytes 393216 | tf_op jit(solution)/shard_map/all_to_all | solution.py:41
  59.4 3.0 %fusion.23 = f32[1383,360,2]{0,1,2:T(8,128)} fusion(s32[]{:T(128)S(6)} %select_n.32, bf16[1440,128]{1,0:T(8,128)(2,1)S(1)} %all_gather.6, bf16[360,2,128]{2,1,0:T(2,128)(2,1)S(1)} %reshape_reshape.14), kind=kOutput, calls=%fused_computation.44 | convolution fusion | flops 254914560 | bytes 4536004 | tf_op jit(solution)/shard_map/qhd,kd->hqk/dot_general | solution.py:105
  62.4 4.9 %all-to-all-done.2 = bf16[4,90,256]{2,1,0:T(8,128)(2,1)S(1)} async-done(((bf16[4,90,256]{2,1,0:T(8,128)(2,1)}), bf16[4,90,256]{2,1,0:T(8,128)(2,1)S(1)}, u32[]{:S(2)}, u32[]{:S(2)}) %all-to-all-start.2) | async-done | bytes 184352 | tf_op jit(solution)/shard_map/all_to_all | solution.py:41
  67.3 4.4 %fusion.57 = (f32[2,360]{1,0:T(2,128)S(1)}, f32[2,360,1383]{2,1,0:T(8,128)}) fusion(pred[360,1383]{1,0:T(8,128)(4,1)S(1)} %fusion.11, s32[]{:T(128)S(6)} %select_n.32, bf16[1440,128]{1,0:T(8,128)(2,1)S(1)} %all_gather.7, bf16[360,2,128]{2,1,0:T(2,128)(2,1)S(1)} %reshape_reshape.12), kind=kOutput, calls=%fused_computation.77 | convolution fusion | flops 259894736 | bytes 5552644 | tf_op jit(solution)/shard_map/sub | solution.py:92
  71.7 10.5 %fusion.6 = bf16[1383,128]{1,0:T(8,128)(2,1)S(1)} fusion(f32[1383,360,2]{0,1,2:T(8,128)} %fusion.23, bf16[360,2,128]{2,1,0:T(2,128)(2,1)S(1)} %reshape_reshape.12, f32[2,360,1383]{2,1,0:T(8,128)} %get-tuple-element.9, f32[2,360]{1,0:T(2,128)S(1)} %get-tuple-element.8), kind=kOutput, calls=%fused_computation.20 | convolution fusion | flops 262064000 | bytes 8507328 | tf_op jit(solution)/shard_map/hqk,qhd->kd/dot_general | solution.py:115
  83.6 3.1 %fusion.7 = bf16[1383,128]{1,0:T(8,128)(2,1)S(1)} fusion(bf16[360,2,128]{2,1,0:T(2,128)(2,1)S(1)} %reshape_reshape.14, f32[2,360,1383]{2,1,0:T(8,128)} %get-tuple-element.9, f32[2,360]{1,0:T(2,128)S(1)} %get-tuple-element.8), kind=kOutput, calls=%fused_computation.21 | convolution fusion | flops 257083104 | bytes 4524288 | tf_op jit(solution)/shard_map/hqk,qhd->kd/dot_general | solution.py:103
  87.8 3.3 %fusion.16 = bf16[360,2,128]{2,0,1:T(8,128)(2,1)S(1)} fusion(s32[]{:T(128)S(6)} %select_n.32, bf16[1440,128]{1,0:T(8,128)(2,1)S(1)} %all_gather.6, f32[2,360,1383]{2,1,0:T(8,128)} %get-tuple-element.9, f32[2,360]{1,0:T(2,128)S(1)} %get-tuple-element.8), kind=kOutput, calls=%fused_computation.33 | convolution fusion | flops 256998240 | bytes 4538884 | tf_op jit(solution)/shard_map/hqk,kd->qhd/dot_general | solution.py:95
  92.1 3.4 %all-to-all-start.3 = ((bf16[4,90,256]{2,1,0:T(8,128)(2,1)}), bf16[4,90,256]{2,1,0:T(8,128)(2,1)S(1)}, u32[]{:S(2)}, u32[]{:S(2)}) async-start(bf16[4,90,256]{2,1,0:T(8,128)(2,1)} %reshape_reshape.13), calls=%async_computation.3 | async-start | bytes 393216 | tf_op jit(solution)/shard_map/all_to_all | solution.py:142
  95.4 9.1 %fusion.15 = bf16[360,2,128]{2,0,1:T(8,128)(2,1)S(1)} fusion(f32[1383,360,2]{0,1,2:T(8,128)} %fusion.23, s32[]{:T(128)S(6)} %select_n.32, bf16[1440,128]{1,0:T(8,128)(2,1)S(1)} %all_gather.7, f32[2,360,1383]{2,1,0:T(8,128)} %get-tuple-element.9, f32[2,360]{1,0:T(2,128)S(1)} %get-tuple-element.8), kind=kOutput, calls=%fused_computation.32 | convolution fusion | flops 261979136 | bytes 16779268 | tf_op jit(solution)/shard_map/hqk,kd->qhd/dot_general | solution.py:111
  105.5 5.0 %all-to-all-start.5 = ((bf16[4,90,256]{2,1,0:T(8,128)(2,1)}), bf16[4,90,256]{2,1,0:T(8,128)(2,1)S(1)}, u32[]{:S(2)}, u32[]{:S(2)}) async-start(bf16[4,90,256]{2,1,0:T(8,128)(2,1)} %reshape_reshape.15), calls=%async_computation.5 | async-start | bytes 393216 | tf_op jit(solution)/shard_map/all_to_all | solution.py:143
  110.5 1.6 %reshape.137 = bf16[4,90,128]{2,1,0:T(8,128)(2,1)} reshape(bf16[360,128]{1,0:T(8,128)(2,1)} %reduce-scatter.7.cloned.1.call-done) | data formatting | bytes 184320 | tf_op jit(solution)/shard_map/reshape | solution.py:35
  112.1 4.7 %all-to-all-done.5 = bf16[4,90,256]{2,1,0:T(8,128)(2,1)S(1)} async-done(((bf16[4,90,256]{2,1,0:T(8,128)(2,1)}), bf16[4,90,256]{2,1,0:T(8,128)(2,1)S(1)}, u32[]{:S(2)}, u32[]{:S(2)}) %all-to-all-start.5) | async-done | bytes 184352 | tf_op jit(solution)/shard_map/all_to_all | solution.py:143
  116.8 3.3 %all-to-all-start.6 = ((bf16[4,90,128]{2,1,0:T(8,128)(2,1)}), bf16[4,90,128]{2,1,0:T(8,128)(2,1)S(1)}, u32[]{:S(2)}, u32[]{:S(2)}) async-start(bf16[4,90,128]{2,1,0:T(8,128)(2,1)} %reshape.137), calls=%async_computation.6 | async-start | bytes 196608 | tf_op jit(solution)/shard_map/all_to_all | solution.py:144
  120.1 3.8 %sort.32 = (s32[360]{0:T(512)}, s32[360]{0:T(512)S(1)}) sort(s32[360]{0:T(512)S(1)} %get-tuple-element.6, s32[360]{0:T(512)S(1)} %iota.31), dimensions={0}, to_apply=%region_5.6 | sort | flops 3240 | bytes 5760 | tf_op jit(solution)/shard_map/jit(argsort)/sort | solution.py:29
  123.9 1.9 %reduce-scatter.9.cloned.1.call-done = bf16[360,128]{1,0:T(8,128)(2,1)} async-done(((bf16[1440,128]{1,0:T(8,128)(2,1)}), bf16[360,128]{1,0:T(8,128)(2,1)}) %reduce-scatter.9.cloned.1.call-update) | async-done | bytes 92176
  125.8 1.5 %reshape.139 = bf16[4,90,128]{2,1,0:T(8,128)(2,1)} reshape(bf16[360,128]{1,0:T(8,128)(2,1)} %reduce-scatter.9.cloned.1.call-done) | data formatting | bytes 184320 | tf_op jit(solution)/shard_map/reshape | solution.py:35
  127.3 4.6 %all-to-all-start.7 = ((bf16[4,90,128]{2,1,0:T(8,128)(2,1)}), bf16[4,90,128]{2,1,0:T(8,128)(2,1)S(1)}, u32[]{:S(2)}, u32[]{:S(2)}) async-start(bf16[4,90,128]{2,1,0:T(8,128)(2,1)} %reshape.139), calls=%async_computation.7 | async-start | bytes 196608 | tf_op jit(solution)/shard_map/all_to_all | solution.py:145
  132.0 2.5 %gather_fusion.3 = bf16[360,256]{1,0:T(8,128)(2,1)} fusion(bf16[360,256]{1,0:T(8,128)(2,1)S(1)} %reshape.134, s32[1024]{0:T(1024)S(1)} %pad_clamp_fusion), kind=kCustom, calls=%fused_computation.3 | custom fusion | bytes 370080 | tf_op jit(solution)/shard_map/gather | solution.py:38
  134.6 2.5 %gather_fusion.5 = bf16[360,256]{1,0:T(8,128)(2,1)} fusion(bf16[360,256]{1,0:T(8,128)(2,1)S(1)} %reshape.136, s32[1024]{0:T(1024)S(1)} %pad_clamp_fusion), kind=kCustom, calls=%fused_computation.5 | custom fusion | bytes 370080 | tf_op jit(solution)/shard_map/gather | solution.py:38
  137.2 1.9 %gather_fusion.6 = bf16[360,128]{1,0:T(8,128)(2,1)} fusion(bf16[360,128]{1,0:T(8,128)(2,1)S(1)} %reshape.138, s32[1024]{0:T(1024)S(1)} %pad_clamp_fusion), kind=kCustom, calls=%fused_computation.6 | custom fusion | bytes 185760 | tf_op jit(solution)/shard_map/gather | solution.py:38
  139.1 1.9 %gather_fusion.7 = bf16[360,128]{1,0:T(8,128)(2,1)} fusion(bf16[360,128]{1,0:T(8,128)(2,1)S(1)} %reshape.140, s32[1024]{0:T(1024)S(1)} %pad_clamp_fusion), kind=kCustom, calls=%fused_computation.7 | custom fusion | bytes 185760 | tf_op jit(solution)/shard_map/gather | solution.py:38
  (52 shorter events, 10.1 us)
Async XLA Ops:
  7.2 23.6 %copy-start = (bf16[1,360,256]{2,1,0:T(8,128)(2,1)S(1)}, bf16[1,360,256]{2,1,0:T(8,128)(2,1)}, u32[]{:S(2)}) copy-start(bf16[1,360,256]{2,1,0:T(8,128)(2,1)} %param.6) | copy-start | bytes 552964
  7.2 26.4 %copy-start.1 = (bf16[1,360,256]{2,1,0:T(8,128)(2,1)S(1)}, bf16[1,360,256]{2,1,0:T(8,128)(2,1)}, u32[]{:S(2)}) copy-start(bf16[1,360,256]{2,1,0:T(8,128)(2,1)} %param.9) | copy-start | bytes 552964
  14.5 12.2 %all-to-all-start = ((bf16[4,90,128]{2,1,0:T(8,128)(2,1)}), bf16[4,90,128]{2,1,0:T(8,128)(2,1)S(1)}, u32[]{:S(2)}, u32[]{:S(2)}) async-start(bf16[4,90,128]{2,1,0:T(8,128)(2,1)} %reshape.127), calls=%async_computation | async-start | bytes 196608 | tf_op jit(solution)/shard_map/all_to_all | solution.py:43
  26.6 9.7 %all-to-all-start.1 = ((bf16[4,90,128]{2,1,0:T(8,128)(2,1)}), bf16[4,90,128]{2,1,0:T(8,128)(2,1)S(1)}, u32[]{:S(2)}, u32[]{:S(2)}) async-start(bf16[4,90,128]{2,1,0:T(8,128)(2,1)} %reshape.131), calls=%async_computation.1 | async-start | bytes 196608 | tf_op jit(solution)/shard_map/all_to_all | solution.py:42
  36.4 17.9 %all-to-all-start.4 = ((bf16[4,90,256]{2,1,0:T(8,128)(2,1)}), bf16[4,90,256]{2,1,0:T(8,128)(2,1)S(1)}, u32[]{:S(2)}, u32[]{:S(2)}) async-start(bf16[4,90,256]{2,1,0:T(8,128)(2,1)} %reshape.135), calls=%async_computation.4 | async-start | bytes 393216 | tf_op jit(solution)/shard_map/all_to_all | solution.py:44
  54.2 13.1 %all-to-all-start.2 = ((bf16[4,90,256]{2,1,0:T(8,128)(2,1)}), bf16[4,90,256]{2,1,0:T(8,128)(2,1)S(1)}, u32[]{:S(2)}, u32[]{:S(2)}) async-start(bf16[4,90,256]{2,1,0:T(8,128)(2,1)} %reshape.133), calls=%async_computation.2 | async-start | bytes 393216 | tf_op jit(solution)/shard_map/all_to_all | solution.py:41
  59.3 51.2 %reduce-scatter.7.cloned.1.call-start = ((), (), s32[]{:S(2)}) async-start(), calls=%async_computation.10 | async-start | bytes 460800
  83.3 42.4 %reduce-scatter.9.cloned.1.call-start = ((), (), s32[]{:S(2)}) async-start(), calls=%async_computation.11 | async-start | bytes 460800
  92.1 13.4 %all-to-all-start.3 = ((bf16[4,90,256]{2,1,0:T(8,128)(2,1)}), bf16[4,90,256]{2,1,0:T(8,128)(2,1)S(1)}, u32[]{:S(2)}, u32[]{:S(2)}) async-start(bf16[4,90,256]{2,1,0:T(8,128)(2,1)} %reshape_reshape.13), calls=%async_computation.3 | async-start | bytes 393216 | tf_op jit(solution)/shard_map/all_to_all | solution.py:142
  105.5 11.3 %all-to-all-start.5 = ((bf16[4,90,256]{2,1,0:T(8,128)(2,1)}), bf16[4,90,256]{2,1,0:T(8,128)(2,1)S(1)}, u32[]{:S(2)}, u32[]{:S(2)}) async-start(bf16[4,90,256]{2,1,0:T(8,128)(2,1)} %reshape_reshape.15), calls=%async_computation.5 | async-start | bytes 393216 | tf_op jit(solution)/shard_map/all_to_all | solution.py:143
  116.8 10.6 %all-to-all-start.6 = ((bf16[4,90,128]{2,1,0:T(8,128)(2,1)}), bf16[4,90,128]{2,1,0:T(8,128)(2,1)S(1)}, u32[]{:S(2)}, u32[]{:S(2)}) async-start(bf16[4,90,128]{2,1,0:T(8,128)(2,1)} %reshape.137), calls=%async_computation.6 | async-start | bytes 196608 | tf_op jit(solution)/shard_map/all_to_all | solution.py:144
  127.3 11.8 %all-to-all-start.7 = ((bf16[4,90,128]{2,1,0:T(8,128)(2,1)}), bf16[4,90,128]{2,1,0:T(8,128)(2,1)S(1)}, u32[]{:S(2)}, u32[]{:S(2)}) async-start(bf16[4,90,128]{2,1,0:T(8,128)(2,1)} %reshape.139), calls=%async_computation.7 | async-start | bytes 196608 | tf_op jit(solution)/shard_map/all_to_all | solution.py:145
Sparse Core Ops, SparseCore 0:
  83.5 19.2 reduce-scatter.6
  105.3 20.4 reduce-scatter.8
where the time goes:
time: 149 us; the launch traced here: 148 us
  starting transfers between devices  36.3 us (24%)
  matrix products  33.4 us (22%)
  local copies, waits for them, and re-layouts  27.4 us (18%)
  between operations  14.3 us (10%)
  waiting for transfers between devices  13.6 us (9%)
  blocking collectives  12.8 us (9%)
  other arithmetic  10.2 us (7%)
    dot_general x1, matrix products, local(): jnp.einsum('hqk,qhd->kd', dscore, query_three, preferred_element_type=jnp...  10.5 us
    dot_general x1, matrix products, local(): jnp.einsum('hqk,kd->qhd', dscore, key_group, preferred_element_type=jnp.f...  9.08 us
    gather x4, local copies, waits for them, and re-layouts, settle(): return values.reshape(row_count, values.shape[2])[back_order][None]  8.89 us
    gather x4, local copies, waits for them, and re-layouts, outgoing(): values[0][send_order].reshape(peer_count, group_rows, values.shape[2])  8.19 us
    all_gather x1, blocking collectives, local(): lax.all_gather(key_here, 'seq', axis=0, tiled=True)  6.43 us
    all_gather x1, blocking collectives, local(): lax.all_gather(value_here, 'seq', axis=0, tiled=True)  6.33 us
    all_to_all x1, starting transfers between devices, local(): lax.all_to_all(outgoing(value_rows), 'dp', split_axis=0, concat_axis=0, t...  6.32 us
    all_to_all x1, starting transfers between devices, local(): lax.all_to_all(outgoing(queries), 'dp', split_axis=0, concat_axis=0, tile...  5.09 us
  transfers between devices with their start and end apart: 10, of which 4 were waited for; matrix products, arithmetic and copies ran while one was open for 31% of the time, Pallas kernels for 0%

commit v1 on v0

v1 whole, which is shorter than its diff:
```python
import functools
import math

import jax
import jax.numpy as jnp
from jax import lax
from jax.experimental import pallas as pl
from jax.experimental.pallas import tpu as pltpu
from jax.sharding import PartitionSpec as P

HEAD_DIM = 128
WINDOW = 1024
TILE = 16
LANES = 128

score_scale = 168.0 ** (-0.5)
log2_e = 1.4426950408889634
neg_large = -1e30
vmem_bytes = 24 * 1024 * 1024
brief = pl.CostEstimate(flops=1, bytes_accessed=1, transcendentals=0)
pause = pl.CostEstimate(flops=10**11, bytes_accessed=10**8, transcendentals=0)

F32 = jnp.float32
BF16 = jnp.bfloat16
NT = (((1,), (1,)), ((), ()))
TN = (((0,), (0,)), ((), ()))


def dot(a, b, dims=(((1,), (0,)), ((), ()))):
    return lax.dot_general(a, b, dims, preferred_element_type=F32)


def receiver_of(me, step, peers):
    return me ^ step if peers & (peers - 1) == 0 else (me + step) % peers


def travel_order(peers):
    return list(range(2, peers)) + [1, 0]


def step_to(me, other, peers):
    if peers & (peers - 1) == 0:
        return other ^ me
    step = other - me
    return jnp.where(step < 0, step + peers, step)


def position_of(row, pad, group_rows):
    group, inner = row // pad, row % pad
    last = group_rows - 1
    return group * group_rows + (min(inner, last) if isinstance(row, int) else jnp.minimum(inner, last)), inner


def query_positions(rows, pad, row_count):
    lane = lax.broadcasted_iota(jnp.int32, (1, 2 * rows), 1)
    row = lane // (2 * LANES) * LANES + lane % LANES
    return position_of(row, pad, row_count * pad // rows)[0]


def stacked_row(row, head, unit):
    return pl.multiple_of(row // LANES * (2 * LANES) + head * LANES + row % LANES, unit)


def load(pairs, sems):
    copies = [pltpu.make_async_copy(*pair, sems.at[i]) for i, pair in enumerate(pairs)]
    for copy in copies:
        copy.start()
    return copies


def place_of(slot, slots):
    here = lax.broadcasted_iota(jnp.int32, (slots, slot.shape[1]), 0) == slot
    return here.astype(F32).astype(BF16)


def sort_kernel(peers, pad, dest_hbm, k_hbm, v_hbm, *refs):
    outs, slot_ref = refs[:peers], refs[peers]
    dest_ref, k_ref, v_ref, sems = refs[peers + 1 :]
    copies = load(((dest_hbm, dest_ref), (k_hbm, k_ref), (v_hbm, v_ref)), sems)
    rows = k_ref.shape[0]
    me = lax.axis_index("dp")
    wide = -(-peers // TILE) * TILE
    lane = lax.broadcasted_iota(jnp.int32, (wide, rows), 0)
    upto = (
        lax.broadcasted_iota(jnp.int32, (rows, rows), 0)
        <= lax.broadcasted_iota(jnp.int32, (rows, rows), 1)
    ).astype(F32)
    copies[0].wait()
    member = (lane == step_to(me, dest_ref[...], peers)).astype(F32)
    count = dot(member.astype(BF16), upto.astype(BF16))
    slot = jnp.sum(member * (count + (lane * pad - 1).astype(F32)), axis=0, keepdims=True)
    slot = slot.astype(jnp.int32)
    slot_ref[...] = slot
    place = place_of(slot, peers * pad)
    for copy, ref, at in zip(copies[1:], (k_ref, v_ref), (0, 1)):
        copy.wait()
        moved = dot(place, ref[...]).astype(BF16)
        for p in range(peers):
            outs[p][:, at * HEAD_DIM : (at + 1) * HEAD_DIM] = moved[p * pad : (p + 1) * pad]


def follow_kernel(peers, pad, slot_ref, lengths_hbm, q_hbm, g_hbm, *refs):
    outs, first_ref = refs[:peers], refs[peers]
    lengths_ref, q_ref, g_ref, sems = refs[peers + 1 :]
    copies = load(((q_hbm, q_ref), (g_hbm, g_ref), (lengths_hbm, lengths_ref)), sems)
    rows = q_ref.shape[0]
    place = place_of(slot_ref[...], peers * pad)
    for copy, ref, at in zip(copies, (q_ref, g_ref), (0, 2)):
        copy.wait()
        moved = dot(place, ref[...]).astype(BF16)
        for p in range(peers):
            outs[p][:, at * HEAD_DIM : (at + 2) * HEAD_DIM] = moved[p * pad : (p + 1) * pad]
    copies[2].wait()
    query_pos = query_positions(peers * pad, pad, rows) + lax.axis_index("seq") * rows
    first = jnp.maximum(query_pos - (WINDOW - 1), 0)
    edge = jnp.int32(0)
    for e in range(lengths_ref.shape[1]):
        edge = edge + lengths_ref[0, e]
        first = jnp.maximum(first, jnp.where(edge <= query_pos, edge, 0))
    first_ref[...] = first


def back_kernel(slot_ref, back_ref):
    rows, slots = back_ref.shape
    slot = slot_ref[...]
    eye = lax.broadcasted_iota(jnp.int32, (rows, rows), 0) == lax.broadcasted_iota(
        jnp.int32, (rows, rows), 1
    )
    column = jnp.sum(jnp.where(eye, slot, 0), axis=1, keepdims=True)
    back_ref[...] = (
        (lax.broadcasted_iota(jnp.int32, (rows, slots), 1) == column).astype(F32).astype(BF16)
    )


def windows(here, rows, pad, row_count):
    group_rows = row_count // (rows // pad)
    blocks = []
    for b in range(rows // LANES):
        reach = here * row_count + position_of(b * LANES, pad, group_rows)[0] - (WINDOW - 1)
        reach = max(reach, 0)
        row = reach // row_count * rows + reach % row_count // group_rows * pad + reach % group_rows
        keys = slice(row // LANES * LANES, here * rows + (b + 1) * LANES)
        blocks.append((keys, slice(2 * b * LANES, 2 * (b + 1) * LANES)))
    return blocks


def attend_kernel(peers, pad, row_count, span, sequence_ref, q_ref, g_ref, first_ref, *refs):
    own_grad_ref, far_grad_ref, low_ref, ds_ref = refs[:4]
    w_scr, dp_scr, dv_scr, dk_scr = refs[4:]
    rows = peers * pad
    shard = lax.axis_index("seq")
    factor = score_scale * log2_e
    first, last = first_ref[...], query_positions(rows, pad, row_count)
    group_rows = row_count // peers
    offset, inner = position_of(lax.broadcasted_iota(jnp.int32, (rows, 1), 0), pad, group_rows)
    offset = jnp.where(inner < group_rows, offset, -(2**24))

    def attend(here):
        blocks = windows(here, rows, pad, row_count)

        def strips(window):
            at = window.start
            while at < window.stop:
                end = min(at - at % rows + rows, window.stop)
                yield at // rows, slice(at, end), slice(at % rows, at % rows + end - at)
                at = end

        def products(window, cols):
            w_scr[window, cols] = dot(sequence_ref[window, :HEAD_DIM], q_ref[cols, :], NT)
            dp_scr[window, cols] = dot(sequence_ref[window, HEAD_DIM:], g_ref[cols, :], NT)

        def weigh(window, cols):
            parts = []
            for c, at, inside in strips(window):
                allowed = offset[inside] >= first[:, cols] - c * row_count
                if c == here:
                    allowed = allowed & (offset[inside] <= last[:, cols])
                part = jnp.where(allowed, w_scr[at, cols], neg_large)
                w_scr[at, cols] = part
                parts.append(jnp.max(part, axis=0, keepdims=True))
            peak = functools.reduce(jnp.maximum, parts)
            total, mean = 0.0, 0.0
            for _, at, _ in strips(window):
                w = jnp.exp2((w_scr[at, cols] - peak) * factor)
                w_scr[at, cols] = w
                total += jnp.sum(w, axis=0, keepdims=True)
                mean += jnp.sum(w * dp_scr[at, cols], axis=0, keepdims=True)
            share = 1.0 / total
            center = mean * share
            for _, at, _ in strips(window):
                p = w_scr[at, cols] * share
                low_ref[at, cols] = p.astype(BF16)
                ds_ref[at, cols] = (p * (dp_scr[at, cols] - center)).astype(BF16)

        def spread(window, cols, start):
            dv = dot(low_ref[window, cols], g_ref[cols, :])
            dk = dot(ds_ref[window, cols], q_ref[cols, :])
            old = slice(window.start, start)
            if start > window.start:
                dv_scr[old, :] += dv[: start - window.start]
                dk_scr[old, :] += dk[: start - window.start]
            dv_scr[start : window.stop, :] = dv[start - window.start :]
            dk_scr[start : window.stop, :] = dk[start - window.start :]

        products(*blocks[0])
        start = blocks[0][0].start
        for b, (window, cols) in enumerate(blocks):
            if b + 1 < len(blocks):
                products(*blocks[b + 1])
            weigh(window, cols)
            spread(window, cols, start)
            start = window.stop
        for c in range(span):
            grad, half = ((own_grad_ref, 0), (far_grad_ref, 0), (own_grad_ref, 1), (far_grad_ref, 1))[here ^ c]
            to, at = slice(half * rows, (half + 1) * rows), slice(c * rows, (c + 1) * rows)
            if c <= here and at.stop > blocks[0][0].start:
                grad[to, HEAD_DIM:] = dv_scr[at, :].astype(BF16)
                grad[to, :HEAD_DIM] = (dk_scr[at, :] * score_scale).astype(BF16)
            else:
                grad[to, :] = jnp.zeros((rows, 2 * HEAD_DIM), BF16)

    for here in range(span):
        pl.when(shard == here)(functools.partial(attend, here))


def gather_kernel(peers, pad, row_count, span, sequence_ref, low_ref, ds_ref, *refs):
    out_refs, turned_scr, whole_scr = refs[:peers], refs[peers], refs[peers + 1]
    rows = peers * pad
    me = lax.axis_index("dp")
    shard = lax.axis_index("seq")

    def gather(here):
        for window, cols in windows(here, rows, pad, row_count):
            turned_scr[:HEAD_DIM, cols] = dot(sequence_ref[window, HEAD_DIM:], low_ref[window, cols], TN)
            turned_scr[HEAD_DIM:, cols] = (
                dot(sequence_ref[window, :HEAD_DIM], ds_ref[window, cols], TN) * score_scale
            )

    for here in range(span):
        pl.when(shard == here)(functools.partial(gather, here))

    unit = math.gcd(pad, LANES)
    for column in range(2):
        whole_scr[...] = turned_scr[column * HEAD_DIM : (column + 1) * HEAD_DIM, :].T.astype(BF16)
        for p in range(peers):
            for t in range(pad // unit):
                for h in range(2):
                    at = pl.ds(stacked_row(step_to(p, me, peers) * pad + t * unit, h, unit), unit)
                    to = (2 * column + h) * HEAD_DIM
                    out_refs[p][t * unit : (t + 1) * unit, to : to + HEAD_DIM] = whole_scr[at, :]


def settle_kernel(peers, back_ref, *refs):
    pieces, outs = refs[:peers], refs[peers:]
    order = travel_order(peers)
    whole = jnp.concatenate([pieces[order.index(p)][...] for p in range(peers)], axis=0)
    settled = dot(back_ref[...], whole).astype(BF16)
    at = 0
    for out in outs:
        out[...] = settled[:, at : at + out.shape[1]]
        at += out.shape[1]


def join_kernel(peers, *refs):
    whole = refs[-1]
    pad = refs[0].shape[0]
    me = lax.axis_index("dp")
    for step, ref in zip(travel_order(peers), refs):
        whole[pl.ds(pl.multiple_of(step_to(step, me, peers) * pad, pad), pad), :] = ref[...]


def stack_kernel(peers, *refs):
    stacks = refs[peers:]
    pad = refs[0].shape[0]
    unit = math.gcd(pad, LANES)
    me = lax.axis_index("dp")
    for step, ref in zip(travel_order(peers), refs):
        for t in range(pad // unit):
            for h in range(2):
                to = pl.ds(stacked_row(step_to(step, me, peers) * pad + t * unit, h, unit), unit)
                for column, out in enumerate(stacks):
                    at = (2 * column + h) * HEAD_DIM
                    out[to, :] = ref[t * unit : (t + 1) * unit, at : at + HEAD_DIM]


def part_kernel(peers, a_ref, b_ref, *outs):
    pad = outs[0].shape[0]
    me = lax.axis_index("dp")
    for step, out in enumerate(outs):
        at = pl.ds(pl.multiple_of(step_to(step, me, peers) * pad, pad), pad)
        out[...] = (a_ref[at, :] + b_ref[at, :].astype(F32)).astype(BF16)


def add_kernel(a_ref, b_ref, after_ref, *outs):
    at = 0
    for out in outs:
        size = out.shape[0]
        both = a_ref[at : at + size, :].astype(F32) + b_ref[at : at + size, :].astype(F32)
        out[...] = both.astype(out.dtype)
        at += size


def call(kernel, outs, *args, scratch=(), in_specs=None, cost=None):
    return pl.pallas_call(
        kernel,
        out_shape=outs,
        in_specs=in_specs or [pl.BlockSpec(memory_space=pltpu.VMEM)] * len(args),
        scratch_shapes=scratch,
        compiler_params=pltpu.CompilerParams(vmem_limit_bytes=vmem_bytes),
        cost_estimate=cost,
    )(*args)


def local(queries, key_rows, value_rows, grad_out, doc_lengths, dest_index):
    row_count = queries.shape[1]
    peers = lax.axis_size("dp")
    span = lax.axis_size("seq")
    group_rows = row_count // peers
    pad = -(-group_rows // TILE) * TILE
    rows = peers * pad
    shape = jax.ShapeDtypeStruct

    sources = [
        pltpu.with_memory_space_constraint(a, pltpu.HBM)
        for a in (doc_lengths, dest_index, queries[0], key_rows[0], value_rows[0], grad_out[0])
    ]
    in_hbm = pl.BlockSpec(memory_space=pltpu.HBM)
    in_vmem = pl.BlockSpec(memory_space=pltpu.VMEM)

    def loaded(*arrays):
        return [pltpu.VMEM(a.shape, a.dtype) for a in arrays]

    lengths, dest, q, k, v, g = sources
    *kv, slot = call(
        functools.partial(sort_kernel, peers, pad),
        [shape((pad, 2 * HEAD_DIM), BF16)] * peers + [shape((1, row_count), jnp.int32)],
        dest,
        k,
        v,
        in_specs=[in_hbm] * 3,
        scratch=loaded(dest, k, v) + [pltpu.SemaphoreType.DMA((3,))],
    )
    *qg, first_seen = call(
        functools.partial(follow_kernel, peers, pad),
        [shape((pad, 4 * HEAD_DIM), BF16)] * peers + [shape((1, 2 * rows), jnp.int32)],
        slot,
        lengths,
        q,
        g,
        in_specs=[in_vmem] + [in_hbm] * 3,
        scratch=[pltpu.SMEM(lengths.shape, jnp.int32)]
        + loaded(q, g)
        + [pltpu.SemaphoreType.DMA((3,))],
        cost=pause,
    )

    def exchange(pieces, home=False):
        arrived = []
        for k in travel_order(peers):
            way = [(i, receiver_of(i, k, peers)) for i in range(peers)]
            if home:
                way = [(j, i) for i, j in way]
            arrived.append(lax.ppermute(pieces[k], "dp", way) if k else pieces[k])
        return arrived

    def to_partner(values, distance):
        return lax.ppermute(values, "seq", [(i, i ^ distance) for i in range(span)])

    def join(pieces):
        return call(functools.partial(join_kernel, peers), shape((rows, 2 * HEAD_DIM), BF16), *pieces, cost=brief)

    kv = exchange(kv)
    qg = exchange(qg)
    sequence = lax.all_gather(join(kv), "seq", axis=0, tiled=True)
    tall = shape((2 * rows, HEAD_DIM), BF16)
    stacked = call(
        functools.partial(stack_kernel, peers),
        [tall, tall],
        *qg,
        cost=brief,
    )

    back = call(back_kernel, shape((row_count, rows), BF16), slot)

    wide = (span * rows, 2 * rows)
    own_grad, far_grad, low, ds = call(
        functools.partial(attend_kernel, peers, pad, row_count, span),
        [shape((2 * rows, 2 * HEAD_DIM), BF16)] * 2 + [shape(wide, BF16)] * 2,
        sequence,
        *stacked,
        first_seen,
        scratch=[pltpu.VMEM(wide, F32)] * 2 + [pltpu.VMEM((span * rows, HEAD_DIM), F32)] * 2,
    )
    attended = call(
        functools.partial(gather_kernel, peers, pad, row_count, span),
        [shape((pad, 4 * HEAD_DIM), BF16)] * peers,
        sequence,
        low,
        ds,
        scratch=[pltpu.VMEM((2 * HEAD_DIM, 2 * rows), F32), pltpu.VMEM((2 * rows, HEAD_DIM), BF16)],
    )

    attended = exchange(attended, home=True)
    returned = to_partner(far_grad, 1)
    half = shape((rows, 2 * HEAD_DIM), BF16)
    mine, theirs = call(add_kernel, [shape(half.shape, F32), half], own_grad, returned, attended[-1], cost=pause)
    theirs = to_partner(theirs, 2)
    pair_grad = call(
        functools.partial(part_kernel, peers),
        [shape((pad, 2 * HEAD_DIM), BF16)] * peers,
        mine,
        theirs,
        cost=pause,
    )
    pair_grad = exchange(pair_grad, home=True)

    wide, narrow = shape((row_count, 2 * HEAD_DIM), BF16), shape((row_count, HEAD_DIM), BF16)
    first = call(
        functools.partial(settle_kernel, peers), [wide, wide], back, *attended
    )
    last = call(functools.partial(settle_kernel, peers), [narrow, narrow], back, *pair_grad)
    return first[0][None], first[1][None], last[0][None], last[1][None]


def solution(mesh):
    split = P("dp", "seq", "head")
    return jax.shard_map(
        local,
        mesh=mesh,
        in_specs=(split, split, split, split, P("dp", None), P("dp", "seq")),
        out_specs=(split, split, split, split),
        check_vma=False,
    )
```

time: 149 us -> 46.4 us (0.31)
  matrix products: 33.4 us -> 0 us
  local copies, waits for them, and re-layouts: 27.4 us -> 0.01 us
  starting transfers between devices: 36.3 us -> 22.6 us
  between operations: 14.3 us -> 0.75 us
  other arithmetic: 10.2 us -> 0 us
  Pallas kernels: 0 us -> 7.51 us
  waiting for transfers between devices: 13.6 us -> 6.76 us
  blocking collectives: 12.8 us -> 8.6 us
    all_to_all x8 -> x0, starting transfers between devices: 36.1 us -> none  [the longest x1 6.32 us: local(): lax.all_to_all(outgoing(value_rows), 'dp', split_axis=0, concat_axis=0, t...]
    dot_general x5 -> x0, matrix products: 29 us -> none  [the longest x1 10.5 us: local(): jnp.einsum('hqk,qhd->kd', dscore, query_three, preferred_element_type=jnp...]
    ppermute x0 -> x14, starting transfers between devices: none -> 22.6 us  [the longest x12 18.7 us: exchange(): arrived.append(lax.ppermute(pieces[k], 'dp', way) if k else pieces[k])]
    gather x8 -> x0, local copies, waits for them, and re-layouts: 17.1 us -> none  [the longest x4 8.89 us: settle(): return values.reshape(row_count, values.shape[2])[back_order][None]]
    all_to_all x8 -> x0, waiting for transfers between devices: 11.6 us -> none  [the longest x1 4.91 us: local(): lax.all_to_all(outgoing(queries), 'dp', split_axis=0, concat_axis=0, tile...]
    sort x2 -> x0, other arithmetic: 7.56 us -> none  [the longest x1 3.78 us: local(): send_order = jnp.argsort(dest_index[0] * row_count + local_rows)]
    pallas_call x0 -> x11, Pallas kernels: none -> 7.51 us  [call(): pl.pallas_call(kernel, out_shape=outs, in_specs=in_specs or [pl.BlockSpec...]
    ppermute x0 -> x14, waiting for transfers between devices: none -> 6.76 us  [the longest x12 4.94 us: exchange(): arrived.append(lax.ppermute(pieces[k], 'dp', way) if k else pieces[k])]
  transfers between devices with their start and end apart: 10 -> 14, of which waited for: 4 -> 4; matrix products, arithmetic and copies ran while one was open for 31% -> 0% of each run, Pallas kernels for 0% -> 8%
where the time goes in v1:
time: 46.4 us; the launch traced here: 46.2 us
  starting transfers between devices  22.6 us (49%)
  blocking collectives  8.6 us (19%)
  Pallas kernels  7.51 us (16%)
  waiting for transfers between devices  6.76 us (15%)
  between operations  0.75 us (2%)
    ppermute x12, starting transfers between devices, exchange(): arrived.append(lax.ppermute(pieces[k], 'dp', way) if k else pieces[k])  18.7 us
    all_gather x1, blocking collectives, local(): sequence = lax.all_gather(join(kv), 'seq', axis=0, tiled=True)  8.6 us
    pallas_call x11, Pallas kernels, call(): pl.pallas_call(kernel, out_shape=outs, in_specs=in_specs or [pl.BlockSpec...  7.51 us
    ppermute x12, waiting for transfers between devices, exchange(): arrived.append(lax.ppermute(pieces[k], 'dp', way) if k else pieces[k])  4.94 us
    ppermute x2, starting transfers between devices, to_partner(): return lax.ppermute(values, 'seq', [(i, i ^ distance) for i in range(span)])  3.85 us
    ppermute x2, waiting for transfers between devices, to_partner(): return lax.ppermute(values, 'seq', [(i, i ^ distance) for i in range(span)])  1.82 us
  transfers between devices with their start and end apart: 14, of which 4 were waited for; matrix products, arithmetic and copies ran while one was open for 0% of the time, Pallas kernels for 8%

profile of v1, /device:TPU:0, one launch (start us, length us, event | category | flops | bytes accessed | tf_op | source)
XLA Modules:
  0.0 46.2 jit_solution(8659673429460730494)
XLA Ops:
  0.6 1.5 %shard_map.93 = (bf16[96,256]{1,0:T(8,128)(2,1)S(1)}, bf16[96,256]{1,0:T(8,128)(2,1)S(1)}, bf16[96,256]{1,0:T(8,128)(2,1)S(1)}, bf16[96,256]{1,0:T(8,128)(2,1)S(1)}, s32[1,360]{1,0:T(1,128)S(1)}) custom-call(s32[1,360]{1,0:T(1,128)} %dest_hbm.1, bf16[360,128]{1,0:T(8,128)(2,1)} %bitcast.8, bf16[360,128]{1,0:T(8,128)(2,1)} %bitcast.9), custom_call_target="tpu_custom_call" | custom-call | tf_op jit(solution)/shard_map/pallas_call | solution.py:304
  2.1 0.0 copy-start
  2.1 4.1 %collective-permute-start = (bf16[96,256]{1,0:T(8,128)(2,1)S(1)}, bf16[96,256]{1,0:T(8,128)(2,1)S(1)}, u32[]{:S(2)}, u32[]{:S(2)}) collective-permute-start(bf16[96,256]{1,0:T(8,128)(2,1)S(1)} %get-tuple-element.35), channel_id=1, source_target_pairs={{0,16},{8,24},{16,0},{24,8},{1,17},{9,25},{17,1},{25,9},{2,18},{10... | collective-permute-start | bytes 147464 | tf_op jit(solution)/shard_map/ppermute | solution.py:363
  6.2 1.3 %collective-permute-start.1 = (bf16[96,256]{1,0:T(8,128)(2,1)S(1)}, bf16[96,256]{1,0:T(8,128)(2,1)S(1)}, u32[]{:S(2)}, u32[]{:S(2)}) collective-permute-start(bf16[96,256]{1,0:T(8,128)(2,1)S(1)} %get-tuple-element.36), channel_id=1, source_target_pairs={{0,24},{8,16},{16,8},{24,0},{1,25},{9,17},{17,9},{25,1},{2,26},{10... | collective-permute-start | bytes 147464 | tf_op jit(solution)/shard_map/ppermute | solution.py:363
  7.6 0.2 collective-permute-start.2
  7.8 1.7 %shard_map.96 = (bf16[96,512]{1,0:T(8,128)(2,1)S(1)}, bf16[96,512]{1,0:T(8,128)(2,1)S(1)}, bf16[96,512]{1,0:T(8,128)(2,1)S(1)}, bf16[96,512]{1,0:T(8,128)(2,1)S(1)}, s32[1,768]{1,0:T(1,128)S(1)}) custom-call(s32[1,360]{1,0:T(1,128)S(1)} %get-tuple-element.34.slot_ref, s32[1,4]{1,0:T(1,128)} %lengths_hbm.1, bf16[360,256]{1,0:T(8,128)(2,1)} %bitcast.10, ...), custom_call_target="tpu_custom_call" | custom-call | flops 99999997952 | bytes 100000000 | tf_op jit(solution)/shard_map/pallas_call | solution.py:304
  9.5 2.9 %collective-permute-start.3 = (bf16[96,512]{1,0:T(8,128)(2,1)S(1)}, bf16[96,512]{1,0:T(8,128)(2,1)S(1)}, u32[]{:S(2)}, u32[]{:S(2)}) collective-permute-start(bf16[96,512]{1,0:T(8,128)(2,1)S(1)} %get-tuple-element.39), channel_id=1, source_target_pairs={{0,16},{8,24},{16,0},{24,8},{1,17},{9,25},{17,1},{25,9},{2,18},{10... | collective-permute-start | bytes 294920 | tf_op jit(solution)/shard_map/ppermute | solution.py:363
  12.4 1.3 %collective-permute-start.4 = (bf16[96,512]{1,0:T(8,128)(2,1)S(1)}, bf16[96,512]{1,0:T(8,128)(2,1)S(1)}, u32[]{:S(2)}, u32[]{:S(2)}) collective-permute-start(bf16[96,512]{1,0:T(8,128)(2,1)S(1)} %get-tuple-element.40), channel_id=1, source_target_pairs={{0,24},{8,16},{16,8},{24,0},{1,25},{9,17},{17,9},{25,1},{2,26},{10... | collective-permute-start | bytes 294920 | tf_op jit(solution)/shard_map/ppermute | solution.py:363
  13.8 0.0 collective-permute-done.refs_0_
  13.8 0.0 collective-permute-start.5
  13.8 0.0 collective-permute-done.1.refs_1_
  13.8 0.0 collective-permute-done.2.refs_2_
  13.8 8.6 %all_gather.3.sequence_ref = bf16[1536,256]{1,0:T(8,128)(2,1)S(1)} all-gather(bf16[384,256]{1,0:T(8,128)(2,1)S(1)} %shard_map.95), channel_id=1, replica_groups=mesh['dp'=4,'seq'=4,'head'=2] {'seq'}, dimensions={0}, use_global_device_ids=true | all-gather | bytes 983040 | tf_op jit(solution)/shard_map/all_gather | solution.py:374
  22.4 0.0 collective-permute-done.3.refs_0_
  22.4 0.2 shard_map.97
  22.6 1.2 %shard_map.98 = (bf16[768,256]{1,0:T(8,128)(2,1)S(1)}, bf16[768,256]{1,0:T(8,128)(2,1)S(1)}, bf16[1536,768]{1,0:T(8,128)(2,1)S(1)}, bf16[1536,768]{1,0:T(8,128)(2,1)S(1)}) custom-call(bf16[1536,256]{1,0:T(8,128)(2,1)S(1)} %all_gather.3.sequence_ref, bf16[768,128]{1,0:T(8,128)(2,1)S(1)} %get-tuple-element.43.q_ref, ...), custom_call_target="tpu_custom_call" | custom-call | tf_op jit(solution)/shard_map/pallas_call | solution.py:304
  23.9 1.3 %collective-permute-start.9 = (bf16[768,256]{1,0:T(8,128)(2,1)S(1)}, bf16[768,256]{1,0:T(8,128)(2,1)S(1)}, u32[]{:S(2)}, u32[]{:S(2)}) collective-permute-start(bf16[768,256]{1,0:T(8,128)(2,1)S(1)} %get-tuple-element.55), channel_id=1, source_target_pairs={{0,2},{2,0},{4,6},{6,4},{1,3},{3,1},{5,7},{7,5},{8,10},{10,8},{12,... | collective-permute-start | bytes 1179656 | tf_op jit(solution)/shard_map/ppermute | solution.py:367
  25.1 0.6 %shard_map.99 = (bf16[96,512]{1,0:T(8,128)(2,1)S(1)}, bf16[96,512]{1,0:T(8,128)(2,1)S(1)}, bf16[96,512]{1,0:T(8,128)(2,1)S(1)}, bf16[96,512]{1,0:T(8,128)(2,1)S(1)}) custom-call(bf16[1536,256]{1,0:T(8,128)(2,1)S(1)} %all_gather.3.sequence_ref, bf16[1536,768]{1,0:T(8,128)(2,1)S(1)} %get-tuple-element.46.low_ref, bf16[1536,768]{1,0:T(8,128)(2,1)S(1)} %get-tuple-element.47.ds_ref), custom_call_target="tpu_custom_call" | custom-call | tf_op jit(solution)/shard_map/pallas_call | solution.py:304
  25.7 0.8 %collective-permute-done.9.b_ref = bf16[768,256]{1,0:T(8,128)(2,1)S(1)} collective-permute-done((bf16[768,256]{1,0:T(8,128)(2,1)S(1)}, bf16[768,256]{1,0:T(8,128)(2,1)S(1)}, u32[]{:S(2)}, u32[]{:S(2)}) %collective-permute-start.9) | collective-permute-done | bytes 393248 | tf_op jit(solution)/shard_map/ppermute | solution.py:367
  26.5 0.1 shard_map.101
  26.6 2.6 %collective-permute-start.10 = (bf16[384,256]{1,0:T(8,128)(2,1)S(1)}, bf16[384,256]{1,0:T(8,128)(2,1)S(1)}, u32[]{:S(2)}, u32[]{:S(2)}) collective-permute-start(bf16[384,256]{1,0:T(8,128)(2,1)S(1)} %get-tuple-element.57), channel_id=1, source_target_pairs={{0,4},{2,6},{4,0},{6,2},{1,5},{3,7},{5,1},{7,3},{8,12},{10,14},{12... | collective-permute-start | bytes 589832 | tf_op jit(solution)/shard_map/ppermute | solution.py:367
  29.1 3.0 %collective-permute-start.6 = (bf16[96,512]{1,0:T(8,128)(2,1)S(1)}, bf16[96,512]{1,0:T(8,128)(2,1)S(1)}, u32[]{:S(2)}, u32[]{:S(2)}) collective-permute-start(bf16[96,512]{1,0:T(8,128)(2,1)S(1)} %get-tuple-element.48), channel_id=1, source_target_pairs={{16,0},{24,8},{0,16},{8,24},{17,1},{25,9},{1,17},{9,25},{18,2},{26... | collective-permute-start | bytes 294920 | tf_op jit(solution)/shard_map/ppermute | solution.py:363
  32.2 1.3 %collective-permute-start.7 = (bf16[96,512]{1,0:T(8,128)(2,1)S(1)}, bf16[96,512]{1,0:T(8,128)(2,1)S(1)}, u32[]{:S(2)}, u32[]{:S(2)}) collective-permute-start(bf16[96,512]{1,0:T(8,128)(2,1)S(1)} %get-tuple-element.49), channel_id=1, source_target_pairs={{24,0},{16,8},{8,16},{0,24},{25,1},{17,9},{9,17},{1,25},{26,2},{18... | collective-permute-start | bytes 294920 | tf_op jit(solution)/shard_map/ppermute | solution.py:363
  33.5 1.0 %collective-permute-done.10.b_ref = bf16[384,256]{1,0:T(8,128)(2,1)S(1)} collective-permute-done((bf16[384,256]{1,0:T(8,128)(2,1)S(1)}, bf16[384,256]{1,0:T(8,128)(2,1)S(1)}, u32[]{:S(2)}, u32[]{:S(2)}) %collective-permute-start.10) | collective-permute-done | bytes 196640 | tf_op jit(solution)/shard_map/ppermute | solution.py:367
  34.6 3.1 %collective-permute-start.11 = (bf16[96,256]{1,0:T(8,128)(2,1)S(1)}, bf16[96,256]{1,0:T(8,128)(2,1)S(1)}, u32[]{:S(2)}, u32[]{:S(2)}) collective-permute-start(bf16[96,256]{1,0:T(8,128)(2,1)S(1)} %get-tuple-element.58), channel_id=1, source_target_pairs={{16,0},{24,8},{0,16},{8,24},{17,1},{25,9},{1,17},{9,25},{18,2},{26... | collective-permute-start | bytes 147464 | tf_op jit(solution)/shard_map/ppermute | solution.py:363
  37.7 1.3 %collective-permute-start.12 = (bf16[96,256]{1,0:T(8,128)(2,1)S(1)}, bf16[96,256]{1,0:T(8,128)(2,1)S(1)}, u32[]{:S(2)}, u32[]{:S(2)}) collective-permute-start(bf16[96,256]{1,0:T(8,128)(2,1)S(1)} %get-tuple-element.59), channel_id=1, source_target_pairs={{24,0},{16,8},{8,16},{0,24},{25,1},{17,9},{9,17},{1,25},{26,2},{18... | collective-permute-start | bytes 147464 | tf_op jit(solution)/shard_map/ppermute | solution.py:363
  39.0 1.5 %collective-permute-done.6.refs_0_ = bf16[96,512]{1,0:T(8,128)(2,1)S(1)} collective-permute-done((bf16[96,512]{1,0:T(8,128)(2,1)S(1)}, bf16[96,512]{1,0:T(8,128)(2,1)S(1)}, u32[]{:S(2)}, u32[]{:S(2)}) %collective-permute-start.6) | collective-permute-done | bytes 98336 | tf_op jit(solution)/shard_map/ppermute | solution.py:363
  40.6 0.2 shard_map.94.back_ref
  40.8 0.0 collective-permute-done.8.refs_2_
  40.8 1.1 %shard_map.100 = (bf16[360,256]{1,0:T(8,128)(2,1)}, bf16[360,256]{1,0:T(8,128)(2,1)}) custom-call(bf16[360,384]{1,0:T(8,128)(2,1)S(1)} %shard_map.94.back_ref, bf16[96,512]{1,0:T(8,128)(2,1)S(1)} %collective-permute-done.6.refs_0_, bf16[96,512]{1,0:T(8,128)(2,1)S(1)} %collective-permute-done.7.refs_1_, bf16[96,512]{1,0:T(8,128)(2,1)S(1)} %collective-permute-done.8.refs_2_, ...), custom_call_target="tpu_custom_call" | custom-call | tf_op jit(solution)/shard_map/pallas_call | solution.py:304
  41.9 3.4 %collective-permute-done.11.refs_0_ = bf16[96,256]{1,0:T(8,128)(2,1)S(1)} collective-permute-done((bf16[96,256]{1,0:T(8,128)(2,1)S(1)}, bf16[96,256]{1,0:T(8,128)(2,1)S(1)}, u32[]{:S(2)}, u32[]{:S(2)}) %collective-permute-start.11) | collective-permute-done | bytes 49184 | tf_op jit(solution)/shard_map/ppermute | solution.py:363
  45.3 0.9 %shard_map.103 = (bf16[360,128]{1,0:T(8,128)(2,1)}, bf16[360,128]{1,0:T(8,128)(2,1)}) custom-call(bf16[360,384]{1,0:T(8,128)(2,1)S(1)} %shard_map.94.back_ref, bf16[96,256]{1,0:T(8,128)(2,1)S(1)} %collective-permute-done.11.refs_0_, bf16[96,256]{1,0:T(8,128)(2,1)S(1)} %collective-permute-done.12.refs_1_, ...), custom_call_target="tpu_custom_call" | custom-call | tf_op jit(solution)/shard_map/pallas_call | solution.py:304
  (12 shorter events, 0.1 us)
Async XLA Ops:
  2.1 7.4 %copy-start = (s32[1,360]{1,0:T(1,128)}, s32[1,360]{1,0:T(1,128)S(1)}, u32[]{:S(2)}) copy-start(s32[1,360]{1,0:T(1,128)S(1)} %get-tuple-element.34.slot_ref) | copy-start | bytes 4324
  2.1 11.6 %collective-permute-start = (bf16[96,256]{1,0:T(8,128)(2,1)S(1)}, bf16[96,256]{1,0:T(8,128)(2,1)S(1)}, u32[]{:S(2)}, u32[]{:S(2)}) collective-permute-start(bf16[96,256]{1,0:T(8,128)(2,1)S(1)} %get-tuple-element.35), channel_id=1, source_target_pairs={{0,16},{8,24},{16,0},{24,8},{1,17},{9,25},{17,1},{25,9},{2,18},{10... | collective-permute-start | bytes 147464 | tf_op jit(solution)/shard_map/ppermute | solution.py:363
  6.2 7.5 %collective-permute-start.1 = (bf16[96,256]{1,0:T(8,128)(2,1)S(1)}, bf16[96,256]{1,0:T(8,128)(2,1)S(1)}, u32[]{:S(2)}, u32[]{:S(2)}) collective-permute-start(bf16[96,256]{1,0:T(8,128)(2,1)S(1)} %get-tuple-element.36), channel_id=1, source_target_pairs={{0,24},{8,16},{16,8},{24,0},{1,25},{9,17},{17,9},{25,1},{2,26},{10... | collective-permute-start | bytes 147464 | tf_op jit(solution)/shard_map/ppermute | solution.py:363
  7.6 6.2 %collective-permute-start.2 = (bf16[96,256]{1,0:T(8,128)(2,1)S(1)}, bf16[96,256]{1,0:T(8,128)(2,1)S(1)}, u32[]{:S(2)}, u32[]{:S(2)}) collective-permute-start(bf16[96,256]{1,0:T(8,128)(2,1)S(1)} %get-tuple-element.37), channel_id=1, source_target_pairs={{0,8},{8,0},{16,24},{24,16},{1,9},{9,1},{17,25},{25,17},{2,10},{10... | collective-permute-start | bytes 147464 | tf_op jit(solution)/shard_map/ppermute | solution.py:363
  9.5 12.9 %collective-permute-start.3 = (bf16[96,512]{1,0:T(8,128)(2,1)S(1)}, bf16[96,512]{1,0:T(8,128)(2,1)S(1)}, u32[]{:S(2)}, u32[]{:S(2)}) collective-permute-start(bf16[96,512]{1,0:T(8,128)(2,1)S(1)} %get-tuple-element.39), channel_id=1, source_target_pairs={{0,16},{8,24},{16,0},{24,8},{1,17},{9,25},{17,1},{25,9},{2,18},{10... | collective-permute-start | bytes 294920 | tf_op jit(solution)/shard_map/ppermute | solution.py:363
  12.4 10.0 %collective-permute-start.4 = (bf16[96,512]{1,0:T(8,128)(2,1)S(1)}, bf16[96,512]{1,0:T(8,128)(2,1)S(1)}, u32[]{:S(2)}, u32[]{:S(2)}) collective-permute-start(bf16[96,512]{1,0:T(8,128)(2,1)S(1)} %get-tuple-element.40), channel_id=1, source_target_pairs={{0,24},{8,16},{16,8},{24,0},{1,25},{9,17},{17,9},{25,1},{2,26},{10... | collective-permute-start | bytes 294920 | tf_op jit(solution)/shard_map/ppermute | solution.py:363
  13.8 8.7 %collective-permute-start.5 = (bf16[96,512]{1,0:T(8,128)(2,1)S(1)}, bf16[96,512]{1,0:T(8,128)(2,1)S(1)}, u32[]{:S(2)}, u32[]{:S(2)}) collective-permute-start(bf16[96,512]{1,0:T(8,128)(2,1)S(1)} %get-tuple-element.41), channel_id=1, source_target_pairs={{0,8},{8,0},{16,24},{24,16},{1,9},{9,1},{17,25},{25,17},{2,10},{10... | collective-permute-start | bytes 294920 | tf_op jit(solution)/shard_map/ppermute | solution.py:363
  23.9 2.6 %collective-permute-start.9 = (bf16[768,256]{1,0:T(8,128)(2,1)S(1)}, bf16[768,256]{1,0:T(8,128)(2,1)S(1)}, u32[]{:S(2)}, u32[]{:S(2)}) collective-permute-start(bf16[768,256]{1,0:T(8,128)(2,1)S(1)} %get-tuple-element.55), channel_id=1, source_target_pairs={{0,2},{2,0},{4,6},{6,4},{1,3},{3,1},{5,7},{7,5},{8,10},{10,8},{12,... | collective-permute-start | bytes 1179656 | tf_op jit(solution)/shard_map/ppermute | solution.py:367
  26.6 8.0 %collective-permute-start.10 = (bf16[384,256]{1,0:T(8,128)(2,1)S(1)}, bf16[384,256]{1,0:T(8,128)(2,1)S(1)}, u32[]{:S(2)}, u32[]{:S(2)}) collective-permute-start(bf16[384,256]{1,0:T(8,128)(2,1)S(1)} %get-tuple-element.57), channel_id=1, source_target_pairs={{0,4},{2,6},{4,0},{6,2},{1,5},{3,7},{5,1},{7,3},{8,12},{10,14},{12... | collective-permute-start | bytes 589832 | tf_op jit(solution)/shard_map/ppermute | solution.py:367
  29.1 11.4 %collective-permute-start.6 = (bf16[96,512]{1,0:T(8,128)(2,1)S(1)}, bf16[96,512]{1,0:T(8,128)(2,1)S(1)}, u32[]{:S(2)}, u32[]{:S(2)}) collective-permute-start(bf16[96,512]{1,0:T(8,128)(2,1)S(1)} %get-tuple-element.48), channel_id=1, source_target_pairs={{16,0},{24,8},{0,16},{8,24},{17,1},{25,9},{1,17},{9,25},{18,2},{26... | collective-permute-start | bytes 294920 | tf_op jit(solution)/shard_map/ppermute | solution.py:363
  32.2 8.6 %collective-permute-start.7 = (bf16[96,512]{1,0:T(8,128)(2,1)S(1)}, bf16[96,512]{1,0:T(8,128)(2,1)S(1)}, u32[]{:S(2)}, u32[]{:S(2)}) collective-permute-start(bf16[96,512]{1,0:T(8,128)(2,1)S(1)} %get-tuple-element.49), channel_id=1, source_target_pairs={{24,0},{16,8},{8,16},{0,24},{25,1},{17,9},{9,17},{1,25},{26,2},{18... | collective-permute-start | bytes 294920 | tf_op jit(solution)/shard_map/ppermute | solution.py:363
  33.5 7.3 %collective-permute-start.8 = (bf16[96,512]{1,0:T(8,128)(2,1)S(1)}, bf16[96,512]{1,0:T(8,128)(2,1)S(1)}, u32[]{:S(2)}, u32[]{:S(2)}) collective-permute-start(bf16[96,512]{1,0:T(8,128)(2,1)S(1)} %get-tuple-element.50), channel_id=1, source_target_pairs={{8,0},{0,8},{24,16},{16,24},{9,1},{1,9},{25,17},{17,25},{10,2},{2,... | collective-permute-start | bytes 294920 | tf_op jit(solution)/shard_map/ppermute | solution.py:363
  34.6 6.0 %copy-start.1 = (s32[1,360]{1,0:T(1,128)S(1)}, s32[1,360]{1,0:T(1,128)}, u32[]{:S(2)}) copy-start(s32[1,360]{1,0:T(1,128)} %copy-done) | copy-start | bytes 4324
  34.6 10.7 %collective-permute-start.11 = (bf16[96,256]{1,0:T(8,128)(2,1)S(1)}, bf16[96,256]{1,0:T(8,128)(2,1)S(1)}, u32[]{:S(2)}, u32[]{:S(2)}) collective-permute-start(bf16[96,256]{1,0:T(8,128)(2,1)S(1)} %get-tuple-element.58), channel_id=1, source_target_pairs={{16,0},{24,8},{0,16},{8,24},{17,1},{25,9},{1,17},{9,25},{18,2},{26... | collective-permute-start | bytes 147464 | tf_op jit(solution)/shard_map/ppermute | solution.py:363
  37.7 7.6 %collective-permute-start.12 = (bf16[96,256]{1,0:T(8,128)(2,1)S(1)}, bf16[96,256]{1,0:T(8,128)(2,1)S(1)}, u32[]{:S(2)}, u32[]{:S(2)}) collective-permute-start(bf16[96,256]{1,0:T(8,128)(2,1)S(1)} %get-tuple-element.59), channel_id=1, source_target_pairs={{24,0},{16,8},{8,16},{0,24},{25,1},{17,9},{9,17},{1,25},{26,2},{18... | collective-permute-start | bytes 147464 | tf_op jit(solution)/shard_map/ppermute | solution.py:363
  40.5 4.7 %collective-permute-start.13 = (bf16[96,256]{1,0:T(8,128)(2,1)S(1)}, bf16[96,256]{1,0:T(8,128)(2,1)S(1)}, u32[]{:S(2)}, u32[]{:S(2)}) collective-permute-start(bf16[96,256]{1,0:T(8,128)(2,1)S(1)} %get-tuple-element.60), channel_id=1, source_target_pairs={{8,0},{0,8},{24,16},{16,24},{9,1},{1,9},{25,17},{17,25},{10,2},{2,... | collective-permute-start | bytes 147464 | tf_op jit(solution)/shard_map/ppermute | solution.py:363

commit v2 on v1

--- a/solution.py
+++ b/solution.py
@@ -12,6 +12,7 @@
 WINDOW = 1024
 TILE = 16
 LANES = 128
+PARTS = 2
 
 score_scale = 168.0 ** (-0.5)
 log2_e = 1.4426950408889634
@@ -61,22 +62,25 @@
     return pl.multiple_of(row // LANES * (2 * LANES) + head * LANES + row % LANES, unit)
 
 
-def load(pairs, sems):
-    copies = [pltpu.make_async_copy(*pair, sems.at[i]) for i, pair in enumerate(pairs)]
-    for copy in copies:
-        copy.start()
-    return copies
-
-
 def place_of(slot, slots):
     here = lax.broadcasted_iota(jnp.int32, (slots, slot.shape[1]), 0) == slot
     return here.astype(F32).astype(BF16)
 
 
-def sort_kernel(peers, pad, dest_hbm, k_hbm, v_hbm, *refs):
-    outs, slot_ref = refs[:peers], refs[peers]
-    dest_ref, k_ref, v_ref, sems = refs[peers + 1 :]
-    copies = load(((dest_hbm, dest_ref), (k_hbm, k_ref), (v_hbm, v_ref)), sems)
+def sort_kernel(peers, pad, lengths_hbm, dest_hbm, k_hbm, v_hbm, q_hbm, g_hbm, *refs):
+    outs, slot_ref, first_ref, q_ref, g_ref = refs[:peers], *refs[peers : peers + 4]
+    lengths_ref, dest_ref, k_ref, v_ref, sems = refs[peers + 4 :]
+    loads = (
+        (dest_hbm, dest_ref),
+        (k_hbm, k_ref),
+        (v_hbm, v_ref),
+        (lengths_hbm, lengths_ref),
+        (q_hbm, q_ref),
+        (g_hbm, g_ref),
+    )
+    copies = [pltpu.make_async_copy(*pair, sems.at[i]) for i, pair in enumerate(loads)]
+    for copy in copies:
+        copy.start()
     rows = k_ref.shape[0]
     me = lax.axis_index("dp")
     wide = -(-peers // TILE) * TILE
@@ -92,25 +96,12 @@
     slot = slot.astype(jnp.int32)
     slot_ref[...] = slot
     place = place_of(slot, peers * pad)
-    for copy, ref, at in zip(copies[1:], (k_ref, v_ref), (0, 1)):
+    for copy, ref, at in zip(copies[1:3], (k_ref, v_ref), (0, 1)):
         copy.wait()
         moved = dot(place, ref[...]).astype(BF16)
         for p in range(peers):
             outs[p][:, at * HEAD_DIM : (at + 1) * HEAD_DIM] = moved[p * pad : (p + 1) * pad]
-
-
-def follow_kernel(peers, pad, slot_ref, lengths_hbm, q_hbm, g_hbm, *refs):
-    outs, first_ref = refs[:peers], refs[peers]
-    lengths_ref, q_ref, g_ref, sems = refs[peers + 1 :]
-    copies = load(((q_hbm, q_ref), (g_hbm, g_ref), (lengths_hbm, lengths_ref)), sems)
-    rows = q_ref.shape[0]
-    place = place_of(slot_ref[...], peers * pad)
-    for copy, ref, at in zip(copies, (q_ref, g_ref), (0, 2)):
-        copy.wait()
-        moved = dot(place, ref[...]).astype(BF16)
-        for p in range(peers):
-            outs[p][:, at * HEAD_DIM : (at + 2) * HEAD_DIM] = moved[p * pad : (p + 1) * pad]
-    copies[2].wait()
+    copies[3].wait()
     query_pos = query_positions(peers * pad, pad, rows) + lax.axis_index("seq") * rows
     first = jnp.maximum(query_pos - (WINDOW - 1), 0)
     edge = jnp.int32(0)
@@ -118,6 +109,16 @@
         edge = edge + lengths_ref[0, e]
         first = jnp.maximum(first, jnp.where(edge <= query_pos, edge, 0))
     first_ref[...] = first
+    for copy in copies[4:]:
+        copy.wait()
+
+
+def follow_kernel(peers, pad, slot_ref, q_ref, g_ref, *outs):
+    place = place_of(slot_ref[...], peers * pad)
+    for ref, at in ((q_ref, 0), (g_ref, 2)):
+        moved = dot(place, ref[...]).astype(BF16)
+        for p in range(peers):
+            outs[p][:, at * HEAD_DIM : (at + 2) * HEAD_DIM] = moved[p * pad : (p + 1) * pad]
 
 
 def back_kernel(slot_ref, back_ref):
@@ -269,12 +270,13 @@
         whole[pl.ds(pl.multiple_of(step_to(step, me, peers) * pad, pad), pad), :] = ref[...]
 
 
-def stack_kernel(peers, *refs):
+def stack_kernel(order, *refs):
+    peers = len(order)
     stacks = refs[peers:]
     pad = refs[0].shape[0]
     unit = math.gcd(pad, LANES)
     me = lax.axis_index("dp")
-    for step, ref in zip(travel_order(peers), refs):
+    for step, ref in zip(order, refs):
         for t in range(pad // unit):
             for h in range(2):
                 to = pl.ds(stacked_row(step_to(step, me, peers) * pad + t * unit, h, unit), unit)
@@ -283,21 +285,31 @@
                     out[to, :] = ref[t * unit : (t + 1) * unit, at : at + HEAD_DIM]
 
 
-def part_kernel(peers, a_ref, b_ref, *outs):
+def pair_kernel(peers, own_ref, returned_ref, after_ref, *outs):
+    rows = own_ref.shape[0] // 2
+    pad = rows // peers
+    me = lax.axis_index("dp")
+    for half in range(2):
+        for step in range(peers):
+            row = half * rows + step_to(step, me, peers) * pad
+            at = pl.ds(pl.multiple_of(row, pad), pad)
+            both = own_ref[at, :].astype(F32) + returned_ref[at, :].astype(F32)
+            if half == 0:
+                outs[0][step * pad : (step + 1) * pad, :] = both
+            else:
+                part, place = divmod(step * pad, outs[1].shape[0])
+                outs[1 + part][place : place + pad, :] = both.astype(BF16)
+
+
+def sum_kernel(parts, mine_ref, *refs):
+    theirs, outs = refs[:parts], refs[parts + 1 :]
     pad = outs[0].shape[0]
-    me = lax.axis_index("dp")
     for step, out in enumerate(outs):
-        at = pl.ds(pl.multiple_of(step_to(step, me, peers) * pad, pad), pad)
-        out[...] = (a_ref[at, :] + b_ref[at, :].astype(F32)).astype(BF16)
-
-
-def add_kernel(a_ref, b_ref, after_ref, *outs):
-    at = 0
-    for out in outs:
-        size = out.shape[0]
-        both = a_ref[at : at + size, :].astype(F32) + b_ref[at : at + size, :].astype(F32)
-        out[...] = both.astype(out.dtype)
-        at += size
+        part, place = divmod(step * pad, theirs[0].shape[0])
+        out[...] = (
+            mine_ref[step * pad : (step + 1) * pad, :]
+            + theirs[part][place : place + pad, :].astype(F32)
+        ).astype(BF16)
 
 
 def call(kernel, outs, *args, scratch=(), in_specs=None, cost=None):
@@ -324,39 +336,35 @@
         pltpu.with_memory_space_constraint(a, pltpu.HBM)
         for a in (doc_lengths, dest_index, queries[0], key_rows[0], value_rows[0], grad_out[0])
     ]
-    in_hbm = pl.BlockSpec(memory_space=pltpu.HBM)
-    in_vmem = pl.BlockSpec(memory_space=pltpu.VMEM)
-
-    def loaded(*arrays):
-        return [pltpu.VMEM(a.shape, a.dtype) for a in arrays]
-
     lengths, dest, q, k, v, g = sources
-    *kv, slot = call(
+    *kv, slot, first_seen, q, g = call(
         functools.partial(sort_kernel, peers, pad),
-        [shape((pad, 2 * HEAD_DIM), BF16)] * peers + [shape((1, row_count), jnp.int32)],
+        [shape((pad, 2 * HEAD_DIM), BF16)] * peers
+        + [shape((1, row_count), jnp.int32), shape((1, 2 * rows), jnp.int32)]
+        + [shape(q.shape, BF16)] * 2,
+        lengths,
         dest,
         k,
         v,
-        in_specs=[in_hbm] * 3,
-        scratch=loaded(dest, k, v) + [pltpu.SemaphoreType.DMA((3,))],
-    )
-    *qg, first_seen = call(
-        functools.partial(follow_kernel, peers, pad),
-        [shape((pad, 4 * HEAD_DIM), BF16)] * peers + [shape((1, 2 * rows), jnp.int32)],
-        slot,
-        lengths,
         q,
         g,
-        in_specs=[in_vmem] + [in_hbm] * 3,
-        scratch=[pltpu.SMEM(lengths.shape, jnp.int32)]
-        + loaded(q, g)
-        + [pltpu.SemaphoreType.DMA((3,))],
+        in_specs=[pl.BlockSpec(memory_space=pltpu.HBM)] * 6,
+        scratch=[pltpu.SMEM(lengths.shape, jnp.int32), pltpu.VMEM(dest.shape, jnp.int32)]
+        + [pltpu.VMEM(k.shape, BF16)] * 2
+        + [pltpu.SemaphoreType.DMA((6,))],
+    )
+    qg = call(
+        functools.partial(follow_kernel, peers, pad),
+        [shape((pad, 4 * HEAD_DIM), BF16)] * peers,
+        slot,
+        q,
+        g,
         cost=pause,
     )
 
-    def exchange(pieces, home=False):
+    def exchange(pieces, home=False, order=travel_order(peers)):
         arrived = []
-        for k in travel_order(peers):
+        for k in order:
             way = [(i, receiver_of(i, k, peers)) for i in range(peers)]
             if home:
                 way = [(j, i) for i, j in way]
@@ -370,11 +378,12 @@
         return call(functools.partial(join_kernel, peers), shape((rows, 2 * HEAD_DIM), BF16), *pieces, cost=brief)
 
     kv = exchange(kv)
-    qg = exchange(qg)
+    near_first = [1, *range(peers - 1, 1, -1), 0]
+    qg = exchange(qg, order=near_first)
     sequence = lax.all_gather(join(kv), "seq", axis=0, tiled=True)
     tall = shape((2 * rows, HEAD_DIM), BF16)
     stacked = call(
-        functools.partial(stack_kernel, peers),
+        functools.partial(stack_kernel, near_first),
         [tall, tall],
         *qg,
         cost=brief,
@@ -400,16 +409,23 @@
         scratch=[pltpu.VMEM((2 * HEAD_DIM, 2 * rows), F32), pltpu.VMEM((2 * rows, HEAD_DIM), BF16)],
     )
 
+    returned = to_partner(far_grad, 1)
+    parts = PARTS
+    mine, *theirs = call(
+        functools.partial(pair_kernel, peers),
+        [shape((rows, 2 * HEAD_DIM), F32)] + [shape((rows // parts, 2 * HEAD_DIM), BF16)] * parts,
+        own_grad,
+        returned,
+        attended[0],
+        cost=pause,
+    )
     attended = exchange(attended, home=True)
-    returned = to_partner(far_grad, 1)
-    half = shape((rows, 2 * HEAD_DIM), BF16)
-    mine, theirs = call(add_kernel, [shape(half.shape, F32), half], own_grad, returned, attended[-1], cost=pause)
-    theirs = to_partner(theirs, 2)
     pair_grad = call(
-        functools.partial(part_kernel, peers),
+        functools.partial(sum_kernel, parts),
         [shape((pad, 2 * HEAD_DIM), BF16)] * peers,
         mine,
-        theirs,
+        *[to_partner(part, 2) for part in theirs],
+        attended[0],
         cost=pause,
     )
     pair_grad = exchange(pair_grad, home=True)

time: 46.4 us -> 44 us (0.948)
  Pallas kernels: 7.51 us -> 6.25 us
  waiting for transfers between devices: 6.76 us -> 5.87 us
    ppermute x12, waiting for transfers between devices: 4.94 us -> 3.55 us  [exchange(): arrived.append(lax.ppermute(pieces[k], 'dp', way) if k else pieces[k])]
    pallas_call x11, Pallas kernels: 7.51 us -> 6.25 us  [call(): pl.pallas_call(kernel, out_shape=outs, in_specs=in_specs or [pl.BlockSpec...]
    ppermute x12, starting transfers between devices: 18.7 us -> 18.2 us  [exchange(): arrived.append(lax.ppermute(pieces[k], 'dp', way) if k else pieces[k])]
    ppermute x2 -> x3, waiting for transfers between devices: 1.82 us -> 2.32 us  [to_partner(): return lax.ppermute(values, 'seq', [(i, i ^ distance) for i in range(span)])]
    ppermute x2 -> x3, starting transfers between devices: 3.85 us -> 4.23 us  [to_partner(): return lax.ppermute(values, 'seq', [(i, i ^ distance) for i in range(span)])]
  transfers between devices with their start and end apart: 14 -> 15, of which waited for: 4 -> 7; matrix products, arithmetic and copies ran while one was open for 0% -> 0% of each run, Pallas kernels for 8% -> 5%
where the time goes in v2:
time: 44 us; the launch traced here: 43.9 us
  starting transfers between devices  22.4 us (51%)
  blocking collectives  8.6 us (20%)
  Pallas kernels  6.25 us (14%)
  waiting for transfers between devices  5.87 us (13%)
  between operations  0.75 us (2%)
    ppermute x12, starting transfers between devices, exchange(): arrived.append(lax.ppermute(pieces[k], 'dp', way) if k else pieces[k])  18.2 us
    all_gather x1, blocking collectives, local(): sequence = lax.all_gather(join(kv), 'seq', axis=0, tiled=True)  8.6 us
    pallas_call x11, Pallas kernels, call(): pl.pallas_call(kernel, out_shape=outs, in_specs=in_specs or [pl.BlockSpec...  6.25 us
    ppermute x3, starting transfers between devices, to_partner(): return lax.ppermute(values, 'seq', [(i, i ^ distance) for i in range(span)])  4.23 us
    ppermute x12, waiting for transfers between devices, exchange(): arrived.append(lax.ppermute(pieces[k], 'dp', way) if k else pieces[k])  3.55 us
    ppermute x3, waiting for transfers between devices, to_partner(): return lax.ppermute(values, 'seq', [(i, i ^ distance) for i in range(span)])  2.32 us
  transfers between devices with their start and end apart: 15, of which 7 were waited for; matrix products, arithmetic and copies ran while one was open for 0% of the time, Pallas kernels for 5%

profile of v2, /device:TPU:0, one launch (start us, length us, event | category | flops | bytes accessed | tf_op | source)
XLA Modules:
  0.0 43.9 jit_solution(6091305338038940832)
XLA Ops:
  0.6 1.6 %shard_map.93 = (bf16[96,256]{1,0:T(8,128)(2,1)S(1)}, bf16[96,256]{1,0:T(8,128)(2,1)S(1)}, bf16[96,256]{1,0:T(8,128)(2,1)S(1)}, bf16[96,256]{1,0:T(8,128)(2,1)S(...) custom-call(s32[1,4]{1,0:T(1,128)} %lengths_hbm.1, ...), custom_call_target="tpu_custom_call" | custom-call | tf_op jit(solution)/shard_map/pallas_call | solution.py:316
  2.2 0.0 copy-start
  2.2 4.1 %collective-permute-start = (bf16[96,256]{1,0:T(8,128)(2,1)S(1)}, bf16[96,256]{1,0:T(8,128)(2,1)S(1)}, u32[]{:S(2)}, u32[]{:S(2)}) collective-permute-start(bf16[96,256]{1,0:T(8,128)(2,1)S(1)} %get-tuple-element.38), channel_id=1, source_target_pairs={{0,16},{8,24},{16,0},{24,8},{1,17},{9,25},{17,1},{25,9},{2,18},{10... | collective-permute-start | bytes 147464 | tf_op jit(solution)/shard_map/ppermute | solution.py:371
  6.3 1.3 %collective-permute-start.1 = (bf16[96,256]{1,0:T(8,128)(2,1)S(1)}, bf16[96,256]{1,0:T(8,128)(2,1)S(1)}, u32[]{:S(2)}, u32[]{:S(2)}) collective-permute-start(bf16[96,256]{1,0:T(8,128)(2,1)S(1)} %get-tuple-element.39), channel_id=1, source_target_pairs={{0,24},{8,16},{16,8},{24,0},{1,25},{9,17},{17,9},{25,1},{2,26},{10... | collective-permute-start | bytes 147464 | tf_op jit(solution)/shard_map/ppermute | solution.py:371
  7.7 0.2 collective-permute-start.2
  7.9 0.4 shard_map.96
  8.3 1.9 %collective-permute-start.3 = (bf16[96,512]{1,0:T(8,128)(2,1)S(1)}, bf16[96,512]{1,0:T(8,128)(2,1)S(1)}, u32[]{:S(2)}, u32[]{:S(2)}) collective-permute-start(bf16[96,512]{1,0:T(8,128)(2,1)S(1)} %get-tuple-element.44), channel_id=1, source_target_pairs={{0,8},{8,0},{16,24},{24,16},{1,9},{9,1},{17,25},{25,17},{2,10},{10... | collective-permute-start | bytes 294920 | tf_op jit(solution)/shard_map/ppermute | solution.py:371
  10.1 2.5 %collective-permute-start.4 = (bf16[96,512]{1,0:T(8,128)(2,1)S(1)}, bf16[96,512]{1,0:T(8,128)(2,1)S(1)}, u32[]{:S(2)}, u32[]{:S(2)}) collective-permute-start(bf16[96,512]{1,0:T(8,128)(2,1)S(1)} %get-tuple-element.45), channel_id=1, source_target_pairs={{0,24},{8,16},{16,8},{24,0},{1,25},{9,17},{17,9},{25,1},{2,26},{10... | collective-permute-start | bytes 294920 | tf_op jit(solution)/shard_map/ppermute | solution.py:371
  12.6 0.0 collective-permute-start.5
  12.6 0.2 collective-permute-done.2.refs_2_
  12.8 8.6 %all_gather.3.sequence_ref = bf16[1536,256]{1,0:T(8,128)(2,1)S(1)} all-gather(bf16[384,256]{1,0:T(8,128)(2,1)S(1)} %shard_map.95), channel_id=1, replica_groups=mesh['dp'=4,'seq'=4,'head'=2] {'seq'}, dimensions={0}, use_global_device_ids=true | all-gather | bytes 983040 | tf_op jit(solution)/shard_map/all_gather | solution.py:383
  21.4 0.2 shard_map.97
  21.6 1.2 %shard_map.98 = (bf16[768,256]{1,0:T(8,128)(2,1)S(1)}, bf16[768,256]{1,0:T(8,128)(2,1)S(1)}, bf16[1536,768]{1,0:T(8,128)(2,1)S(1)}, bf16[1536,768]{1,0:T(8,128)(2,1)S(1)}) custom-call(bf16[1536,256]{1,0:T(8,128)(2,1)S(1)} %all_gather.3.sequence_ref, bf16[768,128]{1,0:T(8,128)(2,1)S(1)} %get-tuple-element.48.q_ref, ...), custom_call_target="tpu_custom_call" | custom-call | tf_op jit(solution)/shard_map/pallas_call | solution.py:316
  22.9 1.3 %collective-permute-start.9 = (bf16[768,256]{1,0:T(8,128)(2,1)S(1)}, bf16[768,256]{1,0:T(8,128)(2,1)S(1)}, u32[]{:S(2)}, u32[]{:S(2)}) collective-permute-start(bf16[768,256]{1,0:T(8,128)(2,1)S(1)} %get-tuple-element.60), channel_id=1, source_target_pairs={{0,2},{2,0},{4,6},{6,4},{1,3},{3,1},{5,7},{7,5},{8,10},{10,8},{12,... | collective-permute-start | bytes 1179656 | tf_op jit(solution)/shard_map/ppermute | solution.py:375
  24.2 0.6 %shard_map.99 = (bf16[96,512]{1,0:T(8,128)(2,1)S(1)}, bf16[96,512]{1,0:T(8,128)(2,1)S(1)}, bf16[96,512]{1,0:T(8,128)(2,1)S(1)}, bf16[96,512]{1,0:T(8,128)(2,1)S(1)}) custom-call(bf16[1536,256]{1,0:T(8,128)(2,1)S(1)} %all_gather.3.sequence_ref, bf16[1536,768]{1,0:T(8,128)(2,1)S(1)} %get-tuple-element.51.low_ref, bf16[1536,768]{1,0:T(8,128)(2,1)S(1)} %get-tuple-element.52.ds_ref), custom_call_target="tpu_custom_call" | custom-call | tf_op jit(solution)/shard_map/pallas_call | solution.py:316
  24.7 2.8 %collective-permute-start.6 = (bf16[96,512]{1,0:T(8,128)(2,1)S(1)}, bf16[96,512]{1,0:T(8,128)(2,1)S(1)}, u32[]{:S(2)}, u32[]{:S(2)}) collective-permute-start(bf16[96,512]{1,0:T(8,128)(2,1)S(1)} %get-tuple-element.53), channel_id=1, source_target_pairs={{16,0},{24,8},{0,16},{8,24},{17,1},{25,9},{1,17},{9,25},{18,2},{26... | collective-permute-start | bytes 294920 | tf_op jit(solution)/shard_map/ppermute | solution.py:371
  27.6 0.1 shard_map.101
  27.7 2.9 %collective-permute-start.10 = (bf16[192,256]{1,0:T(8,128)(2,1)S(1)}, bf16[192,256]{1,0:T(8,128)(2,1)S(1)}, u32[]{:S(2)}, u32[]{:S(2)}) collective-permute-start(bf16[192,256]{1,0:T(8,128)(2,1)S(1)} %get-tuple-element.62), channel_id=1, source_target_pairs={{0,4},{2,6},{4,0},{6,2},{1,5},{3,7},{5,1},{7,3},{8,12},{10,14},{12... | collective-permute-start | bytes 294920 | tf_op jit(solution)/shard_map/ppermute | solution.py:375
  30.5 0.1 collective-permute-start.11
  30.6 1.8 %collective-permute-start.7 = (bf16[96,512]{1,0:T(8,128)(2,1)S(1)}, bf16[96,512]{1,0:T(8,128)(2,1)S(1)}, u32[]{:S(2)}, u32[]{:S(2)}) collective-permute-start(bf16[96,512]{1,0:T(8,128)(2,1)S(1)} %get-tuple-element.54), channel_id=1, source_target_pairs={{24,0},{16,8},{8,16},{0,24},{25,1},{17,9},{9,17},{1,25},{26,2},{18... | collective-permute-start | bytes 294920 | tf_op jit(solution)/shard_map/ppermute | solution.py:371
  32.3 0.9 %collective-permute-done.6.refs_0_.refs_2_ = bf16[96,512]{1,0:T(8,128)(2,1)S(1)} collective-permute-done((bf16[96,512]{1,0:T(8,128)(2,1)S(1)}, bf16[96,512]{1,0:T(8,128)(2,1)S(1)}, u32[]{:S(2)}, u32[]{:S(2)}) %collective-permute-start.6) | collective-permute-done | bytes 98336 | tf_op jit(solution)/shard_map/ppermute | solution.py:371
  33.3 0.8 %collective-permute-done.10.refs_0_ = bf16[192,256]{1,0:T(8,128)(2,1)S(1)} collective-permute-done((bf16[192,256]{1,0:T(8,128)(2,1)S(1)}, bf16[192,256]{1,0:T(8,128)(2,1)S(1)}, u32[]{:S(2)}, u32[]{:S(2)}) %collective-permute-start.10) | collective-permute-done | bytes 98336 | tf_op jit(solution)/shard_map/ppermute | solution.py:375
  34.1 1.5 %collective-permute-done.11.refs_1_ = bf16[192,256]{1,0:T(8,128)(2,1)S(1)} collective-permute-done((bf16[192,256]{1,0:T(8,128)(2,1)S(1)}, bf16[192,256]{1,0:T(8,128)(2,1)S(1)}, u32[]{:S(2)}, u32[]{:S(2)}) %collective-permute-start.11) | collective-permute-done | bytes 98336 | tf_op jit(solution)/shard_map/ppermute | solution.py:375
  35.6 0.8 %collective-permute-start.12 = (bf16[96,256]{1,0:T(8,128)(2,1)S(1)}, bf16[96,256]{1,0:T(8,128)(2,1)S(1)}, u32[]{:S(2)}, u32[]{:S(2)}) collective-permute-start(bf16[96,256]{1,0:T(8,128)(2,1)S(1)} %get-tuple-element.64), channel_id=1, source_target_pairs={{16,0},{24,8},{0,16},{8,24},{17,1},{25,9},{1,17},{9,25},{18,2},{26... | collective-permute-start | bytes 147464 | tf_op jit(solution)/shard_map/ppermute | solution.py:371
  36.4 1.9 %collective-permute-start.13 = (bf16[96,256]{1,0:T(8,128)(2,1)S(1)}, bf16[96,256]{1,0:T(8,128)(2,1)S(1)}, u32[]{:S(2)}, u32[]{:S(2)}) collective-permute-start(bf16[96,256]{1,0:T(8,128)(2,1)S(1)} %get-tuple-element.65), channel_id=1, source_target_pairs={{24,0},{16,8},{8,16},{0,24},{25,1},{17,9},{9,17},{1,25},{26,2},{18... | collective-permute-start | bytes 147464 | tf_op jit(solution)/shard_map/ppermute | solution.py:371
  38.3 0.9 %collective-permute-start.14 = (bf16[96,256]{1,0:T(8,128)(2,1)S(1)}, bf16[96,256]{1,0:T(8,128)(2,1)S(1)}, u32[]{:S(2)}, u32[]{:S(2)}) collective-permute-start(bf16[96,256]{1,0:T(8,128)(2,1)S(1)} %get-tuple-element.66), channel_id=1, source_target_pairs={{8,0},{0,8},{24,16},{16,24},{9,1},{1,9},{25,17},{17,25},{10,2},{2,... | collective-permute-start | bytes 147464 | tf_op jit(solution)/shard_map/ppermute | solution.py:371
  39.2 0.2 shard_map.94.back_ref
  39.4 1.1 %shard_map.100 = (bf16[360,256]{1,0:T(8,128)(2,1)}, bf16[360,256]{1,0:T(8,128)(2,1)}) custom-call(bf16[360,384]{1,0:T(8,128)(2,1)S(1)} %shard_map.94.back_ref, bf16[96,512]{1,0:T(8,128)(2,1)S(1)} %collective-permute-done.6.refs_0_.refs_2_, bf16[96,512]{1,0:T(8,128)(2,1)S(1)} %collective-permute-done.7.refs_1_, ...), custom_call_target="tpu_custom_call" | custom-call | tf_op jit(solution)/shard_map/pallas_call | solution.py:316
  40.5 1.2 %collective-permute-done.12.refs_0_ = bf16[96,256]{1,0:T(8,128)(2,1)S(1)} collective-permute-done((bf16[96,256]{1,0:T(8,128)(2,1)S(1)}, bf16[96,256]{1,0:T(8,128)(2,1)S(1)}, u32[]{:S(2)}, u32[]{:S(2)}) %collective-permute-start.12) | collective-permute-done | bytes 49184 | tf_op jit(solution)/shard_map/ppermute | solution.py:371
  41.7 0.8 %collective-permute-done.13.refs_1_ = bf16[96,256]{1,0:T(8,128)(2,1)S(1)} collective-permute-done((bf16[96,256]{1,0:T(8,128)(2,1)S(1)}, bf16[96,256]{1,0:T(8,128)(2,1)S(1)}, u32[]{:S(2)}, u32[]{:S(2)}) %collective-permute-start.13) | collective-permute-done | bytes 49184 | tf_op jit(solution)/shard_map/ppermute | solution.py:371
  42.5 0.4 collective-permute-done.14.refs_2_
  42.9 0.9 %shard_map.103 = (bf16[360,128]{1,0:T(8,128)(2,1)}, bf16[360,128]{1,0:T(8,128)(2,1)}) custom-call(bf16[360,384]{1,0:T(8,128)(2,1)S(1)} %shard_map.94.back_ref, bf16[96,256]{1,0:T(8,128)(2,1)S(1)} %collective-permute-done.12.refs_0_, bf16[96,256]{1,0:T(8,128)(2,1)S(1)} %collective-permute-done.13.refs_1_, ...), custom_call_target="tpu_custom_call" | custom-call | tf_op jit(solution)/shard_map/pallas_call | solution.py:316
  (14 shorter events, 0.1 us)
Async XLA Ops:
  2.2 6.1 %copy-start = (s32[1,360]{1,0:T(1,128)}, s32[1,360]{1,0:T(1,128)S(1)}, u32[]{:S(2)}) copy-start(s32[1,360]{1,0:T(1,128)S(1)} %get-tuple-element.37.slot_ref) | copy-start | bytes 4324
  2.2 10.4 %collective-permute-start = (bf16[96,256]{1,0:T(8,128)(2,1)S(1)}, bf16[96,256]{1,0:T(8,128)(2,1)S(1)}, u32[]{:S(2)}, u32[]{:S(2)}) collective-permute-start(bf16[96,256]{1,0:T(8,128)(2,1)S(1)} %get-tuple-element.38), channel_id=1, source_target_pairs={{0,16},{8,24},{16,0},{24,8},{1,17},{9,25},{17,1},{25,9},{2,18},{10... | collective-permute-start | bytes 147464 | tf_op jit(solution)/shard_map/ppermute | solution.py:371
  6.3 6.3 %collective-permute-start.1 = (bf16[96,256]{1,0:T(8,128)(2,1)S(1)}, bf16[96,256]{1,0:T(8,128)(2,1)S(1)}, u32[]{:S(2)}, u32[]{:S(2)}) collective-permute-start(bf16[96,256]{1,0:T(8,128)(2,1)S(1)} %get-tuple-element.39), channel_id=1, source_target_pairs={{0,24},{8,16},{16,8},{24,0},{1,25},{9,17},{17,9},{25,1},{2,26},{10... | collective-permute-start | bytes 147464 | tf_op jit(solution)/shard_map/ppermute | solution.py:371
  7.7 5.1 %collective-permute-start.2 = (bf16[96,256]{1,0:T(8,128)(2,1)S(1)}, bf16[96,256]{1,0:T(8,128)(2,1)S(1)}, u32[]{:S(2)}, u32[]{:S(2)}) collective-permute-start(bf16[96,256]{1,0:T(8,128)(2,1)S(1)} %get-tuple-element.40), channel_id=1, source_target_pairs={{0,8},{8,0},{16,24},{24,16},{1,9},{9,1},{17,25},{25,17},{2,10},{10... | collective-permute-start | bytes 147464 | tf_op jit(solution)/shard_map/ppermute | solution.py:371
  8.3 13.2 %collective-permute-start.3 = (bf16[96,512]{1,0:T(8,128)(2,1)S(1)}, bf16[96,512]{1,0:T(8,128)(2,1)S(1)}, u32[]{:S(2)}, u32[]{:S(2)}) collective-permute-start(bf16[96,512]{1,0:T(8,128)(2,1)S(1)} %get-tuple-element.44), channel_id=1, source_target_pairs={{0,8},{8,0},{16,24},{24,16},{1,9},{9,1},{17,25},{25,17},{2,10},{10... | collective-permute-start | bytes 294920 | tf_op jit(solution)/shard_map/ppermute | solution.py:371
  10.1 11.3 %collective-permute-start.4 = (bf16[96,512]{1,0:T(8,128)(2,1)S(1)}, bf16[96,512]{1,0:T(8,128)(2,1)S(1)}, u32[]{:S(2)}, u32[]{:S(2)}) collective-permute-start(bf16[96,512]{1,0:T(8,128)(2,1)S(1)} %get-tuple-element.45), channel_id=1, source_target_pairs={{0,24},{8,16},{16,8},{24,0},{1,25},{9,17},{17,9},{25,1},{2,26},{10... | collective-permute-start | bytes 294920 | tf_op jit(solution)/shard_map/ppermute | solution.py:371
  12.6 8.8 %collective-permute-start.5 = (bf16[96,512]{1,0:T(8,128)(2,1)S(1)}, bf16[96,512]{1,0:T(8,128)(2,1)S(1)}, u32[]{:S(2)}, u32[]{:S(2)}) collective-permute-start(bf16[96,512]{1,0:T(8,128)(2,1)S(1)} %get-tuple-element.46), channel_id=1, source_target_pairs={{0,16},{8,24},{16,0},{24,8},{1,17},{9,25},{17,1},{25,9},{2,18},{10... | collective-permute-start | bytes 294920 | tf_op jit(solution)/shard_map/ppermute | solution.py:371
  22.9 4.7 %collective-permute-start.9 = (bf16[768,256]{1,0:T(8,128)(2,1)S(1)}, bf16[768,256]{1,0:T(8,128)(2,1)S(1)}, u32[]{:S(2)}, u32[]{:S(2)}) collective-permute-start(bf16[768,256]{1,0:T(8,128)(2,1)S(1)} %get-tuple-element.60), channel_id=1, source_target_pairs={{0,2},{2,0},{4,6},{6,4},{1,3},{3,1},{5,7},{7,5},{8,10},{10,8},{12,... | collective-permute-start | bytes 1179656 | tf_op jit(solution)/shard_map/ppermute | solution.py:375
  24.7 8.5 %collective-permute-start.6 = (bf16[96,512]{1,0:T(8,128)(2,1)S(1)}, bf16[96,512]{1,0:T(8,128)(2,1)S(1)}, u32[]{:S(2)}, u32[]{:S(2)}) collective-permute-start(bf16[96,512]{1,0:T(8,128)(2,1)S(1)} %get-tuple-element.53), channel_id=1, source_target_pairs={{16,0},{24,8},{0,16},{8,24},{17,1},{25,9},{1,17},{9,25},{18,2},{26... | collective-permute-start | bytes 294920 | tf_op jit(solution)/shard_map/ppermute | solution.py:371
  27.7 6.4 %collective-permute-start.10 = (bf16[192,256]{1,0:T(8,128)(2,1)S(1)}, bf16[192,256]{1,0:T(8,128)(2,1)S(1)}, u32[]{:S(2)}, u32[]{:S(2)}) collective-permute-start(bf16[192,256]{1,0:T(8,128)(2,1)S(1)} %get-tuple-element.62), channel_id=1, source_target_pairs={{0,4},{2,6},{4,0},{6,2},{1,5},{3,7},{5,1},{7,3},{8,12},{10,14},{12... | collective-permute-start | bytes 294920 | tf_op jit(solution)/shard_map/ppermute | solution.py:375
  30.5 5.1 %collective-permute-start.11 = (bf16[192,256]{1,0:T(8,128)(2,1)S(1)}, bf16[192,256]{1,0:T(8,128)(2,1)S(1)}, u32[]{:S(2)}, u32[]{:S(2)}) collective-permute-start(bf16[192,256]{1,0:T(8,128)(2,1)S(1)} %get-tuple-element.63), channel_id=1, source_target_pairs={{0,4},{2,6},{4,0},{6,2},{1,5},{3,7},{5,1},{7,3},{8,12},{10,14},{12... | collective-permute-start | bytes 294920 | tf_op jit(solution)/shard_map/ppermute | solution.py:375
  30.6 8.8 %collective-permute-start.7 = (bf16[96,512]{1,0:T(8,128)(2,1)S(1)}, bf16[96,512]{1,0:T(8,128)(2,1)S(1)}, u32[]{:S(2)}, u32[]{:S(2)}) collective-permute-start(bf16[96,512]{1,0:T(8,128)(2,1)S(1)} %get-tuple-element.54), channel_id=1, source_target_pairs={{24,0},{16,8},{8,16},{0,24},{25,1},{17,9},{9,17},{1,25},{26,2},{18... | collective-permute-start | bytes 294920 | tf_op jit(solution)/shard_map/ppermute | solution.py:371
  32.3 7.0 %collective-permute-start.8 = (bf16[96,512]{1,0:T(8,128)(2,1)S(1)}, bf16[96,512]{1,0:T(8,128)(2,1)S(1)}, u32[]{:S(2)}, u32[]{:S(2)}) collective-permute-start(bf16[96,512]{1,0:T(8,128)(2,1)S(1)} %get-tuple-element.55), channel_id=1, source_target_pairs={{8,0},{0,8},{24,16},{16,24},{9,1},{1,9},{25,17},{17,25},{10,2},{2,... | collective-permute-start | bytes 294920 | tf_op jit(solution)/shard_map/ppermute | solution.py:371
  35.6 3.6 %copy-start.1 = (s32[1,360]{1,0:T(1,128)S(1)}, s32[1,360]{1,0:T(1,128)}, u32[]{:S(2)}) copy-start(s32[1,360]{1,0:T(1,128)} %copy-done) | copy-start | bytes 4324
  35.6 6.1 %collective-permute-start.12 = (bf16[96,256]{1,0:T(8,128)(2,1)S(1)}, bf16[96,256]{1,0:T(8,128)(2,1)S(1)}, u32[]{:S(2)}, u32[]{:S(2)}) collective-permute-start(bf16[96,256]{1,0:T(8,128)(2,1)S(1)} %get-tuple-element.64), channel_id=1, source_target_pairs={{16,0},{24,8},{0,16},{8,24},{17,1},{25,9},{1,17},{9,25},{18,2},{26... | collective-permute-start | bytes 147464 | tf_op jit(solution)/shard_map/ppermute | solution.py:371
  36.4 6.1 %collective-permute-start.13 = (bf16[96,256]{1,0:T(8,128)(2,1)S(1)}, bf16[96,256]{1,0:T(8,128)(2,1)S(1)}, u32[]{:S(2)}, u32[]{:S(2)}) collective-permute-start(bf16[96,256]{1,0:T(8,128)(2,1)S(1)} %get-tuple-element.65), channel_id=1, source_target_pairs={{24,0},{16,8},{8,16},{0,24},{25,1},{17,9},{9,17},{1,25},{26,2},{18... | collective-permute-start | bytes 147464 | tf_op jit(solution)/shard_map/ppermute | solution.py:371
  38.3 4.6 %collective-permute-start.14 = (bf16[96,256]{1,0:T(8,128)(2,1)S(1)}, bf16[96,256]{1,0:T(8,128)(2,1)S(1)}, u32[]{:S(2)}, u32[]{:S(2)}) collective-permute-start(bf16[96,256]{1,0:T(8,128)(2,1)S(1)} %get-tuple-element.66), channel_id=1, source_target_pairs={{8,0},{0,8},{24,16},{16,24},{9,1},{1,9},{25,17},{17,25},{10,2},{2,... | collective-permute-start | bytes 147464 | tf_op jit(solution)/shard_map/ppermute | solution.py:371

commit v3 on v2

--- a/solution.py
+++ b/solution.py
@@ -166,29 +166,40 @@
                 yield at // rows, slice(at, end), slice(at % rows, at % rows + end - at)
                 at = end
 
+        def tiles(window):
+            for c, at, inside in strips(window):
+                for i in range(0, at.stop - at.start, 64):
+                    yield c, slice(at.start + i, at.start + i + 64), slice(inside.start + i, inside.start + i + 64)
+
+        def fold(x):
+            return x.reshape(-1, 8, x.shape[1])
+
         def products(window, cols):
-            w_scr[window, cols] = dot(sequence_ref[window, :HEAD_DIM], q_ref[cols, :], NT)
             dp_scr[window, cols] = dot(sequence_ref[window, HEAD_DIM:], g_ref[cols, :], NT)
-
-        def weigh(window, cols):
-            parts = []
-            for c, at, inside in strips(window):
+            scores = dot(sequence_ref[window, :HEAD_DIM], q_ref[cols, :], NT)
+            peak8 = jnp.full((8, cols.stop - cols.start), neg_large, F32)
+            for c, at, inside in tiles(window):
                 allowed = offset[inside] >= first[:, cols] - c * row_count
-                if c == here:
+                if c == here and inside.stop > cols.start // 2:
                     allowed = allowed & (offset[inside] <= last[:, cols])
-                part = jnp.where(allowed, w_scr[at, cols], neg_large)
+                part = scores[at.start - window.start : at.stop - window.start]
+                part = jnp.where(allowed, part, neg_large)
                 w_scr[at, cols] = part
-                parts.append(jnp.max(part, axis=0, keepdims=True))
-            peak = functools.reduce(jnp.maximum, parts)
-            total, mean = 0.0, 0.0
-            for _, at, _ in strips(window):
+                peak8 = jnp.maximum(peak8, jnp.max(fold(part), axis=0))
+            return jnp.max(peak8, axis=0, keepdims=True)
+
+        def weigh(window, cols, peak):
+            width = cols.stop - cols.start
+            total8 = jnp.zeros((8, width), F32)
+            mean8 = jnp.zeros((8, width), F32)
+            for _, at, _ in tiles(window):
                 w = jnp.exp2((w_scr[at, cols] - peak) * factor)
                 w_scr[at, cols] = w
-                total += jnp.sum(w, axis=0, keepdims=True)
-                mean += jnp.sum(w * dp_scr[at, cols], axis=0, keepdims=True)
-            share = 1.0 / total
-            center = mean * share
-            for _, at, _ in strips(window):
+                total8 += jnp.sum(fold(w), axis=0)
+                mean8 += jnp.sum(fold(w * dp_scr[at, cols]), axis=0)
+            share = 1.0 / jnp.sum(total8, axis=0, keepdims=True)
+            center = jnp.sum(mean8, axis=0, keepdims=True) * share
+            for _, at, _ in tiles(window):
                 p = w_scr[at, cols] * share
                 low_ref[at, cols] = p.astype(BF16)
                 ds_ref[at, cols] = (p * (dp_scr[at, cols] - center)).astype(BF16)
@@ -203,14 +214,16 @@
             dv_scr[start : window.stop, :] = dv[start - window.start :]
             dk_scr[start : window.stop, :] = dk[start - window.start :]
 
-        products(*blocks[0])
         start = blocks[0][0].start
+        peak = products(*blocks[0])
+        starts = [blocks[0][0].start] + [window.stop for window, _ in blocks]
         for b, (window, cols) in enumerate(blocks):
-            if b + 1 < len(blocks):
-                products(*blocks[b + 1])
-            weigh(window, cols)
-            spread(window, cols, start)
-            start = window.stop
+            after = products(*blocks[b + 1]) if b + 1 < len(blocks) else None
+            if b:
+                spread(*blocks[b - 1], starts[b - 1])
+            weigh(window, cols, peak)
+            peak = after
+        spread(*blocks[-1], starts[len(blocks) - 1])
         for c in range(span):
             grad, half = ((own_grad_ref, 0), (far_grad_ref, 0), (own_grad_ref, 1), (far_grad_ref, 1))[here ^ c]
             to, at = slice(half * rows, (half + 1) * rows), slice(c * rows, (c + 1) * rows)

time: 44 us -> 43.1 us (0.980)
  starting transfers between devices: 22.4 us -> 21.7 us
    ppermute x3, starting transfers between devices: 4.23 us -> 3.53 us  [to_partner(): return lax.ppermute(values, 'seq', [(i, i ^ distance) for i in range(span)])]
    ppermute x3, waiting for transfers between devices: 2.32 us -> 1.67 us  [to_partner(): return lax.ppermute(values, 'seq', [(i, i ^ distance) for i in range(span)])]
    ppermute x12, waiting for transfers between devices: 3.55 us -> 4.1 us  [exchange(): arrived.append(lax.ppermute(pieces[k], 'dp', way) if k else pieces[k])]
where the time goes in v3:
time: 43.1 us; the launch traced here: 43 us
  starting transfers between devices  21.7 us (50%)
  blocking collectives  8.6 us (20%)
  Pallas kernels  6.16 us (14%)
  waiting for transfers between devices  5.76 us (13%)
  between operations  0.75 us (2%)
    ppermute x12, starting transfers between devices, exchange(): arrived.append(lax.ppermute(pieces[k], 'dp', way) if k else pieces[k])  18.2 us
    all_gather x1, blocking collectives, local(): sequence = lax.all_gather(join(kv), 'seq', axis=0, tiled=True)  8.6 us
    pallas_call x11, Pallas kernels, call(): pl.pallas_call(kernel, out_shape=outs, in_specs=in_specs or [pl.BlockSpec...  6.16 us
    ppermute x12, waiting for transfers between devices, exchange(): arrived.append(lax.ppermute(pieces[k], 'dp', way) if k else pieces[k])  4.1 us
    ppermute x3, starting transfers between devices, to_partner(): return lax.ppermute(values, 'seq', [(i, i ^ distance) for i in range(span)])  3.53 us
    ppermute x3, waiting for transfers between devices, to_partner(): return lax.ppermute(values, 'seq', [(i, i ^ distance) for i in range(span)])  1.67 us
  transfers between devices with their start and end apart: 15, of which 7 were waited for; matrix products, arithmetic and copies ran while one was open for 0% of the time, Pallas kernels for 5%

profile of v3, /device:TPU:0, one launch (start us, length us, event | category | flops | bytes accessed | tf_op | source)
XLA Modules:
  0.0 43.0 jit_solution(15598795237823516051)
XLA Ops:
  0.6 1.6 %shard_map.93 = (bf16[96,256]{1,0:T(8,128)(2,1)S(1)}, bf16[96,256]{1,0:T(8,128)(2,1)S(1)}, bf16[96,256]{1,0:T(8,128)(2,1)S(1)}, bf16[96,256]{1,0:T(8,128)(2,1)S(...) custom-call(s32[1,4]{1,0:T(1,128)} %lengths_hbm.1, ...), custom_call_target="tpu_custom_call" | custom-call | tf_op jit(solution)/shard_map/pallas_call | solution.py:329
  2.2 0.0 copy-start
  2.2 4.1 %collective-permute-start = (bf16[96,256]{1,0:T(8,128)(2,1)S(1)}, bf16[96,256]{1,0:T(8,128)(2,1)S(1)}, u32[]{:S(2)}, u32[]{:S(2)}) collective-permute-start(bf16[96,256]{1,0:T(8,128)(2,1)S(1)} %get-tuple-element.38), channel_id=1, source_target_pairs={{0,16},{8,24},{16,0},{24,8},{1,17},{9,25},{17,1},{25,9},{2,18},{10... | collective-permute-start | bytes 147464 | tf_op jit(solution)/shard_map/ppermute | solution.py:384
  6.3 1.3 %collective-permute-start.1 = (bf16[96,256]{1,0:T(8,128)(2,1)S(1)}, bf16[96,256]{1,0:T(8,128)(2,1)S(1)}, u32[]{:S(2)}, u32[]{:S(2)}) collective-permute-start(bf16[96,256]{1,0:T(8,128)(2,1)S(1)} %get-tuple-element.39), channel_id=1, source_target_pairs={{0,24},{8,16},{16,8},{24,0},{1,25},{9,17},{17,9},{25,1},{2,26},{10... | collective-permute-start | bytes 147464 | tf_op jit(solution)/shard_map/ppermute | solution.py:384
  7.7 0.2 collective-permute-start.2
  7.9 0.4 shard_map.96
  8.3 1.9 %collective-permute-start.3 = (bf16[96,512]{1,0:T(8,128)(2,1)S(1)}, bf16[96,512]{1,0:T(8,128)(2,1)S(1)}, u32[]{:S(2)}, u32[]{:S(2)}) collective-permute-start(bf16[96,512]{1,0:T(8,128)(2,1)S(1)} %get-tuple-element.44), channel_id=1, source_target_pairs={{0,8},{8,0},{16,24},{24,16},{1,9},{9,1},{17,25},{25,17},{2,10},{10... | collective-permute-start | bytes 294920 | tf_op jit(solution)/shard_map/ppermute | solution.py:384
  10.1 2.5 %collective-permute-start.4 = (bf16[96,512]{1,0:T(8,128)(2,1)S(1)}, bf16[96,512]{1,0:T(8,128)(2,1)S(1)}, u32[]{:S(2)}, u32[]{:S(2)}) collective-permute-start(bf16[96,512]{1,0:T(8,128)(2,1)S(1)} %get-tuple-element.45), channel_id=1, source_target_pairs={{0,24},{8,16},{16,8},{24,0},{1,25},{9,17},{17,9},{25,1},{2,26},{10... | collective-permute-start | bytes 294920 | tf_op jit(solution)/shard_map/ppermute | solution.py:384
  12.6 0.0 collective-permute-done.refs_0_
  12.6 0.2 collective-permute-done.2.refs_2_
  12.8 8.6 %all_gather.3.sequence_ref = bf16[1536,256]{1,0:T(8,128)(2,1)S(1)} all-gather(bf16[384,256]{1,0:T(8,128)(2,1)S(1)} %shard_map.95), channel_id=1, replica_groups=mesh['dp'=4,'seq'=4,'head'=2] {'seq'}, dimensions={0}, use_global_device_ids=true | all-gather | bytes 983040 | tf_op jit(solution)/shard_map/all_gather | solution.py:396
  21.4 0.2 shard_map.97
  21.6 1.2 %shard_map.98 = (bf16[768,256]{1,0:T(8,128)(2,1)S(1)}, bf16[768,256]{1,0:T(8,128)(2,1)S(1)}, bf16[1536,768]{1,0:T(8,128)(2,1)S(1)}, bf16[1536,768]{1,0:T(8,128)(2,1)S(1)}) custom-call(bf16[1536,256]{1,0:T(8,128)(2,1)S(1)} %all_gather.3.sequence_ref, bf16[768,128]{1,0:T(8,128)(2,1)S(1)} %get-tuple-element.48.q_ref, ...), custom_call_target="tpu_custom_call" | custom-call | tf_op jit(solution)/shard_map/pallas_call | solution.py:329
  22.8 1.1 %collective-permute-start.9 = (bf16[768,256]{1,0:T(8,128)(2,1)S(1)}, bf16[768,256]{1,0:T(8,128)(2,1)S(1)}, u32[]{:S(2)}, u32[]{:S(2)}) collective-permute-start(bf16[768,256]{1,0:T(8,128)(2,1)S(1)} %get-tuple-element.60), channel_id=1, source_target_pairs={{0,2},{2,0},{4,6},{6,4},{1,3},{3,1},{5,7},{7,5},{8,10},{10,8},{12,... | collective-permute-start | bytes 1179656 | tf_op jit(solution)/shard_map/ppermute | solution.py:388
  23.9 0.6 %shard_map.99 = (bf16[96,512]{1,0:T(8,128)(2,1)S(1)}, bf16[96,512]{1,0:T(8,128)(2,1)S(1)}, bf16[96,512]{1,0:T(8,128)(2,1)S(1)}, bf16[96,512]{1,0:T(8,128)(2,1)S(1)}) custom-call(bf16[1536,256]{1,0:T(8,128)(2,1)S(1)} %all_gather.3.sequence_ref, bf16[1536,768]{1,0:T(8,128)(2,1)S(1)} %get-tuple-element.51.low_ref, bf16[1536,768]{1,0:T(8,128)(2,1)S(1)} %get-tuple-element.52.ds_ref), custom_call_target="tpu_custom_call" | custom-call | tf_op jit(solution)/shard_map/pallas_call | solution.py:329
  24.5 2.8 %collective-permute-start.6 = (bf16[96,512]{1,0:T(8,128)(2,1)S(1)}, bf16[96,512]{1,0:T(8,128)(2,1)S(1)}, u32[]{:S(2)}, u32[]{:S(2)}) collective-permute-start(bf16[96,512]{1,0:T(8,128)(2,1)S(1)} %get-tuple-element.53), channel_id=1, source_target_pairs={{16,0},{24,8},{0,16},{8,24},{17,1},{25,9},{1,17},{9,25},{18,2},{26... | collective-permute-start | bytes 294920 | tf_op jit(solution)/shard_map/ppermute | solution.py:384
  27.3 0.1 shard_map.101
  27.4 2.4 %collective-permute-start.10 = (bf16[192,256]{1,0:T(8,128)(2,1)S(1)}, bf16[192,256]{1,0:T(8,128)(2,1)S(1)}, u32[]{:S(2)}, u32[]{:S(2)}) collective-permute-start(bf16[192,256]{1,0:T(8,128)(2,1)S(1)} %get-tuple-element.62), channel_id=1, source_target_pairs={{0,4},{2,6},{4,0},{6,2},{1,5},{3,7},{5,1},{7,3},{8,12},{10,14},{12... | collective-permute-start | bytes 294920 | tf_op jit(solution)/shard_map/ppermute | solution.py:388
  29.7 0.1 collective-permute-start.11
  29.8 1.8 %collective-permute-start.7 = (bf16[96,512]{1,0:T(8,128)(2,1)S(1)}, bf16[96,512]{1,0:T(8,128)(2,1)S(1)}, u32[]{:S(2)}, u32[]{:S(2)}) collective-permute-start(bf16[96,512]{1,0:T(8,128)(2,1)S(1)} %get-tuple-element.54), channel_id=1, source_target_pairs={{24,0},{16,8},{8,16},{0,24},{25,1},{17,9},{9,17},{1,25},{26,2},{18... | collective-permute-start | bytes 294920 | tf_op jit(solution)/shard_map/ppermute | solution.py:384
  31.6 1.4 %collective-permute-done.6.refs_0_.refs_2_ = bf16[96,512]{1,0:T(8,128)(2,1)S(1)} collective-permute-done((bf16[96,512]{1,0:T(8,128)(2,1)S(1)}, bf16[96,512]{1,0:T(8,128)(2,1)S(1)}, u32[]{:S(2)}, u32[]{:S(2)}) %collective-permute-start.6) | collective-permute-done | bytes 98336 | tf_op jit(solution)/shard_map/ppermute | solution.py:384
  33.0 0.3 collective-permute-done.10.refs_0_
  33.2 1.4 %collective-permute-done.11.refs_1_ = bf16[192,256]{1,0:T(8,128)(2,1)S(1)} collective-permute-done((bf16[192,256]{1,0:T(8,128)(2,1)S(1)}, bf16[192,256]{1,0:T(8,128)(2,1)S(1)}, u32[]{:S(2)}, u32[]{:S(2)}) %collective-permute-start.11) | collective-permute-done | bytes 98336 | tf_op jit(solution)/shard_map/ppermute | solution.py:388
  34.7 1.0 %collective-permute-start.12 = (bf16[96,256]{1,0:T(8,128)(2,1)S(1)}, bf16[96,256]{1,0:T(8,128)(2,1)S(1)}, u32[]{:S(2)}, u32[]{:S(2)}) collective-permute-start(bf16[96,256]{1,0:T(8,128)(2,1)S(1)} %get-tuple-element.64), channel_id=1, source_target_pairs={{16,0},{24,8},{0,16},{8,24},{17,1},{25,9},{1,17},{9,25},{18,2},{26... | collective-permute-start | bytes 147464 | tf_op jit(solution)/shard_map/ppermute | solution.py:384
  35.7 1.8 %collective-permute-start.13 = (bf16[96,256]{1,0:T(8,128)(2,1)S(1)}, bf16[96,256]{1,0:T(8,128)(2,1)S(1)}, u32[]{:S(2)}, u32[]{:S(2)}) collective-permute-start(bf16[96,256]{1,0:T(8,128)(2,1)S(1)} %get-tuple-element.65), channel_id=1, source_target_pairs={{24,0},{16,8},{8,16},{0,24},{25,1},{17,9},{9,17},{1,25},{26,2},{18... | collective-permute-start | bytes 147464 | tf_op jit(solution)/shard_map/ppermute | solution.py:384
  37.4 0.8 %collective-permute-start.14 = (bf16[96,256]{1,0:T(8,128)(2,1)S(1)}, bf16[96,256]{1,0:T(8,128)(2,1)S(1)}, u32[]{:S(2)}, u32[]{:S(2)}) collective-permute-start(bf16[96,256]{1,0:T(8,128)(2,1)S(1)} %get-tuple-element.66), channel_id=1, source_target_pairs={{8,0},{0,8},{24,16},{16,24},{9,1},{1,9},{25,17},{17,25},{10,2},{2,... | collective-permute-start | bytes 147464 | tf_op jit(solution)/shard_map/ppermute | solution.py:384
  38.2 0.2 shard_map.94.back_ref
  38.4 1.1 %shard_map.100 = (bf16[360,256]{1,0:T(8,128)(2,1)}, bf16[360,256]{1,0:T(8,128)(2,1)}) custom-call(bf16[360,384]{1,0:T(8,128)(2,1)S(1)} %shard_map.94.back_ref, bf16[96,512]{1,0:T(8,128)(2,1)S(1)} %collective-permute-done.6.refs_0_.refs_2_, bf16[96,512]{1,0:T(8,128)(2,1)S(1)} %collective-permute-done.7.refs_1_, ...), custom_call_target="tpu_custom_call" | custom-call | tf_op jit(solution)/shard_map/pallas_call | solution.py:329
  39.5 1.1 %collective-permute-done.12.refs_0_ = bf16[96,256]{1,0:T(8,128)(2,1)S(1)} collective-permute-done((bf16[96,256]{1,0:T(8,128)(2,1)S(1)}, bf16[96,256]{1,0:T(8,128)(2,1)S(1)}, u32[]{:S(2)}, u32[]{:S(2)}) %collective-permute-start.12) | collective-permute-done | bytes 49184 | tf_op jit(solution)/shard_map/ppermute | solution.py:384
  40.6 1.1 %collective-permute-done.13.refs_1_ = bf16[96,256]{1,0:T(8,128)(2,1)S(1)} collective-permute-done((bf16[96,256]{1,0:T(8,128)(2,1)S(1)}, bf16[96,256]{1,0:T(8,128)(2,1)S(1)}, u32[]{:S(2)}, u32[]{:S(2)}) %collective-permute-start.13) | collective-permute-done | bytes 49184 | tf_op jit(solution)/shard_map/ppermute | solution.py:384
  41.7 0.3 collective-permute-done.14.refs_2_
  42.0 0.9 %shard_map.103 = (bf16[360,128]{1,0:T(8,128)(2,1)}, bf16[360,128]{1,0:T(8,128)(2,1)}) custom-call(bf16[360,384]{1,0:T(8,128)(2,1)S(1)} %shard_map.94.back_ref, bf16[96,256]{1,0:T(8,128)(2,1)S(1)} %collective-permute-done.12.refs_0_, bf16[96,256]{1,0:T(8,128)(2,1)S(1)} %collective-permute-done.13.refs_1_, ...), custom_call_target="tpu_custom_call" | custom-call | tf_op jit(solution)/shard_map/pallas_call | solution.py:329
  (14 shorter events, 0.1 us)
Async XLA Ops:
  2.2 6.1 %copy-start = (s32[1,360]{1,0:T(1,128)}, s32[1,360]{1,0:T(1,128)S(1)}, u32[]{:S(2)}) copy-start(s32[1,360]{1,0:T(1,128)S(1)} %get-tuple-element.37.slot_ref) | copy-start | bytes 4324
  2.2 10.4 %collective-permute-start = (bf16[96,256]{1,0:T(8,128)(2,1)S(1)}, bf16[96,256]{1,0:T(8,128)(2,1)S(1)}, u32[]{:S(2)}, u32[]{:S(2)}) collective-permute-start(bf16[96,256]{1,0:T(8,128)(2,1)S(1)} %get-tuple-element.38), channel_id=1, source_target_pairs={{0,16},{8,24},{16,0},{24,8},{1,17},{9,25},{17,1},{25,9},{2,18},{10... | collective-permute-start | bytes 147464 | tf_op jit(solution)/shard_map/ppermute | solution.py:384
  6.3 6.3 %collective-permute-start.1 = (bf16[96,256]{1,0:T(8,128)(2,1)S(1)}, bf16[96,256]{1,0:T(8,128)(2,1)S(1)}, u32[]{:S(2)}, u32[]{:S(2)}) collective-permute-start(bf16[96,256]{1,0:T(8,128)(2,1)S(1)} %get-tuple-element.39), channel_id=1, source_target_pairs={{0,24},{8,16},{16,8},{24,0},{1,25},{9,17},{17,9},{25,1},{2,26},{10... | collective-permute-start | bytes 147464 | tf_op jit(solution)/shard_map/ppermute | solution.py:384
  7.7 5.1 %collective-permute-start.2 = (bf16[96,256]{1,0:T(8,128)(2,1)S(1)}, bf16[96,256]{1,0:T(8,128)(2,1)S(1)}, u32[]{:S(2)}, u32[]{:S(2)}) collective-permute-start(bf16[96,256]{1,0:T(8,128)(2,1)S(1)} %get-tuple-element.40), channel_id=1, source_target_pairs={{0,8},{8,0},{16,24},{24,16},{1,9},{9,1},{17,25},{25,17},{2,10},{10... | collective-permute-start | bytes 147464 | tf_op jit(solution)/shard_map/ppermute | solution.py:384
  8.3 13.2 %collective-permute-start.3 = (bf16[96,512]{1,0:T(8,128)(2,1)S(1)}, bf16[96,512]{1,0:T(8,128)(2,1)S(1)}, u32[]{:S(2)}, u32[]{:S(2)}) collective-permute-start(bf16[96,512]{1,0:T(8,128)(2,1)S(1)} %get-tuple-element.44), channel_id=1, source_target_pairs={{0,8},{8,0},{16,24},{24,16},{1,9},{9,1},{17,25},{25,17},{2,10},{10... | collective-permute-start | bytes 294920 | tf_op jit(solution)/shard_map/ppermute | solution.py:384
  10.1 11.3 %collective-permute-start.4 = (bf16[96,512]{1,0:T(8,128)(2,1)S(1)}, bf16[96,512]{1,0:T(8,128)(2,1)S(1)}, u32[]{:S(2)}, u32[]{:S(2)}) collective-permute-start(bf16[96,512]{1,0:T(8,128)(2,1)S(1)} %get-tuple-element.45), channel_id=1, source_target_pairs={{0,24},{8,16},{16,8},{24,0},{1,25},{9,17},{17,9},{25,1},{2,26},{10... | collective-permute-start | bytes 294920 | tf_op jit(solution)/shard_map/ppermute | solution.py:384
  12.6 8.8 %collective-permute-start.5 = (bf16[96,512]{1,0:T(8,128)(2,1)S(1)}, bf16[96,512]{1,0:T(8,128)(2,1)S(1)}, u32[]{:S(2)}, u32[]{:S(2)}) collective-permute-start(bf16[96,512]{1,0:T(8,128)(2,1)S(1)} %get-tuple-element.46), channel_id=1, source_target_pairs={{0,16},{8,24},{16,0},{24,8},{1,17},{9,25},{17,1},{25,9},{2,18},{10... | collective-permute-start | bytes 294920 | tf_op jit(solution)/shard_map/ppermute | solution.py:384
  22.8 4.5 %collective-permute-start.9 = (bf16[768,256]{1,0:T(8,128)(2,1)S(1)}, bf16[768,256]{1,0:T(8,128)(2,1)S(1)}, u32[]{:S(2)}, u32[]{:S(2)}) collective-permute-start(bf16[768,256]{1,0:T(8,128)(2,1)S(1)} %get-tuple-element.60), channel_id=1, source_target_pairs={{0,2},{2,0},{4,6},{6,4},{1,3},{3,1},{5,7},{7,5},{8,10},{10,8},{12,... | collective-permute-start | bytes 1179656 | tf_op jit(solution)/shard_map/ppermute | solution.py:388
  24.5 8.5 %collective-permute-start.6 = (bf16[96,512]{1,0:T(8,128)(2,1)S(1)}, bf16[96,512]{1,0:T(8,128)(2,1)S(1)}, u32[]{:S(2)}, u32[]{:S(2)}) collective-permute-start(bf16[96,512]{1,0:T(8,128)(2,1)S(1)} %get-tuple-element.53), channel_id=1, source_target_pairs={{16,0},{24,8},{0,16},{8,24},{17,1},{25,9},{1,17},{9,25},{18,2},{26... | collective-permute-start | bytes 294920 | tf_op jit(solution)/shard_map/ppermute | solution.py:384
  27.4 5.9 %collective-permute-start.10 = (bf16[192,256]{1,0:T(8,128)(2,1)S(1)}, bf16[192,256]{1,0:T(8,128)(2,1)S(1)}, u32[]{:S(2)}, u32[]{:S(2)}) collective-permute-start(bf16[192,256]{1,0:T(8,128)(2,1)S(1)} %get-tuple-element.62), channel_id=1, source_target_pairs={{0,4},{2,6},{4,0},{6,2},{1,5},{3,7},{5,1},{7,3},{8,12},{10,14},{12... | collective-permute-start | bytes 294920 | tf_op jit(solution)/shard_map/ppermute | solution.py:388
  29.7 4.9 %collective-permute-start.11 = (bf16[192,256]{1,0:T(8,128)(2,1)S(1)}, bf16[192,256]{1,0:T(8,128)(2,1)S(1)}, u32[]{:S(2)}, u32[]{:S(2)}) collective-permute-start(bf16[192,256]{1,0:T(8,128)(2,1)S(1)} %get-tuple-element.63), channel_id=1, source_target_pairs={{0,4},{2,6},{4,0},{6,2},{1,5},{3,7},{5,1},{7,3},{8,12},{10,14},{12... | collective-permute-start | bytes 294920 | tf_op jit(solution)/shard_map/ppermute | solution.py:388
  29.8 8.6 %collective-permute-start.7 = (bf16[96,512]{1,0:T(8,128)(2,1)S(1)}, bf16[96,512]{1,0:T(8,128)(2,1)S(1)}, u32[]{:S(2)}, u32[]{:S(2)}) collective-permute-start(bf16[96,512]{1,0:T(8,128)(2,1)S(1)} %get-tuple-element.54), channel_id=1, source_target_pairs={{24,0},{16,8},{8,16},{0,24},{25,1},{17,9},{9,17},{1,25},{26,2},{18... | collective-permute-start | bytes 294920 | tf_op jit(solution)/shard_map/ppermute | solution.py:384
  31.6 6.9 %collective-permute-start.8 = (bf16[96,512]{1,0:T(8,128)(2,1)S(1)}, bf16[96,512]{1,0:T(8,128)(2,1)S(1)}, u32[]{:S(2)}, u32[]{:S(2)}) collective-permute-start(bf16[96,512]{1,0:T(8,128)(2,1)S(1)} %get-tuple-element.55), channel_id=1, source_target_pairs={{8,0},{0,8},{24,16},{16,24},{9,1},{1,9},{25,17},{17,25},{10,2},{2,... | collective-permute-start | bytes 294920 | tf_op jit(solution)/shard_map/ppermute | solution.py:384
  34.6 3.6 %copy-start.1 = (s32[1,360]{1,0:T(1,128)S(1)}, s32[1,360]{1,0:T(1,128)}, u32[]{:S(2)}) copy-start(s32[1,360]{1,0:T(1,128)} %copy-done) | copy-start | bytes 4324
  34.7 5.9 %collective-permute-start.12 = (bf16[96,256]{1,0:T(8,128)(2,1)S(1)}, bf16[96,256]{1,0:T(8,128)(2,1)S(1)}, u32[]{:S(2)}, u32[]{:S(2)}) collective-permute-start(bf16[96,256]{1,0:T(8,128)(2,1)S(1)} %get-tuple-element.64), channel_id=1, source_target_pairs={{16,0},{24,8},{0,16},{8,24},{17,1},{25,9},{1,17},{9,25},{18,2},{26... | collective-permute-start | bytes 147464 | tf_op jit(solution)/shard_map/ppermute | solution.py:384
  35.7 6.0 %collective-permute-start.13 = (bf16[96,256]{1,0:T(8,128)(2,1)S(1)}, bf16[96,256]{1,0:T(8,128)(2,1)S(1)}, u32[]{:S(2)}, u32[]{:S(2)}) collective-permute-start(bf16[96,256]{1,0:T(8,128)(2,1)S(1)} %get-tuple-element.65), channel_id=1, source_target_pairs={{24,0},{16,8},{8,16},{0,24},{25,1},{17,9},{9,17},{1,25},{26,2},{18... | collective-permute-start | bytes 147464 | tf_op jit(solution)/shard_map/ppermute | solution.py:384
  37.4 4.6 %collective-permute-start.14 = (bf16[96,256]{1,0:T(8,128)(2,1)S(1)}, bf16[96,256]{1,0:T(8,128)(2,1)S(1)}, u32[]{:S(2)}, u32[]{:S(2)}) collective-permute-start(bf16[96,256]{1,0:T(8,128)(2,1)S(1)} %get-tuple-element.66), channel_id=1, source_target_pairs={{8,0},{0,8},{24,16},{16,24},{9,1},{1,9},{25,17},{17,25},{10,2},{2,... | collective-permute-start | bytes 147464 | tf_op jit(solution)/shard_map/ppermute | solution.py:384

commit v4 on v3

--- a/solution.py
+++ b/solution.py
@@ -69,11 +69,11 @@
 
 def sort_kernel(peers, pad, lengths_hbm, dest_hbm, k_hbm, v_hbm, q_hbm, g_hbm, *refs):
     outs, slot_ref, first_ref, q_ref, g_ref = refs[:peers], *refs[peers : peers + 4]
-    lengths_ref, dest_ref, k_ref, v_ref, sems = refs[peers + 4 :]
+    lengths_ref, dest_ref, kv_ref, sems = refs[peers + 4 :]
     loads = (
         (dest_hbm, dest_ref),
-        (k_hbm, k_ref),
-        (v_hbm, v_ref),
+        (k_hbm, kv_ref.at[:, :HEAD_DIM]),
+        (v_hbm, kv_ref.at[:, HEAD_DIM:]),
         (lengths_hbm, lengths_ref),
         (q_hbm, q_ref),
         (g_hbm, g_ref),
@@ -81,7 +81,7 @@
     copies = [pltpu.make_async_copy(*pair, sems.at[i]) for i, pair in enumerate(loads)]
     for copy in copies:
         copy.start()
-    rows = k_ref.shape[0]
+    rows = kv_ref.shape[0]
     me = lax.axis_index("dp")
     wide = -(-peers // TILE) * TILE
     lane = lax.broadcasted_iota(jnp.int32, (wide, rows), 0)
@@ -96,11 +96,11 @@
     slot = slot.astype(jnp.int32)
     slot_ref[...] = slot
     place = place_of(slot, peers * pad)
-    for copy, ref, at in zip(copies[1:3], (k_ref, v_ref), (0, 1)):
+    for copy in copies[1:3]:
         copy.wait()
-        moved = dot(place, ref[...]).astype(BF16)
-        for p in range(peers):
-            outs[p][:, at * HEAD_DIM : (at + 1) * HEAD_DIM] = moved[p * pad : (p + 1) * pad]
+    moved = dot(place, kv_ref[...]).astype(BF16)
+    for p in range(peers):
+        outs[p][...] = moved[p * pad : (p + 1) * pad]
     copies[3].wait()
     query_pos = query_positions(peers * pad, pad, rows) + lax.axis_index("seq") * rows
     first = jnp.maximum(query_pos - (WINDOW - 1), 0)
@@ -145,9 +145,25 @@
     return blocks
 
 
-def attend_kernel(peers, pad, row_count, span, sequence_ref, q_ref, g_ref, first_ref, *refs):
-    own_grad_ref, far_grad_ref, low_ref, ds_ref = refs[:4]
-    w_scr, dp_scr, dv_scr, dk_scr = refs[4:]
+def stack(order, pieces, stacks):
+    peers = len(order)
+    pad = pieces[0].shape[0]
+    unit = math.gcd(pad, LANES)
+    me = lax.axis_index("dp")
+    for step, piece in zip(order, pieces):
+        for t in range(pad // unit):
+            for h in range(2):
+                to = pl.ds(stacked_row(step_to(step, me, peers) * pad + t * unit, h, unit), unit)
+                for column, out in enumerate(stacks):
+                    at = (2 * column + h) * HEAD_DIM
+                    out[to, :] = piece[t * unit : (t + 1) * unit, at : at + HEAD_DIM]
+
+
+def attend_kernel(order, pad, row_count, span, sequence_ref, first_ref, *refs):
+    peers = len(order)
+    own_grad_ref, far_grad_ref, low_ref, ds_ref = refs[peers : peers + 4]
+    w_scr, dp_scr, dv_scr, dk_scr, q_ref, g_ref = refs[peers + 4 :]
+    stack(order, refs[:peers], (q_ref, g_ref))
     rows = peers * pad
     shard = lax.axis_index("seq")
     factor = score_scale * log2_e
@@ -244,18 +260,21 @@
     shard = lax.axis_index("seq")
 
     def gather(here):
-        for window, cols in windows(here, rows, pad, row_count):
-            turned_scr[:HEAD_DIM, cols] = dot(sequence_ref[window, HEAD_DIM:], low_ref[window, cols], TN)
-            turned_scr[HEAD_DIM:, cols] = (
-                dot(sequence_ref[window, :HEAD_DIM], ds_ref[window, cols], TN) * score_scale
-            )
+        blocks = windows(here, rows, pad, row_count)
+        seen = slice(blocks[0][0].start, blocks[-1][0].stop)
+        keys, values = sequence_ref[seen, :HEAD_DIM].T, sequence_ref[seen, HEAD_DIM:].T
+        for window, cols in blocks:
+            part = slice(window.start - seen.start, window.stop - seen.start)
+            turned_scr[:HEAD_DIM, cols] = dot(values[:, part], low_ref[window, cols]).astype(BF16)
+            dq = dot(keys[:, part], ds_ref[window, cols]) * score_scale
+            turned_scr[HEAD_DIM:, cols] = dq.astype(BF16)
 
     for here in range(span):
         pl.when(shard == here)(functools.partial(gather, here))
 
     unit = math.gcd(pad, LANES)
     for column in range(2):
-        whole_scr[...] = turned_scr[column * HEAD_DIM : (column + 1) * HEAD_DIM, :].T.astype(BF16)
+        whole_scr[...] = turned_scr[column * HEAD_DIM : (column + 1) * HEAD_DIM, :].T
         for p in range(peers):
             for t in range(pad // unit):
                 for h in range(2):
@@ -281,21 +300,6 @@
     me = lax.axis_index("dp")
     for step, ref in zip(travel_order(peers), refs):
         whole[pl.ds(pl.multiple_of(step_to(step, me, peers) * pad, pad), pad), :] = ref[...]
-
-
-def stack_kernel(order, *refs):
-    peers = len(order)
-    stacks = refs[peers:]
-    pad = refs[0].shape[0]
-    unit = math.gcd(pad, LANES)
-    me = lax.axis_index("dp")
-    for step, ref in zip(order, refs):
-        for t in range(pad // unit):
-            for h in range(2):
-                to = pl.ds(stacked_row(step_to(step, me, peers) * pad + t * unit, h, unit), unit)
-                for column, out in enumerate(stacks):
-                    at = (2 * column + h) * HEAD_DIM
-                    out[to, :] = ref[t * unit : (t + 1) * unit, at : at + HEAD_DIM]
 
 
 def pair_kernel(peers, own_ref, returned_ref, after_ref, *outs):
@@ -363,7 +367,7 @@
         g,
         in_specs=[pl.BlockSpec(memory_space=pltpu.HBM)] * 6,
         scratch=[pltpu.SMEM(lengths.shape, jnp.int32), pltpu.VMEM(dest.shape, jnp.int32)]
-        + [pltpu.VMEM(k.shape, BF16)] * 2
+        + [pltpu.VMEM((row_count, 2 * HEAD_DIM), BF16)]
         + [pltpu.SemaphoreType.DMA((6,))],
     )
     qg = call(
@@ -394,24 +398,18 @@
     near_first = [1, *range(peers - 1, 1, -1), 0]
     qg = exchange(qg, order=near_first)
     sequence = lax.all_gather(join(kv), "seq", axis=0, tiled=True)
-    tall = shape((2 * rows, HEAD_DIM), BF16)
-    stacked = call(
-        functools.partial(stack_kernel, near_first),
-        [tall, tall],
-        *qg,
-        cost=brief,
-    )
-
     back = call(back_kernel, shape((row_count, rows), BF16), slot)
 
     wide = (span * rows, 2 * rows)
     own_grad, far_grad, low, ds = call(
-        functools.partial(attend_kernel, peers, pad, row_count, span),
+        functools.partial(attend_kernel, near_first, pad, row_count, span),
         [shape((2 * rows, 2 * HEAD_DIM), BF16)] * 2 + [shape(wide, BF16)] * 2,
         sequence,
-        *stacked,
         first_seen,
-        scratch=[pltpu.VMEM(wide, F32)] * 2 + [pltpu.VMEM((span * rows, HEAD_DIM), F32)] * 2,
+        *qg,
+        scratch=[pltpu.VMEM(wide, F32)] * 2
+        + [pltpu.VMEM((span * rows, HEAD_DIM), F32)] * 2
+        + [pltpu.VMEM((2 * rows, HEAD_DIM), BF16)] * 2,
     )
     attended = call(
         functools.partial(gather_kernel, peers, pad, row_count, span),
@@ -419,7 +417,7 @@
         sequence,
         low,
         ds,
-        scratch=[pltpu.VMEM((2 * HEAD_DIM, 2 * rows), F32), pltpu.VMEM((2 * rows, HEAD_DIM), BF16)],
+        scratch=[pltpu.VMEM((2 * HEAD_DIM, 2 * rows), BF16), pltpu.VMEM((2 * rows, HEAD_DIM), BF16)],
     )
 
     returned = to_partner(far_grad, 1)

time: 43.1 us -> 42.9 us (level)
    pallas_call x11 -> x10, Pallas kernels: 6.16 us -> 5.89 us  [call(): pl.pallas_call(kernel, out_shape=outs, in_specs=in_specs or [pl.BlockSpec...]
where the time goes in v4:
time: 42.9 us; the launch traced here: 42.7 us
  starting transfers between devices  21.7 us (51%)
  blocking collectives  8.6 us (20%)
  Pallas kernels  5.89 us (14%)
  waiting for transfers between devices  5.78 us (13%)
  between operations  0.74 us (2%)
    ppermute x12, starting transfers between devices, exchange(): arrived.append(lax.ppermute(pieces[k], 'dp', way) if k else pieces[k])  18.2 us
    all_gather x1, blocking collectives, local(): sequence = lax.all_gather(join(kv), 'seq', axis=0, tiled=True)  8.6 us
    pallas_call x10, Pallas kernels, call(): pl.pallas_call(kernel, out_shape=outs, in_specs=in_specs or [pl.BlockSpec...  5.89 us
    ppermute x12, waiting for transfers between devices, exchange(): arrived.append(lax.ppermute(pieces[k], 'dp', way) if k else pieces[k])  4.09 us
    ppermute x3, starting transfers between devices, to_partner(): return lax.ppermute(values, 'seq', [(i, i ^ distance) for i in range(span)])  3.54 us
    ppermute x3, waiting for transfers between devices, to_partner(): return lax.ppermute(values, 'seq', [(i, i ^ distance) for i in range(span)])  1.69 us
  transfers between devices with their start and end apart: 15, of which 7 were waited for; matrix products, arithmetic and copies ran while one was open for 0% of the time, Pallas kernels for 5%

profile of v4, /device:TPU:0, one launch (start us, length us, event | category | flops | bytes accessed | tf_op | source)
XLA Modules:
  0.0 42.7 jit_solution(15720552171507281606)
XLA Ops:
  0.6 1.3 %shard_map.93 = (bf16[96,256]{1,0:T(8,128)(2,1)S(1)}, bf16[96,256]{1,0:T(8,128)(2,1)S(1)}, bf16[96,256]{1,0:T(8,128)(2,1)S(1)}, bf16[96,256]{1,0:T(8,128)(2,1)S(...) custom-call(s32[1,4]{1,0:T(1,128)} %lengths_hbm.1, ...), custom_call_target="tpu_custom_call" | custom-call | tf_op jit(solution)/shard_map/pallas_call | solution.py:333
  2.0 0.0 copy-start
  2.0 4.1 %collective-permute-start = (bf16[96,256]{1,0:T(8,128)(2,1)S(1)}, bf16[96,256]{1,0:T(8,128)(2,1)S(1)}, u32[]{:S(2)}, u32[]{:S(2)}) collective-permute-start(bf16[96,256]{1,0:T(8,128)(2,1)S(1)} %get-tuple-element.36), channel_id=1, source_target_pairs={{0,16},{8,24},{16,0},{24,8},{1,17},{9,25},{17,1},{25,9},{2,18},{10... | collective-permute-start | bytes 147464 | tf_op jit(solution)/shard_map/ppermute | solution.py:388
  6.1 1.3 %collective-permute-start.1 = (bf16[96,256]{1,0:T(8,128)(2,1)S(1)}, bf16[96,256]{1,0:T(8,128)(2,1)S(1)}, u32[]{:S(2)}, u32[]{:S(2)}) collective-permute-start(bf16[96,256]{1,0:T(8,128)(2,1)S(1)} %get-tuple-element.37), channel_id=1, source_target_pairs={{0,24},{8,16},{16,8},{24,0},{1,25},{9,17},{17,9},{25,1},{2,26},{10... | collective-permute-start | bytes 147464 | tf_op jit(solution)/shard_map/ppermute | solution.py:388
  7.4 0.2 collective-permute-start.2
  7.7 0.4 shard_map.96
  8.1 1.9 %collective-permute-start.3 = (bf16[96,512]{1,0:T(8,128)(2,1)S(1)}, bf16[96,512]{1,0:T(8,128)(2,1)S(1)}, u32[]{:S(2)}, u32[]{:S(2)}) collective-permute-start(bf16[96,512]{1,0:T(8,128)(2,1)S(1)} %get-tuple-element.43), channel_id=1, source_target_pairs={{0,8},{8,0},{16,24},{24,16},{1,9},{9,1},{17,25},{25,17},{2,10},{10... | collective-permute-start | bytes 294920 | tf_op jit(solution)/shard_map/ppermute | solution.py:388
  9.9 2.5 %collective-permute-start.4 = (bf16[96,512]{1,0:T(8,128)(2,1)S(1)}, bf16[96,512]{1,0:T(8,128)(2,1)S(1)}, u32[]{:S(2)}, u32[]{:S(2)}) collective-permute-start(bf16[96,512]{1,0:T(8,128)(2,1)S(1)} %get-tuple-element.44), channel_id=1, source_target_pairs={{0,24},{8,16},{16,8},{24,0},{1,25},{9,17},{17,9},{25,1},{2,26},{10... | collective-permute-start | bytes 294920 | tf_op jit(solution)/shard_map/ppermute | solution.py:388
  12.4 0.0 collective-permute-done.1.refs_1_
  12.4 0.2 collective-permute-done.2.refs_2_
  12.6 8.6 %all_gather.3.sequence_ref = bf16[1536,256]{1,0:T(8,128)(2,1)S(1)} all-gather(bf16[384,256]{1,0:T(8,128)(2,1)S(1)} %shard_map.95), channel_id=1, replica_groups=mesh['dp'=4,'seq'=4,'head'=2] {'seq'}, dimensions={0}, use_global_device_ids=true | all-gather | bytes 983040 | tf_op jit(solution)/shard_map/all_gather | solution.py:400
  21.2 1.3 %shard_map.97 = (bf16[768,256]{1,0:T(8,128)(2,1)S(1)}, bf16[768,256]{1,0:T(8,128)(2,1)S(1)}, bf16[1536,768]{1,0:T(8,128)(2,1)S(1)}, bf16[1536,768]{1,0:T(8,128)(2,1)S(1)}) custom-call(bf16[1536,256]{1,0:T(8,128)(2,1)S(1)} %all_gather.3.sequence_ref, s32[1,768]{1,0:T(1,128)S(1)} %get-tuple-element.40.first_ref, ...), custom_call_target="tpu_custom_call" | custom-call | tf_op jit(solution)/shard_map/pallas_call | solution.py:333
  22.5 1.1 %collective-permute-start.9 = (bf16[768,256]{1,0:T(8,128)(2,1)S(1)}, bf16[768,256]{1,0:T(8,128)(2,1)S(1)}, u32[]{:S(2)}, u32[]{:S(2)}) collective-permute-start(bf16[768,256]{1,0:T(8,128)(2,1)S(1)} %get-tuple-element.56), channel_id=1, source_target_pairs={{0,2},{2,0},{4,6},{6,4},{1,3},{3,1},{5,7},{7,5},{8,10},{10,8},{12,... | collective-permute-start | bytes 1179656 | tf_op jit(solution)/shard_map/ppermute | solution.py:392
  23.6 0.5 %shard_map.98 = (bf16[96,512]{1,0:T(8,128)(2,1)S(1)}, bf16[96,512]{1,0:T(8,128)(2,1)S(1)}, bf16[96,512]{1,0:T(8,128)(2,1)S(1)}, bf16[96,512]{1,0:T(8,128)(2,1)S(1)}) custom-call(bf16[1536,256]{1,0:T(8,128)(2,1)S(1)} %all_gather.3.sequence_ref, bf16[1536,768]{1,0:T(8,128)(2,1)S(1)} %get-tuple-element.47.low_ref, bf16[1536,768]{1,0:T(8,128)(2,1)S(1)} %get-tuple-element.48.ds_ref), custom_call_target="tpu_custom_call" | custom-call | tf_op jit(solution)/shard_map/pallas_call | solution.py:333
  24.2 2.8 %collective-permute-start.6 = (bf16[96,512]{1,0:T(8,128)(2,1)S(1)}, bf16[96,512]{1,0:T(8,128)(2,1)S(1)}, u32[]{:S(2)}, u32[]{:S(2)}) collective-permute-start(bf16[96,512]{1,0:T(8,128)(2,1)S(1)} %get-tuple-element.49), channel_id=1, source_target_pairs={{16,0},{24,8},{0,16},{8,24},{17,1},{25,9},{1,17},{9,25},{18,2},{26... | collective-permute-start | bytes 294920 | tf_op jit(solution)/shard_map/ppermute | solution.py:388
  27.0 0.1 shard_map.100
  27.1 2.4 %collective-permute-start.10 = (bf16[192,256]{1,0:T(8,128)(2,1)S(1)}, bf16[192,256]{1,0:T(8,128)(2,1)S(1)}, u32[]{:S(2)}, u32[]{:S(2)}) collective-permute-start(bf16[192,256]{1,0:T(8,128)(2,1)S(1)} %get-tuple-element.58), channel_id=1, source_target_pairs={{0,4},{2,6},{4,0},{6,2},{1,5},{3,7},{5,1},{7,3},{8,12},{10,14},{12... | collective-permute-start | bytes 294920 | tf_op jit(solution)/shard_map/ppermute | solution.py:392
  29.5 0.1 collective-permute-start.11
  29.5 1.8 %collective-permute-start.7 = (bf16[96,512]{1,0:T(8,128)(2,1)S(1)}, bf16[96,512]{1,0:T(8,128)(2,1)S(1)}, u32[]{:S(2)}, u32[]{:S(2)}) collective-permute-start(bf16[96,512]{1,0:T(8,128)(2,1)S(1)} %get-tuple-element.50), channel_id=1, source_target_pairs={{24,0},{16,8},{8,16},{0,24},{25,1},{17,9},{9,17},{1,25},{26,2},{18... | collective-permute-start | bytes 294920 | tf_op jit(solution)/shard_map/ppermute | solution.py:388
  31.3 0.0 collective-permute-start.8
  31.3 1.4 %collective-permute-done.6.refs_0_.refs_2_ = bf16[96,512]{1,0:T(8,128)(2,1)S(1)} collective-permute-done((bf16[96,512]{1,0:T(8,128)(2,1)S(1)}, bf16[96,512]{1,0:T(8,128)(2,1)S(1)}, u32[]{:S(2)}, u32[]{:S(2)}) %collective-permute-start.6) | collective-permute-done | bytes 98336 | tf_op jit(solution)/shard_map/ppermute | solution.py:388
  32.7 0.3 collective-permute-done.10.refs_0_
  33.0 1.4 %collective-permute-done.11.refs_1_ = bf16[192,256]{1,0:T(8,128)(2,1)S(1)} collective-permute-done((bf16[192,256]{1,0:T(8,128)(2,1)S(1)}, bf16[192,256]{1,0:T(8,128)(2,1)S(1)}, u32[]{:S(2)}, u32[]{:S(2)}) %collective-permute-start.11) | collective-permute-done | bytes 98336 | tf_op jit(solution)/shard_map/ppermute | solution.py:392
  34.4 1.0 %collective-permute-start.12 = (bf16[96,256]{1,0:T(8,128)(2,1)S(1)}, bf16[96,256]{1,0:T(8,128)(2,1)S(1)}, u32[]{:S(2)}, u32[]{:S(2)}) collective-permute-start(bf16[96,256]{1,0:T(8,128)(2,1)S(1)} %get-tuple-element.60), channel_id=1, source_target_pairs={{16,0},{24,8},{0,16},{8,24},{17,1},{25,9},{1,17},{9,25},{18,2},{26... | collective-permute-start | bytes 147464 | tf_op jit(solution)/shard_map/ppermute | solution.py:388
  35.4 1.8 %collective-permute-start.13 = (bf16[96,256]{1,0:T(8,128)(2,1)S(1)}, bf16[96,256]{1,0:T(8,128)(2,1)S(1)}, u32[]{:S(2)}, u32[]{:S(2)}) collective-permute-start(bf16[96,256]{1,0:T(8,128)(2,1)S(1)} %get-tuple-element.61), channel_id=1, source_target_pairs={{24,0},{16,8},{8,16},{0,24},{25,1},{17,9},{9,17},{1,25},{26,2},{18... | collective-permute-start | bytes 147464 | tf_op jit(solution)/shard_map/ppermute | solution.py:388
  37.2 0.8 %collective-permute-start.14 = (bf16[96,256]{1,0:T(8,128)(2,1)S(1)}, bf16[96,256]{1,0:T(8,128)(2,1)S(1)}, u32[]{:S(2)}, u32[]{:S(2)}) collective-permute-start(bf16[96,256]{1,0:T(8,128)(2,1)S(1)} %get-tuple-element.62), channel_id=1, source_target_pairs={{8,0},{0,8},{24,16},{16,24},{9,1},{1,9},{25,17},{17,25},{10,2},{2,... | collective-permute-start | bytes 147464 | tf_op jit(solution)/shard_map/ppermute | solution.py:388
  38.0 0.2 shard_map.94.back_ref
  38.2 1.1 %shard_map.99 = (bf16[360,256]{1,0:T(8,128)(2,1)}, bf16[360,256]{1,0:T(8,128)(2,1)}) custom-call(bf16[360,384]{1,0:T(8,128)(2,1)S(1)} %shard_map.94.back_ref, bf16[96,512]{1,0:T(8,128)(2,1)S(1)} %collective-permute-done.6.refs_0_.refs_2_, bf16[96,512]{1,0:T(8,128)(2,1)S(1)} %collective-permute-done.7.refs_1_, ...), custom_call_target="tpu_custom_call" | custom-call | tf_op jit(solution)/shard_map/pallas_call | solution.py:333
  39.3 1.1 %collective-permute-done.12.refs_0_ = bf16[96,256]{1,0:T(8,128)(2,1)S(1)} collective-permute-done((bf16[96,256]{1,0:T(8,128)(2,1)S(1)}, bf16[96,256]{1,0:T(8,128)(2,1)S(1)}, u32[]{:S(2)}, u32[]{:S(2)}) %collective-permute-start.12) | collective-permute-done | bytes 49184 | tf_op jit(solution)/shard_map/ppermute | solution.py:388
  40.4 1.1 %collective-permute-done.13.refs_1_ = bf16[96,256]{1,0:T(8,128)(2,1)S(1)} collective-permute-done((bf16[96,256]{1,0:T(8,128)(2,1)S(1)}, bf16[96,256]{1,0:T(8,128)(2,1)S(1)}, u32[]{:S(2)}, u32[]{:S(2)}) %collective-permute-start.13) | collective-permute-done | bytes 49184 | tf_op jit(solution)/shard_map/ppermute | solution.py:388
  41.5 0.3 collective-permute-done.14.refs_2_
  41.8 0.9 %shard_map.102 = (bf16[360,128]{1,0:T(8,128)(2,1)}, bf16[360,128]{1,0:T(8,128)(2,1)}) custom-call(bf16[360,384]{1,0:T(8,128)(2,1)S(1)} %shard_map.94.back_ref, bf16[96,256]{1,0:T(8,128)(2,1)S(1)} %collective-permute-done.12.refs_0_, bf16[96,256]{1,0:T(8,128)(2,1)S(1)} %collective-permute-done.13.refs_1_, ...), custom_call_target="tpu_custom_call" | custom-call | tf_op jit(solution)/shard_map/pallas_call | solution.py:333
  (13 shorter events, 0.1 us)
Async XLA Ops:
  2.0 6.1 %copy-start = (s32[1,360]{1,0:T(1,128)}, s32[1,360]{1,0:T(1,128)S(1)}, u32[]{:S(2)}) copy-start(s32[1,360]{1,0:T(1,128)S(1)} %get-tuple-element.35.slot_ref) | copy-start | bytes 4324
  2.0 10.4 %collective-permute-start = (bf16[96,256]{1,0:T(8,128)(2,1)S(1)}, bf16[96,256]{1,0:T(8,128)(2,1)S(1)}, u32[]{:S(2)}, u32[]{:S(2)}) collective-permute-start(bf16[96,256]{1,0:T(8,128)(2,1)S(1)} %get-tuple-element.36), channel_id=1, source_target_pairs={{0,16},{8,24},{16,0},{24,8},{1,17},{9,25},{17,1},{25,9},{2,18},{10... | collective-permute-start | bytes 147464 | tf_op jit(solution)/shard_map/ppermute | solution.py:388
  6.1 6.3 %collective-permute-start.1 = (bf16[96,256]{1,0:T(8,128)(2,1)S(1)}, bf16[96,256]{1,0:T(8,128)(2,1)S(1)}, u32[]{:S(2)}, u32[]{:S(2)}) collective-permute-start(bf16[96,256]{1,0:T(8,128)(2,1)S(1)} %get-tuple-element.37), channel_id=1, source_target_pairs={{0,24},{8,16},{16,8},{24,0},{1,25},{9,17},{17,9},{25,1},{2,26},{10... | collective-permute-start | bytes 147464 | tf_op jit(solution)/shard_map/ppermute | solution.py:388
  7.4 5.1 %collective-permute-start.2 = (bf16[96,256]{1,0:T(8,128)(2,1)S(1)}, bf16[96,256]{1,0:T(8,128)(2,1)S(1)}, u32[]{:S(2)}, u32[]{:S(2)}) collective-permute-start(bf16[96,256]{1,0:T(8,128)(2,1)S(1)} %get-tuple-element.38), channel_id=1, source_target_pairs={{0,8},{8,0},{16,24},{24,16},{1,9},{9,1},{17,25},{25,17},{2,10},{10... | collective-permute-start | bytes 147464 | tf_op jit(solution)/shard_map/ppermute | solution.py:388
  8.1 13.2 %collective-permute-start.3 = (bf16[96,512]{1,0:T(8,128)(2,1)S(1)}, bf16[96,512]{1,0:T(8,128)(2,1)S(1)}, u32[]{:S(2)}, u32[]{:S(2)}) collective-permute-start(bf16[96,512]{1,0:T(8,128)(2,1)S(1)} %get-tuple-element.43), channel_id=1, source_target_pairs={{0,8},{8,0},{16,24},{24,16},{1,9},{9,1},{17,25},{25,17},{2,10},{10... | collective-permute-start | bytes 294920 | tf_op jit(solution)/shard_map/ppermute | solution.py:388
  9.9 11.3 %collective-permute-start.4 = (bf16[96,512]{1,0:T(8,128)(2,1)S(1)}, bf16[96,512]{1,0:T(8,128)(2,1)S(1)}, u32[]{:S(2)}, u32[]{:S(2)}) collective-permute-start(bf16[96,512]{1,0:T(8,128)(2,1)S(1)} %get-tuple-element.44), channel_id=1, source_target_pairs={{0,24},{8,16},{16,8},{24,0},{1,25},{9,17},{17,9},{25,1},{2,26},{10... | collective-permute-start | bytes 294920 | tf_op jit(solution)/shard_map/ppermute | solution.py:388
  12.4 8.8 %collective-permute-start.5 = (bf16[96,512]{1,0:T(8,128)(2,1)S(1)}, bf16[96,512]{1,0:T(8,128)(2,1)S(1)}, u32[]{:S(2)}, u32[]{:S(2)}) collective-permute-start(bf16[96,512]{1,0:T(8,128)(2,1)S(1)} %get-tuple-element.45), channel_id=1, source_target_pairs={{0,16},{8,24},{16,0},{24,8},{1,17},{9,25},{17,1},{25,9},{2,18},{10... | collective-permute-start | bytes 294920 | tf_op jit(solution)/shard_map/ppermute | solution.py:388
  22.5 4.5 %collective-permute-start.9 = (bf16[768,256]{1,0:T(8,128)(2,1)S(1)}, bf16[768,256]{1,0:T(8,128)(2,1)S(1)}, u32[]{:S(2)}, u32[]{:S(2)}) collective-permute-start(bf16[768,256]{1,0:T(8,128)(2,1)S(1)} %get-tuple-element.56), channel_id=1, source_target_pairs={{0,2},{2,0},{4,6},{6,4},{1,3},{3,1},{5,7},{7,5},{8,10},{10,8},{12,... | collective-permute-start | bytes 1179656 | tf_op jit(solution)/shard_map/ppermute | solution.py:392
  24.2 8.5 %collective-permute-start.6 = (bf16[96,512]{1,0:T(8,128)(2,1)S(1)}, bf16[96,512]{1,0:T(8,128)(2,1)S(1)}, u32[]{:S(2)}, u32[]{:S(2)}) collective-permute-start(bf16[96,512]{1,0:T(8,128)(2,1)S(1)} %get-tuple-element.49), channel_id=1, source_target_pairs={{16,0},{24,8},{0,16},{8,24},{17,1},{25,9},{1,17},{9,25},{18,2},{26... | collective-permute-start | bytes 294920 | tf_op jit(solution)/shard_map/ppermute | solution.py:388
  27.1 5.9 %collective-permute-start.10 = (bf16[192,256]{1,0:T(8,128)(2,1)S(1)}, bf16[192,256]{1,0:T(8,128)(2,1)S(1)}, u32[]{:S(2)}, u32[]{:S(2)}) collective-permute-start(bf16[192,256]{1,0:T(8,128)(2,1)S(1)} %get-tuple-element.58), channel_id=1, source_target_pairs={{0,4},{2,6},{4,0},{6,2},{1,5},{3,7},{5,1},{7,3},{8,12},{10,14},{12... | collective-permute-start | bytes 294920 | tf_op jit(solution)/shard_map/ppermute | solution.py:392
  29.5 4.9 %collective-permute-start.11 = (bf16[192,256]{1,0:T(8,128)(2,1)S(1)}, bf16[192,256]{1,0:T(8,128)(2,1)S(1)}, u32[]{:S(2)}, u32[]{:S(2)}) collective-permute-start(bf16[192,256]{1,0:T(8,128)(2,1)S(1)} %get-tuple-element.59), channel_id=1, source_target_pairs={{0,4},{2,6},{4,0},{6,2},{1,5},{3,7},{5,1},{7,3},{8,12},{10,14},{12... | collective-permute-start | bytes 294920 | tf_op jit(solution)/shard_map/ppermute | solution.py:392
  29.5 8.6 %collective-permute-start.7 = (bf16[96,512]{1,0:T(8,128)(2,1)S(1)}, bf16[96,512]{1,0:T(8,128)(2,1)S(1)}, u32[]{:S(2)}, u32[]{:S(2)}) collective-permute-start(bf16[96,512]{1,0:T(8,128)(2,1)S(1)} %get-tuple-element.50), channel_id=1, source_target_pairs={{24,0},{16,8},{8,16},{0,24},{25,1},{17,9},{9,17},{1,25},{26,2},{18... | collective-permute-start | bytes 294920 | tf_op jit(solution)/shard_map/ppermute | solution.py:388
  31.3 6.9 %collective-permute-start.8 = (bf16[96,512]{1,0:T(8,128)(2,1)S(1)}, bf16[96,512]{1,0:T(8,128)(2,1)S(1)}, u32[]{:S(2)}, u32[]{:S(2)}) collective-permute-start(bf16[96,512]{1,0:T(8,128)(2,1)S(1)} %get-tuple-element.51), channel_id=1, source_target_pairs={{8,0},{0,8},{24,16},{16,24},{9,1},{1,9},{25,17},{17,25},{10,2},{2,... | collective-permute-start | bytes 294920 | tf_op jit(solution)/shard_map/ppermute | solution.py:388
  34.4 3.6 %copy-start.1 = (s32[1,360]{1,0:T(1,128)S(1)}, s32[1,360]{1,0:T(1,128)}, u32[]{:S(2)}) copy-start(s32[1,360]{1,0:T(1,128)} %copy-done) | copy-start | bytes 4324
  34.4 6.0 %collective-permute-start.12 = (bf16[96,256]{1,0:T(8,128)(2,1)S(1)}, bf16[96,256]{1,0:T(8,128)(2,1)S(1)}, u32[]{:S(2)}, u32[]{:S(2)}) collective-permute-start(bf16[96,256]{1,0:T(8,128)(2,1)S(1)} %get-tuple-element.60), channel_id=1, source_target_pairs={{16,0},{24,8},{0,16},{8,24},{17,1},{25,9},{1,17},{9,25},{18,2},{26... | collective-permute-start | bytes 147464 | tf_op jit(solution)/shard_map/ppermute | solution.py:388
  35.4 6.0 %collective-permute-start.13 = (bf16[96,256]{1,0:T(8,128)(2,1)S(1)}, bf16[96,256]{1,0:T(8,128)(2,1)S(1)}, u32[]{:S(2)}, u32[]{:S(2)}) collective-permute-start(bf16[96,256]{1,0:T(8,128)(2,1)S(1)} %get-tuple-element.61), channel_id=1, source_target_pairs={{24,0},{16,8},{8,16},{0,24},{25,1},{17,9},{9,17},{1,25},{26,2},{18... | collective-permute-start | bytes 147464 | tf_op jit(solution)/shard_map/ppermute | solution.py:388
  37.2 4.6 %collective-permute-start.14 = (bf16[96,256]{1,0:T(8,128)(2,1)S(1)}, bf16[96,256]{1,0:T(8,128)(2,1)S(1)}, u32[]{:S(2)}, u32[]{:S(2)}) collective-permute-start(bf16[96,256]{1,0:T(8,128)(2,1)S(1)} %get-tuple-element.62), channel_id=1, source_target_pairs={{8,0},{0,8},{24,16},{16,24},{9,1},{1,9},{25,17},{17,25},{10,2},{2,... | collective-permute-start | bytes 147464 | tf_op jit(solution)/shard_map/ppermute | solution.py:388

commit v5 on v4

--- a/solution.py
+++ b/solution.py
@@ -37,6 +37,10 @@
 
 def travel_order(peers):
     return list(range(2, peers)) + [1, 0]
+
+
+def far_first(peers):
+    return list(range(peers))[::-1]
 
 
 def step_to(me, other, peers):
@@ -298,7 +302,7 @@
     whole = refs[-1]
     pad = refs[0].shape[0]
     me = lax.axis_index("dp")
-    for step, ref in zip(travel_order(peers), refs):
+    for step, ref in zip(far_first(peers), refs):
         whole[pl.ds(pl.multiple_of(step_to(step, me, peers) * pad, pad), pad), :] = ref[...]
 
 
@@ -394,7 +398,7 @@
     def join(pieces):
         return call(functools.partial(join_kernel, peers), shape((rows, 2 * HEAD_DIM), BF16), *pieces, cost=brief)
 
-    kv = exchange(kv)
+    kv = exchange(kv, order=far_first(peers))
     near_first = [1, *range(peers - 1, 1, -1), 0]
     qg = exchange(qg, order=near_first)
     sequence = lax.all_gather(join(kv), "seq", axis=0, tiled=True)

time: 42.9 us -> 42.7 us (level)
  transfers between devices with their start and end apart: 15 -> 15, of which waited for: 7 -> 6; matrix products, arithmetic and copies ran while one was open for 0% -> 0% of each run, Pallas kernels for 5% -> 5%
where the time goes in v5:
time: 42.7 us; the launch traced here: 42.5 us
  starting transfers between devices  21.3 us (50%)
  blocking collectives  8.6 us (20%)
  waiting for transfers between devices  6.01 us (14%)
  Pallas kernels  5.89 us (14%)
  between operations  0.74 us (2%)
    ppermute x12, starting transfers between devices, exchange(): arrived.append(lax.ppermute(pieces[k], 'dp', way) if k else pieces[k])  17.7 us
    all_gather x1, blocking collectives, local(): sequence = lax.all_gather(join(kv), 'seq', axis=0, tiled=True)  8.6 us
    pallas_call x10, Pallas kernels, call(): pl.pallas_call(kernel, out_shape=outs, in_specs=in_specs or [pl.BlockSpec...  5.89 us
    ppermute x12, waiting for transfers between devices, exchange(): arrived.append(lax.ppermute(pieces[k], 'dp', way) if k else pieces[k])  4.22 us
    ppermute x3, starting transfers between devices, to_partner(): return lax.ppermute(values, 'seq', [(i, i ^ distance) for i in range(span)])  3.56 us
    ppermute x3, waiting for transfers between devices, to_partner(): return lax.ppermute(values, 'seq', [(i, i ^ distance) for i in range(span)])  1.79 us
  transfers between devices with their start and end apart: 15, of which 6 were waited for; matrix products, arithmetic and copies ran while one was open for 0% of the time, Pallas kernels for 5%

profile of v5, /device:TPU:0, one launch (start us, length us, event | category | flops | bytes accessed | tf_op | source)
XLA Modules:
  0.0 42.5 jit_solution(120550465239863820)
XLA Ops:
  0.6 1.3 %shard_map.93 = (bf16[96,256]{1,0:T(8,128)(2,1)S(1)}, bf16[96,256]{1,0:T(8,128)(2,1)S(1)}, bf16[96,256]{1,0:T(8,128)(2,1)S(1)}, bf16[96,256]{1,0:T(8,128)(2,1)S(...) custom-call(s32[1,4]{1,0:T(1,128)} %lengths_hbm.1, ...), custom_call_target="tpu_custom_call" | custom-call | tf_op jit(solution)/shard_map/pallas_call | solution.py:337
  2.0 0.0 copy-start
  2.0 5.1 %collective-permute-start = (bf16[96,256]{1,0:T(8,128)(2,1)S(1)}, bf16[96,256]{1,0:T(8,128)(2,1)S(1)}, u32[]{:S(2)}, u32[]{:S(2)}) collective-permute-start(bf16[96,256]{1,0:T(8,128)(2,1)S(1)} %get-tuple-element.36), channel_id=1, source_target_pairs={{0,24},{8,16},{16,8},{24,0},{1,25},{9,17},{17,9},{25,1},{2,26},{10... | collective-permute-start | bytes 147464 | tf_op jit(solution)/shard_map/ppermute | solution.py:392
  7.1 0.0 collective-permute-start.1
  7.1 0.6 %collective-permute-start.2 = (bf16[96,256]{1,0:T(8,128)(2,1)S(1)}, bf16[96,256]{1,0:T(8,128)(2,1)S(1)}, u32[]{:S(2)}, u32[]{:S(2)}) collective-permute-start(bf16[96,256]{1,0:T(8,128)(2,1)S(1)} %get-tuple-element.38), channel_id=1, source_target_pairs={{0,8},{8,0},{16,24},{24,16},{1,9},{9,1},{17,25},{25,17},{2,10},{10... | collective-permute-start | bytes 147464 | tf_op jit(solution)/shard_map/ppermute | solution.py:392
  7.7 0.4 shard_map.96
  8.1 1.5 %collective-permute-start.3 = (bf16[96,512]{1,0:T(8,128)(2,1)S(1)}, bf16[96,512]{1,0:T(8,128)(2,1)S(1)}, u32[]{:S(2)}, u32[]{:S(2)}) collective-permute-start(bf16[96,512]{1,0:T(8,128)(2,1)S(1)} %get-tuple-element.43), channel_id=1, source_target_pairs={{0,8},{8,0},{16,24},{24,16},{1,9},{9,1},{17,25},{25,17},{2,10},{10... | collective-permute-start | bytes 294920 | tf_op jit(solution)/shard_map/ppermute | solution.py:392
  9.6 2.4 %collective-permute-start.4 = (bf16[96,512]{1,0:T(8,128)(2,1)S(1)}, bf16[96,512]{1,0:T(8,128)(2,1)S(1)}, u32[]{:S(2)}, u32[]{:S(2)}) collective-permute-start(bf16[96,512]{1,0:T(8,128)(2,1)S(1)} %get-tuple-element.44), channel_id=1, source_target_pairs={{0,24},{8,16},{16,8},{24,0},{1,25},{9,17},{17,9},{25,1},{2,26},{10... | collective-permute-start | bytes 294920 | tf_op jit(solution)/shard_map/ppermute | solution.py:392
  12.0 0.0 collective-permute-done.refs_0_
  12.0 0.5 %collective-permute-start.5 = (bf16[96,512]{1,0:T(8,128)(2,1)S(1)}, bf16[96,512]{1,0:T(8,128)(2,1)S(1)}, u32[]{:S(2)}, u32[]{:S(2)}) collective-permute-start(bf16[96,512]{1,0:T(8,128)(2,1)S(1)} %get-tuple-element.45), channel_id=1, source_target_pairs={{0,16},{8,24},{16,0},{24,8},{1,17},{9,25},{17,1},{25,9},{2,18},{10... | collective-permute-start | bytes 294920 | tf_op jit(solution)/shard_map/ppermute | solution.py:392
  12.5 8.6 %all_gather.3.sequence_ref = bf16[1536,256]{1,0:T(8,128)(2,1)S(1)} all-gather(bf16[384,256]{1,0:T(8,128)(2,1)S(1)} %shard_map.95), channel_id=1, replica_groups=mesh['dp'=4,'seq'=4,'head'=2] {'seq'}, dimensions={0}, use_global_device_ids=true | all-gather | bytes 983040 | tf_op jit(solution)/shard_map/all_gather | solution.py:404
  21.1 0.0 collective-permute-done.3.refs_0_
  21.2 1.3 %shard_map.97 = (bf16[768,256]{1,0:T(8,128)(2,1)S(1)}, bf16[768,256]{1,0:T(8,128)(2,1)S(1)}, bf16[1536,768]{1,0:T(8,128)(2,1)S(1)}, bf16[1536,768]{1,0:T(8,128)(2,1)S(1)}) custom-call(bf16[1536,256]{1,0:T(8,128)(2,1)S(1)} %all_gather.3.sequence_ref, s32[1,768]{1,0:T(1,128)S(1)} %get-tuple-element.40.first_ref, ...), custom_call_target="tpu_custom_call" | custom-call | tf_op jit(solution)/shard_map/pallas_call | solution.py:337
  22.5 1.1 %collective-permute-start.9 = (bf16[768,256]{1,0:T(8,128)(2,1)S(1)}, bf16[768,256]{1,0:T(8,128)(2,1)S(1)}, u32[]{:S(2)}, u32[]{:S(2)}) collective-permute-start(bf16[768,256]{1,0:T(8,128)(2,1)S(1)} %get-tuple-element.56), channel_id=1, source_target_pairs={{0,2},{2,0},{4,6},{6,4},{1,3},{3,1},{5,7},{7,5},{8,10},{10,8},{12,... | collective-permute-start | bytes 1179656 | tf_op jit(solution)/shard_map/ppermute | solution.py:396
  23.5 0.5 %shard_map.98 = (bf16[96,512]{1,0:T(8,128)(2,1)S(1)}, bf16[96,512]{1,0:T(8,128)(2,1)S(1)}, bf16[96,512]{1,0:T(8,128)(2,1)S(1)}, bf16[96,512]{1,0:T(8,128)(2,1)S(1)}) custom-call(bf16[1536,256]{1,0:T(8,128)(2,1)S(1)} %all_gather.3.sequence_ref, bf16[1536,768]{1,0:T(8,128)(2,1)S(1)} %get-tuple-element.47.low_ref, bf16[1536,768]{1,0:T(8,128)(2,1)S(1)} %get-tuple-element.48.ds_ref), custom_call_target="tpu_custom_call" | custom-call | tf_op jit(solution)/shard_map/pallas_call | solution.py:337
  24.1 2.5 %collective-permute-start.6 = (bf16[96,512]{1,0:T(8,128)(2,1)S(1)}, bf16[96,512]{1,0:T(8,128)(2,1)S(1)}, u32[]{:S(2)}, u32[]{:S(2)}) collective-permute-start(bf16[96,512]{1,0:T(8,128)(2,1)S(1)} %get-tuple-element.49), channel_id=1, source_target_pairs={{16,0},{24,8},{0,16},{8,24},{17,1},{25,9},{1,17},{9,25},{18,2},{26... | collective-permute-start | bytes 294920 | tf_op jit(solution)/shard_map/ppermute | solution.py:392
  26.6 0.1 shard_map.100
  26.7 2.4 %collective-permute-start.10 = (bf16[192,256]{1,0:T(8,128)(2,1)S(1)}, bf16[192,256]{1,0:T(8,128)(2,1)S(1)}, u32[]{:S(2)}, u32[]{:S(2)}) collective-permute-start(bf16[192,256]{1,0:T(8,128)(2,1)S(1)} %get-tuple-element.58), channel_id=1, source_target_pairs={{0,4},{2,6},{4,0},{6,2},{1,5},{3,7},{5,1},{7,3},{8,12},{10,14},{12... | collective-permute-start | bytes 294920 | tf_op jit(solution)/shard_map/ppermute | solution.py:396
  29.1 0.1 collective-permute-start.11
  29.2 1.6 %collective-permute-start.7 = (bf16[96,512]{1,0:T(8,128)(2,1)S(1)}, bf16[96,512]{1,0:T(8,128)(2,1)S(1)}, u32[]{:S(2)}, u32[]{:S(2)}) collective-permute-start(bf16[96,512]{1,0:T(8,128)(2,1)S(1)} %get-tuple-element.50), channel_id=1, source_target_pairs={{24,0},{16,8},{8,16},{0,24},{25,1},{17,9},{9,17},{1,25},{26,2},{18... | collective-permute-start | bytes 294920 | tf_op jit(solution)/shard_map/ppermute | solution.py:392
  30.7 1.5 %collective-permute-done.6.refs_0_.refs_2_ = bf16[96,512]{1,0:T(8,128)(2,1)S(1)} collective-permute-done((bf16[96,512]{1,0:T(8,128)(2,1)S(1)}, bf16[96,512]{1,0:T(8,128)(2,1)S(1)}, u32[]{:S(2)}, u32[]{:S(2)}) %collective-permute-start.6) | collective-permute-done | bytes 98336 | tf_op jit(solution)/shard_map/ppermute | solution.py:392
  32.2 0.4 collective-permute-done.10.refs_0_
  32.6 1.4 %collective-permute-done.11.refs_1_ = bf16[192,256]{1,0:T(8,128)(2,1)S(1)} collective-permute-done((bf16[192,256]{1,0:T(8,128)(2,1)S(1)}, bf16[192,256]{1,0:T(8,128)(2,1)S(1)}, u32[]{:S(2)}, u32[]{:S(2)}) %collective-permute-start.11) | collective-permute-done | bytes 98336 | tf_op jit(solution)/shard_map/ppermute | solution.py:396
  34.0 1.0 %collective-permute-start.12 = (bf16[96,256]{1,0:T(8,128)(2,1)S(1)}, bf16[96,256]{1,0:T(8,128)(2,1)S(1)}, u32[]{:S(2)}, u32[]{:S(2)}) collective-permute-start(bf16[96,256]{1,0:T(8,128)(2,1)S(1)} %get-tuple-element.60), channel_id=1, source_target_pairs={{16,0},{24,8},{0,16},{8,24},{17,1},{25,9},{1,17},{9,25},{18,2},{26... | collective-permute-start | bytes 147464 | tf_op jit(solution)/shard_map/ppermute | solution.py:392
  35.0 2.5 %collective-permute-start.13 = (bf16[96,256]{1,0:T(8,128)(2,1)S(1)}, bf16[96,256]{1,0:T(8,128)(2,1)S(1)}, u32[]{:S(2)}, u32[]{:S(2)}) collective-permute-start(bf16[96,256]{1,0:T(8,128)(2,1)S(1)} %get-tuple-element.61), channel_id=1, source_target_pairs={{24,0},{16,8},{8,16},{0,24},{25,1},{17,9},{9,17},{1,25},{26,2},{18... | collective-permute-start | bytes 147464 | tf_op jit(solution)/shard_map/ppermute | solution.py:392
  37.5 0.1 collective-permute-start.14
  37.6 0.2 shard_map.94.back_ref
  37.8 1.1 %shard_map.99 = (bf16[360,256]{1,0:T(8,128)(2,1)}, bf16[360,256]{1,0:T(8,128)(2,1)}) custom-call(bf16[360,384]{1,0:T(8,128)(2,1)S(1)} %shard_map.94.back_ref, bf16[96,512]{1,0:T(8,128)(2,1)S(1)} %collective-permute-done.6.refs_0_.refs_2_, bf16[96,512]{1,0:T(8,128)(2,1)S(1)} %collective-permute-done.7.refs_1_, ...), custom_call_target="tpu_custom_call" | custom-call | tf_op jit(solution)/shard_map/pallas_call | solution.py:337
  38.9 1.3 %collective-permute-done.12.refs_0_ = bf16[96,256]{1,0:T(8,128)(2,1)S(1)} collective-permute-done((bf16[96,256]{1,0:T(8,128)(2,1)S(1)}, bf16[96,256]{1,0:T(8,128)(2,1)S(1)}, u32[]{:S(2)}, u32[]{:S(2)}) %collective-permute-start.12) | collective-permute-done | bytes 49184 | tf_op jit(solution)/shard_map/ppermute | solution.py:392
  40.2 0.9 %collective-permute-done.13.refs_1_ = bf16[96,256]{1,0:T(8,128)(2,1)S(1)} collective-permute-done((bf16[96,256]{1,0:T(8,128)(2,1)S(1)}, bf16[96,256]{1,0:T(8,128)(2,1)S(1)}, u32[]{:S(2)}, u32[]{:S(2)}) %collective-permute-start.13) | collective-permute-done | bytes 49184 | tf_op jit(solution)/shard_map/ppermute | solution.py:392
  41.0 0.6 %collective-permute-done.14.refs_2_ = bf16[96,256]{1,0:T(8,128)(2,1)S(1)} collective-permute-done((bf16[96,256]{1,0:T(8,128)(2,1)S(1)}, bf16[96,256]{1,0:T(8,128)(2,1)S(1)}, u32[]{:S(2)}, u32[]{:S(2)}) %collective-permute-start.14) | collective-permute-done | bytes 49184 | tf_op jit(solution)/shard_map/ppermute | solution.py:392
  41.6 0.9 %shard_map.102 = (bf16[360,128]{1,0:T(8,128)(2,1)}, bf16[360,128]{1,0:T(8,128)(2,1)}) custom-call(bf16[360,384]{1,0:T(8,128)(2,1)S(1)} %shard_map.94.back_ref, bf16[96,256]{1,0:T(8,128)(2,1)S(1)} %collective-permute-done.12.refs_0_, bf16[96,256]{1,0:T(8,128)(2,1)S(1)} %collective-permute-done.13.refs_1_, ...), custom_call_target="tpu_custom_call" | custom-call | tf_op jit(solution)/shard_map/pallas_call | solution.py:337
  (13 shorter events, 0.1 us)
Async XLA Ops:
  2.0 6.1 %copy-start = (s32[1,360]{1,0:T(1,128)}, s32[1,360]{1,0:T(1,128)S(1)}, u32[]{:S(2)}) copy-start(s32[1,360]{1,0:T(1,128)S(1)} %get-tuple-element.35.slot_ref) | copy-start | bytes 4324
  2.0 10.0 %collective-permute-start = (bf16[96,256]{1,0:T(8,128)(2,1)S(1)}, bf16[96,256]{1,0:T(8,128)(2,1)S(1)}, u32[]{:S(2)}, u32[]{:S(2)}) collective-permute-start(bf16[96,256]{1,0:T(8,128)(2,1)S(1)} %get-tuple-element.36), channel_id=1, source_target_pairs={{0,24},{8,16},{16,8},{24,0},{1,25},{9,17},{17,9},{25,1},{2,26},{10... | collective-permute-start | bytes 147464 | tf_op jit(solution)/shard_map/ppermute | solution.py:392
  7.1 5.4 %collective-permute-start.1 = (bf16[96,256]{1,0:T(8,128)(2,1)S(1)}, bf16[96,256]{1,0:T(8,128)(2,1)S(1)}, u32[]{:S(2)}, u32[]{:S(2)}) collective-permute-start(bf16[96,256]{1,0:T(8,128)(2,1)S(1)} %get-tuple-element.37), channel_id=1, source_target_pairs={{0,16},{8,24},{16,0},{24,8},{1,17},{9,25},{17,1},{25,9},{2,18},{10... | collective-permute-start | bytes 147464 | tf_op jit(solution)/shard_map/ppermute | solution.py:392
  7.1 5.4 %collective-permute-start.2 = (bf16[96,256]{1,0:T(8,128)(2,1)S(1)}, bf16[96,256]{1,0:T(8,128)(2,1)S(1)}, u32[]{:S(2)}, u32[]{:S(2)}) collective-permute-start(bf16[96,256]{1,0:T(8,128)(2,1)S(1)} %get-tuple-element.38), channel_id=1, source_target_pairs={{0,8},{8,0},{16,24},{24,16},{1,9},{9,1},{17,25},{25,17},{2,10},{10... | collective-permute-start | bytes 147464 | tf_op jit(solution)/shard_map/ppermute | solution.py:392
  8.1 13.0 %collective-permute-start.3 = (bf16[96,512]{1,0:T(8,128)(2,1)S(1)}, bf16[96,512]{1,0:T(8,128)(2,1)S(1)}, u32[]{:S(2)}, u32[]{:S(2)}) collective-permute-start(bf16[96,512]{1,0:T(8,128)(2,1)S(1)} %get-tuple-element.43), channel_id=1, source_target_pairs={{0,8},{8,0},{16,24},{24,16},{1,9},{9,1},{17,25},{25,17},{2,10},{10... | collective-permute-start | bytes 294920 | tf_op jit(solution)/shard_map/ppermute | solution.py:392
  9.6 11.6 %collective-permute-start.4 = (bf16[96,512]{1,0:T(8,128)(2,1)S(1)}, bf16[96,512]{1,0:T(8,128)(2,1)S(1)}, u32[]{:S(2)}, u32[]{:S(2)}) collective-permute-start(bf16[96,512]{1,0:T(8,128)(2,1)S(1)} %get-tuple-element.44), channel_id=1, source_target_pairs={{0,24},{8,16},{16,8},{24,0},{1,25},{9,17},{17,9},{25,1},{2,26},{10... | collective-permute-start | bytes 294920 | tf_op jit(solution)/shard_map/ppermute | solution.py:392
  12.0 9.1 %collective-permute-start.5 = (bf16[96,512]{1,0:T(8,128)(2,1)S(1)}, bf16[96,512]{1,0:T(8,128)(2,1)S(1)}, u32[]{:S(2)}, u32[]{:S(2)}) collective-permute-start(bf16[96,512]{1,0:T(8,128)(2,1)S(1)} %get-tuple-element.45), channel_id=1, source_target_pairs={{0,16},{8,24},{16,0},{24,8},{1,17},{9,25},{17,1},{25,9},{2,18},{10... | collective-permute-start | bytes 294920 | tf_op jit(solution)/shard_map/ppermute | solution.py:392
  22.5 4.1 %collective-permute-start.9 = (bf16[768,256]{1,0:T(8,128)(2,1)S(1)}, bf16[768,256]{1,0:T(8,128)(2,1)S(1)}, u32[]{:S(2)}, u32[]{:S(2)}) collective-permute-start(bf16[768,256]{1,0:T(8,128)(2,1)S(1)} %get-tuple-element.56), channel_id=1, source_target_pairs={{0,2},{2,0},{4,6},{6,4},{1,3},{3,1},{5,7},{7,5},{8,10},{10,8},{12,... | collective-permute-start | bytes 1179656 | tf_op jit(solution)/shard_map/ppermute | solution.py:396
  24.1 8.1 %collective-permute-start.6 = (bf16[96,512]{1,0:T(8,128)(2,1)S(1)}, bf16[96,512]{1,0:T(8,128)(2,1)S(1)}, u32[]{:S(2)}, u32[]{:S(2)}) collective-permute-start(bf16[96,512]{1,0:T(8,128)(2,1)S(1)} %get-tuple-element.49), channel_id=1, source_target_pairs={{16,0},{24,8},{0,16},{8,24},{17,1},{25,9},{1,17},{9,25},{18,2},{26... | collective-permute-start | bytes 294920 | tf_op jit(solution)/shard_map/ppermute | solution.py:392
  26.7 5.9 %collective-permute-start.10 = (bf16[192,256]{1,0:T(8,128)(2,1)S(1)}, bf16[192,256]{1,0:T(8,128)(2,1)S(1)}, u32[]{:S(2)}, u32[]{:S(2)}) collective-permute-start(bf16[192,256]{1,0:T(8,128)(2,1)S(1)} %get-tuple-element.58), channel_id=1, source_target_pairs={{0,4},{2,6},{4,0},{6,2},{1,5},{3,7},{5,1},{7,3},{8,12},{10,14},{12... | collective-permute-start | bytes 294920 | tf_op jit(solution)/shard_map/ppermute | solution.py:396
  29.1 4.9 %collective-permute-start.11 = (bf16[192,256]{1,0:T(8,128)(2,1)S(1)}, bf16[192,256]{1,0:T(8,128)(2,1)S(1)}, u32[]{:S(2)}, u32[]{:S(2)}) collective-permute-start(bf16[192,256]{1,0:T(8,128)(2,1)S(1)} %get-tuple-element.59), channel_id=1, source_target_pairs={{0,4},{2,6},{4,0},{6,2},{1,5},{3,7},{5,1},{7,3},{8,12},{10,14},{12... | collective-permute-start | bytes 294920 | tf_op jit(solution)/shard_map/ppermute | solution.py:396
  29.2 8.6 %collective-permute-start.7 = (bf16[96,512]{1,0:T(8,128)(2,1)S(1)}, bf16[96,512]{1,0:T(8,128)(2,1)S(1)}, u32[]{:S(2)}, u32[]{:S(2)}) collective-permute-start(bf16[96,512]{1,0:T(8,128)(2,1)S(1)} %get-tuple-element.50), channel_id=1, source_target_pairs={{24,0},{16,8},{8,16},{0,24},{25,1},{17,9},{9,17},{1,25},{26,2},{18... | collective-permute-start | bytes 294920 | tf_op jit(solution)/shard_map/ppermute | solution.py:392
  30.7 7.1 %collective-permute-start.8 = (bf16[96,512]{1,0:T(8,128)(2,1)S(1)}, bf16[96,512]{1,0:T(8,128)(2,1)S(1)}, u32[]{:S(2)}, u32[]{:S(2)}) collective-permute-start(bf16[96,512]{1,0:T(8,128)(2,1)S(1)} %get-tuple-element.51), channel_id=1, source_target_pairs={{8,0},{0,8},{24,16},{16,24},{9,1},{1,9},{25,17},{17,25},{10,2},{2,... | collective-permute-start | bytes 294920 | tf_op jit(solution)/shard_map/ppermute | solution.py:392
  34.0 3.6 %copy-start.1 = (s32[1,360]{1,0:T(1,128)S(1)}, s32[1,360]{1,0:T(1,128)}, u32[]{:S(2)}) copy-start(s32[1,360]{1,0:T(1,128)} %copy-done) | copy-start | bytes 4324
  34.0 6.1 %collective-permute-start.12 = (bf16[96,256]{1,0:T(8,128)(2,1)S(1)}, bf16[96,256]{1,0:T(8,128)(2,1)S(1)}, u32[]{:S(2)}, u32[]{:S(2)}) collective-permute-start(bf16[96,256]{1,0:T(8,128)(2,1)S(1)} %get-tuple-element.60), channel_id=1, source_target_pairs={{16,0},{24,8},{0,16},{8,24},{17,1},{25,9},{1,17},{9,25},{18,2},{26... | collective-permute-start | bytes 147464 | tf_op jit(solution)/shard_map/ppermute | solution.py:392
  35.0 6.0 %collective-permute-start.13 = (bf16[96,256]{1,0:T(8,128)(2,1)S(1)}, bf16[96,256]{1,0:T(8,128)(2,1)S(1)}, u32[]{:S(2)}, u32[]{:S(2)}) collective-permute-start(bf16[96,256]{1,0:T(8,128)(2,1)S(1)} %get-tuple-element.61), channel_id=1, source_target_pairs={{24,0},{16,8},{8,16},{0,24},{25,1},{17,9},{9,17},{1,25},{26,2},{18... | collective-permute-start | bytes 147464 | tf_op jit(solution)/shard_map/ppermute | solution.py:392
  37.5 4.1 %collective-permute-start.14 = (bf16[96,256]{1,0:T(8,128)(2,1)S(1)}, bf16[96,256]{1,0:T(8,128)(2,1)S(1)}, u32[]{:S(2)}, u32[]{:S(2)}) collective-permute-start(bf16[96,256]{1,0:T(8,128)(2,1)S(1)} %get-tuple-element.62), channel_id=1, source_target_pairs={{8,0},{0,8},{24,16},{16,24},{9,1},{1,9},{25,17},{17,25},{10,2},{2,... | collective-permute-start | bytes 147464 | tf_op jit(solution)/shard_map/ppermute | solution.py:392

commit v6 on v5

--- a/solution.py
+++ b/solution.py
@@ -188,8 +188,8 @@
 
         def tiles(window):
             for c, at, inside in strips(window):
-                for i in range(0, at.stop - at.start, 64):
-                    yield c, slice(at.start + i, at.start + i + 64), slice(inside.start + i, inside.start + i + 64)
+                for i in range(0, at.stop - at.start, 128):
+                    yield c, slice(at.start + i, at.start + i + 128), slice(inside.start + i, inside.start + i + 128)
 
         def fold(x):
             return x.reshape(-1, 8, x.shape[1])

time: 42.7 us -> 42.7 us (level)
  no operation moved by 1% of the time
where the time goes in v6:
time: 42.7 us; the launch traced here: 42.5 us
  starting transfers between devices  21.3 us (50%)
  blocking collectives  8.6 us (20%)
  waiting for transfers between devices  6 us (14%)
  Pallas kernels  5.89 us (14%)
  between operations  0.74 us (2%)
    ppermute x12, starting transfers between devices, exchange(): arrived.append(lax.ppermute(pieces[k], 'dp', way) if k else pieces[k])  17.8 us
    all_gather x1, blocking collectives, local(): sequence = lax.all_gather(join(kv), 'seq', axis=0, tiled=True)  8.6 us
    pallas_call x10, Pallas kernels, call(): pl.pallas_call(kernel, out_shape=outs, in_specs=in_specs or [pl.BlockSpec...  5.89 us
    ppermute x12, waiting for transfers between devices, exchange(): arrived.append(lax.ppermute(pieces[k], 'dp', way) if k else pieces[k])  4.26 us
    ppermute x3, starting transfers between devices, to_partner(): return lax.ppermute(values, 'seq', [(i, i ^ distance) for i in range(span)])  3.56 us
    ppermute x3, waiting for transfers between devices, to_partner(): return lax.ppermute(values, 'seq', [(i, i ^ distance) for i in range(span)])  1.74 us
  transfers between devices with their start and end apart: 15, of which 6 were waited for; matrix products, arithmetic and copies ran while one was open for 0% of the time, Pallas kernels for 5%

profile of v6, /device:TPU:0, one launch (start us, length us, event | category | flops | bytes accessed | tf_op | source)
XLA Modules:
  0.0 42.5 jit_solution(7670586257381447383)
XLA Ops:
  0.6 1.3 %shard_map.93 = (bf16[96,256]{1,0:T(8,128)(2,1)S(1)}, bf16[96,256]{1,0:T(8,128)(2,1)S(1)}, bf16[96,256]{1,0:T(8,128)(2,1)S(1)}, bf16[96,256]{1,0:T(8,128)(2,1)S(...) custom-call(s32[1,4]{1,0:T(1,128)} %lengths_hbm.1, ...), custom_call_target="tpu_custom_call" | custom-call | tf_op jit(solution)/shard_map/pallas_call | solution.py:337
  2.0 0.0 copy-start
  2.0 5.1 %collective-permute-start = (bf16[96,256]{1,0:T(8,128)(2,1)S(1)}, bf16[96,256]{1,0:T(8,128)(2,1)S(1)}, u32[]{:S(2)}, u32[]{:S(2)}) collective-permute-start(bf16[96,256]{1,0:T(8,128)(2,1)S(1)} %get-tuple-element.36), channel_id=1, source_target_pairs={{0,24},{8,16},{16,8},{24,0},{1,25},{9,17},{17,9},{25,1},{2,26},{10... | collective-permute-start | bytes 147464 | tf_op jit(solution)/shard_map/ppermute | solution.py:392
  7.1 0.0 collective-permute-start.1
  7.1 0.6 %collective-permute-start.2 = (bf16[96,256]{1,0:T(8,128)(2,1)S(1)}, bf16[96,256]{1,0:T(8,128)(2,1)S(1)}, u32[]{:S(2)}, u32[]{:S(2)}) collective-permute-start(bf16[96,256]{1,0:T(8,128)(2,1)S(1)} %get-tuple-element.38), channel_id=1, source_target_pairs={{0,8},{8,0},{16,24},{24,16},{1,9},{9,1},{17,25},{25,17},{2,10},{10... | collective-permute-start | bytes 147464 | tf_op jit(solution)/shard_map/ppermute | solution.py:392
  7.7 0.4 shard_map.96
  8.1 1.5 %collective-permute-start.3 = (bf16[96,512]{1,0:T(8,128)(2,1)S(1)}, bf16[96,512]{1,0:T(8,128)(2,1)S(1)}, u32[]{:S(2)}, u32[]{:S(2)}) collective-permute-start(bf16[96,512]{1,0:T(8,128)(2,1)S(1)} %get-tuple-element.43), channel_id=1, source_target_pairs={{0,8},{8,0},{16,24},{24,16},{1,9},{9,1},{17,25},{25,17},{2,10},{10... | collective-permute-start | bytes 294920 | tf_op jit(solution)/shard_map/ppermute | solution.py:392
  9.6 2.4 %collective-permute-start.4 = (bf16[96,512]{1,0:T(8,128)(2,1)S(1)}, bf16[96,512]{1,0:T(8,128)(2,1)S(1)}, u32[]{:S(2)}, u32[]{:S(2)}) collective-permute-start(bf16[96,512]{1,0:T(8,128)(2,1)S(1)} %get-tuple-element.44), channel_id=1, source_target_pairs={{0,24},{8,16},{16,8},{24,0},{1,25},{9,17},{17,9},{25,1},{2,26},{10... | collective-permute-start | bytes 294920 | tf_op jit(solution)/shard_map/ppermute | solution.py:392
  12.0 0.0 collective-permute-done.refs_0_
  12.0 0.5 %collective-permute-start.5 = (bf16[96,512]{1,0:T(8,128)(2,1)S(1)}, bf16[96,512]{1,0:T(8,128)(2,1)S(1)}, u32[]{:S(2)}, u32[]{:S(2)}) collective-permute-start(bf16[96,512]{1,0:T(8,128)(2,1)S(1)} %get-tuple-element.45), channel_id=1, source_target_pairs={{0,16},{8,24},{16,0},{24,8},{1,17},{9,25},{17,1},{25,9},{2,18},{10... | collective-permute-start | bytes 294920 | tf_op jit(solution)/shard_map/ppermute | solution.py:392
  12.5 8.6 %all_gather.3.sequence_ref = bf16[1536,256]{1,0:T(8,128)(2,1)S(1)} all-gather(bf16[384,256]{1,0:T(8,128)(2,1)S(1)} %shard_map.95), channel_id=1, replica_groups=mesh['dp'=4,'seq'=4,'head'=2] {'seq'}, dimensions={0}, use_global_device_ids=true | all-gather | bytes 983040 | tf_op jit(solution)/shard_map/all_gather | solution.py:404
  21.1 0.0 collective-permute-done.3.refs_0_
  21.2 1.3 %shard_map.97 = (bf16[768,256]{1,0:T(8,128)(2,1)S(1)}, bf16[768,256]{1,0:T(8,128)(2,1)S(1)}, bf16[1536,768]{1,0:T(8,128)(2,1)S(1)}, bf16[1536,768]{1,0:T(8,128)(2,1)S(1)}) custom-call(bf16[1536,256]{1,0:T(8,128)(2,1)S(1)} %all_gather.3.sequence_ref, s32[1,768]{1,0:T(1,128)S(1)} %get-tuple-element.40.first_ref, ...), custom_call_target="tpu_custom_call" | custom-call | tf_op jit(solution)/shard_map/pallas_call | solution.py:337
  22.5 1.1 %collective-permute-start.9 = (bf16[768,256]{1,0:T(8,128)(2,1)S(1)}, bf16[768,256]{1,0:T(8,128)(2,1)S(1)}, u32[]{:S(2)}, u32[]{:S(2)}) collective-permute-start(bf16[768,256]{1,0:T(8,128)(2,1)S(1)} %get-tuple-element.56), channel_id=1, source_target_pairs={{0,2},{2,0},{4,6},{6,4},{1,3},{3,1},{5,7},{7,5},{8,10},{10,8},{12,... | collective-permute-start | bytes 1179656 | tf_op jit(solution)/shard_map/ppermute | solution.py:396
  23.6 0.5 %shard_map.98 = (bf16[96,512]{1,0:T(8,128)(2,1)S(1)}, bf16[96,512]{1,0:T(8,128)(2,1)S(1)}, bf16[96,512]{1,0:T(8,128)(2,1)S(1)}, bf16[96,512]{1,0:T(8,128)(2,1)S(1)}) custom-call(bf16[1536,256]{1,0:T(8,128)(2,1)S(1)} %all_gather.3.sequence_ref, bf16[1536,768]{1,0:T(8,128)(2,1)S(1)} %get-tuple-element.47.low_ref, bf16[1536,768]{1,0:T(8,128)(2,1)S(1)} %get-tuple-element.48.ds_ref), custom_call_target="tpu_custom_call" | custom-call | tf_op jit(solution)/shard_map/pallas_call | solution.py:337
  24.1 2.5 %collective-permute-start.6 = (bf16[96,512]{1,0:T(8,128)(2,1)S(1)}, bf16[96,512]{1,0:T(8,128)(2,1)S(1)}, u32[]{:S(2)}, u32[]{:S(2)}) collective-permute-start(bf16[96,512]{1,0:T(8,128)(2,1)S(1)} %get-tuple-element.49), channel_id=1, source_target_pairs={{16,0},{24,8},{0,16},{8,24},{17,1},{25,9},{1,17},{9,25},{18,2},{26... | collective-permute-start | bytes 294920 | tf_op jit(solution)/shard_map/ppermute | solution.py:392
  26.6 0.1 shard_map.100
  26.7 2.4 %collective-permute-start.10 = (bf16[192,256]{1,0:T(8,128)(2,1)S(1)}, bf16[192,256]{1,0:T(8,128)(2,1)S(1)}, u32[]{:S(2)}, u32[]{:S(2)}) collective-permute-start(bf16[192,256]{1,0:T(8,128)(2,1)S(1)} %get-tuple-element.58), channel_id=1, source_target_pairs={{0,4},{2,6},{4,0},{6,2},{1,5},{3,7},{5,1},{7,3},{8,12},{10,14},{12... | collective-permute-start | bytes 294920 | tf_op jit(solution)/shard_map/ppermute | solution.py:396
  29.1 0.1 collective-permute-start.11
  29.2 1.6 %collective-permute-start.7 = (bf16[96,512]{1,0:T(8,128)(2,1)S(1)}, bf16[96,512]{1,0:T(8,128)(2,1)S(1)}, u32[]{:S(2)}, u32[]{:S(2)}) collective-permute-start(bf16[96,512]{1,0:T(8,128)(2,1)S(1)} %get-tuple-element.50), channel_id=1, source_target_pairs={{24,0},{16,8},{8,16},{0,24},{25,1},{17,9},{9,17},{1,25},{26,2},{18... | collective-permute-start | bytes 294920 | tf_op jit(solution)/shard_map/ppermute | solution.py:392
  30.7 1.5 %collective-permute-done.6.refs_0_.refs_2_ = bf16[96,512]{1,0:T(8,128)(2,1)S(1)} collective-permute-done((bf16[96,512]{1,0:T(8,128)(2,1)S(1)}, bf16[96,512]{1,0:T(8,128)(2,1)S(1)}, u32[]{:S(2)}, u32[]{:S(2)}) %collective-permute-start.6) | collective-permute-done | bytes 98336 | tf_op jit(solution)/shard_map/ppermute | solution.py:392
  32.3 0.3 collective-permute-done.10.refs_0_
  32.6 1.4 %collective-permute-done.11.refs_1_ = bf16[192,256]{1,0:T(8,128)(2,1)S(1)} collective-permute-done((bf16[192,256]{1,0:T(8,128)(2,1)S(1)}, bf16[192,256]{1,0:T(8,128)(2,1)S(1)}, u32[]{:S(2)}, u32[]{:S(2)}) %collective-permute-start.11) | collective-permute-done | bytes 98336 | tf_op jit(solution)/shard_map/ppermute | solution.py:396
  34.1 1.0 %collective-permute-start.12 = (bf16[96,256]{1,0:T(8,128)(2,1)S(1)}, bf16[96,256]{1,0:T(8,128)(2,1)S(1)}, u32[]{:S(2)}, u32[]{:S(2)}) collective-permute-start(bf16[96,256]{1,0:T(8,128)(2,1)S(1)} %get-tuple-element.60), channel_id=1, source_target_pairs={{16,0},{24,8},{0,16},{8,24},{17,1},{25,9},{1,17},{9,25},{18,2},{26... | collective-permute-start | bytes 147464 | tf_op jit(solution)/shard_map/ppermute | solution.py:392
  35.1 2.5 %collective-permute-start.13 = (bf16[96,256]{1,0:T(8,128)(2,1)S(1)}, bf16[96,256]{1,0:T(8,128)(2,1)S(1)}, u32[]{:S(2)}, u32[]{:S(2)}) collective-permute-start(bf16[96,256]{1,0:T(8,128)(2,1)S(1)} %get-tuple-element.61), channel_id=1, source_target_pairs={{24,0},{16,8},{8,16},{0,24},{25,1},{17,9},{9,17},{1,25},{26,2},{18... | collective-permute-start | bytes 147464 | tf_op jit(solution)/shard_map/ppermute | solution.py:392
  37.5 0.1 collective-permute-start.14
  37.6 0.2 shard_map.94.back_ref
  37.8 1.1 %shard_map.99 = (bf16[360,256]{1,0:T(8,128)(2,1)}, bf16[360,256]{1,0:T(8,128)(2,1)}) custom-call(bf16[360,384]{1,0:T(8,128)(2,1)S(1)} %shard_map.94.back_ref, bf16[96,512]{1,0:T(8,128)(2,1)S(1)} %collective-permute-done.6.refs_0_.refs_2_, bf16[96,512]{1,0:T(8,128)(2,1)S(1)} %collective-permute-done.7.refs_1_, ...), custom_call_target="tpu_custom_call" | custom-call | tf_op jit(solution)/shard_map/pallas_call | solution.py:337
  38.9 1.2 %collective-permute-done.12.refs_0_ = bf16[96,256]{1,0:T(8,128)(2,1)S(1)} collective-permute-done((bf16[96,256]{1,0:T(8,128)(2,1)S(1)}, bf16[96,256]{1,0:T(8,128)(2,1)S(1)}, u32[]{:S(2)}, u32[]{:S(2)}) %collective-permute-start.12) | collective-permute-done | bytes 49184 | tf_op jit(solution)/shard_map/ppermute | solution.py:392
  40.2 0.9 %collective-permute-done.13.refs_1_ = bf16[96,256]{1,0:T(8,128)(2,1)S(1)} collective-permute-done((bf16[96,256]{1,0:T(8,128)(2,1)S(1)}, bf16[96,256]{1,0:T(8,128)(2,1)S(1)}, u32[]{:S(2)}, u32[]{:S(2)}) %collective-permute-start.13) | collective-permute-done | bytes 49184 | tf_op jit(solution)/shard_map/ppermute | solution.py:392
  41.0 0.6 %collective-permute-done.14.refs_2_ = bf16[96,256]{1,0:T(8,128)(2,1)S(1)} collective-permute-done((bf16[96,256]{1,0:T(8,128)(2,1)S(1)}, bf16[96,256]{1,0:T(8,128)(2,1)S(1)}, u32[]{:S(2)}, u32[]{:S(2)}) %collective-permute-start.14) | collective-permute-done | bytes 49184 | tf_op jit(solution)/shard_map/ppermute | solution.py:392
  41.6 0.9 %shard_map.102 = (bf16[360,128]{1,0:T(8,128)(2,1)}, bf16[360,128]{1,0:T(8,128)(2,1)}) custom-call(bf16[360,384]{1,0:T(8,128)(2,1)S(1)} %shard_map.94.back_ref, bf16[96,256]{1,0:T(8,128)(2,1)S(1)} %collective-permute-done.12.refs_0_, bf16[96,256]{1,0:T(8,128)(2,1)S(1)} %collective-permute-done.13.refs_1_, ...), custom_call_target="tpu_custom_call" | custom-call | tf_op jit(solution)/shard_map/pallas_call | solution.py:337
  (13 shorter events, 0.1 us)
Async XLA Ops:
  2.0 6.1 %copy-start = (s32[1,360]{1,0:T(1,128)}, s32[1,360]{1,0:T(1,128)S(1)}, u32[]{:S(2)}) copy-start(s32[1,360]{1,0:T(1,128)S(1)} %get-tuple-element.35.slot_ref) | copy-start | bytes 4324
  2.0 10.0 %collective-permute-start = (bf16[96,256]{1,0:T(8,128)(2,1)S(1)}, bf16[96,256]{1,0:T(8,128)(2,1)S(1)}, u32[]{:S(2)}, u32[]{:S(2)}) collective-permute-start(bf16[96,256]{1,0:T(8,128)(2,1)S(1)} %get-tuple-element.36), channel_id=1, source_target_pairs={{0,24},{8,16},{16,8},{24,0},{1,25},{9,17},{17,9},{25,1},{2,26},{10... | collective-permute-start | bytes 147464 | tf_op jit(solution)/shard_map/ppermute | solution.py:392
  7.1 5.4 %collective-permute-start.1 = (bf16[96,256]{1,0:T(8,128)(2,1)S(1)}, bf16[96,256]{1,0:T(8,128)(2,1)S(1)}, u32[]{:S(2)}, u32[]{:S(2)}) collective-permute-start(bf16[96,256]{1,0:T(8,128)(2,1)S(1)} %get-tuple-element.37), channel_id=1, source_target_pairs={{0,16},{8,24},{16,0},{24,8},{1,17},{9,25},{17,1},{25,9},{2,18},{10... | collective-permute-start | bytes 147464 | tf_op jit(solution)/shard_map/ppermute | solution.py:392
  7.1 5.4 %collective-permute-start.2 = (bf16[96,256]{1,0:T(8,128)(2,1)S(1)}, bf16[96,256]{1,0:T(8,128)(2,1)S(1)}, u32[]{:S(2)}, u32[]{:S(2)}) collective-permute-start(bf16[96,256]{1,0:T(8,128)(2,1)S(1)} %get-tuple-element.38), channel_id=1, source_target_pairs={{0,8},{8,0},{16,24},{24,16},{1,9},{9,1},{17,25},{25,17},{2,10},{10... | collective-permute-start | bytes 147464 | tf_op jit(solution)/shard_map/ppermute | solution.py:392
  8.1 13.0 %collective-permute-start.3 = (bf16[96,512]{1,0:T(8,128)(2,1)S(1)}, bf16[96,512]{1,0:T(8,128)(2,1)S(1)}, u32[]{:S(2)}, u32[]{:S(2)}) collective-permute-start(bf16[96,512]{1,0:T(8,128)(2,1)S(1)} %get-tuple-element.43), channel_id=1, source_target_pairs={{0,8},{8,0},{16,24},{24,16},{1,9},{9,1},{17,25},{25,17},{2,10},{10... | collective-permute-start | bytes 294920 | tf_op jit(solution)/shard_map/ppermute | solution.py:392
  9.6 11.6 %collective-permute-start.4 = (bf16[96,512]{1,0:T(8,128)(2,1)S(1)}, bf16[96,512]{1,0:T(8,128)(2,1)S(1)}, u32[]{:S(2)}, u32[]{:S(2)}) collective-permute-start(bf16[96,512]{1,0:T(8,128)(2,1)S(1)} %get-tuple-element.44), channel_id=1, source_target_pairs={{0,24},{8,16},{16,8},{24,0},{1,25},{9,17},{17,9},{25,1},{2,26},{10... | collective-permute-start | bytes 294920 | tf_op jit(solution)/shard_map/ppermute | solution.py:392
  12.0 9.1 %collective-permute-start.5 = (bf16[96,512]{1,0:T(8,128)(2,1)S(1)}, bf16[96,512]{1,0:T(8,128)(2,1)S(1)}, u32[]{:S(2)}, u32[]{:S(2)}) collective-permute-start(bf16[96,512]{1,0:T(8,128)(2,1)S(1)} %get-tuple-element.45), channel_id=1, source_target_pairs={{0,16},{8,24},{16,0},{24,8},{1,17},{9,25},{17,1},{25,9},{2,18},{10... | collective-permute-start | bytes 294920 | tf_op jit(solution)/shard_map/ppermute | solution.py:392
  22.5 4.2 %collective-permute-start.9 = (bf16[768,256]{1,0:T(8,128)(2,1)S(1)}, bf16[768,256]{1,0:T(8,128)(2,1)S(1)}, u32[]{:S(2)}, u32[]{:S(2)}) collective-permute-start(bf16[768,256]{1,0:T(8,128)(2,1)S(1)} %get-tuple-element.56), channel_id=1, source_target_pairs={{0,2},{2,0},{4,6},{6,4},{1,3},{3,1},{5,7},{7,5},{8,10},{10,8},{12,... | collective-permute-start | bytes 1179656 | tf_op jit(solution)/shard_map/ppermute | solution.py:396
  24.1 8.1 %collective-permute-start.6 = (bf16[96,512]{1,0:T(8,128)(2,1)S(1)}, bf16[96,512]{1,0:T(8,128)(2,1)S(1)}, u32[]{:S(2)}, u32[]{:S(2)}) collective-permute-start(bf16[96,512]{1,0:T(8,128)(2,1)S(1)} %get-tuple-element.49), channel_id=1, source_target_pairs={{16,0},{24,8},{0,16},{8,24},{17,1},{25,9},{1,17},{9,25},{18,2},{26... | collective-permute-start | bytes 294920 | tf_op jit(solution)/shard_map/ppermute | solution.py:392
  26.7 5.9 %collective-permute-start.10 = (bf16[192,256]{1,0:T(8,128)(2,1)S(1)}, bf16[192,256]{1,0:T(8,128)(2,1)S(1)}, u32[]{:S(2)}, u32[]{:S(2)}) collective-permute-start(bf16[192,256]{1,0:T(8,128)(2,1)S(1)} %get-tuple-element.58), channel_id=1, source_target_pairs={{0,4},{2,6},{4,0},{6,2},{1,5},{3,7},{5,1},{7,3},{8,12},{10,14},{12... | collective-permute-start | bytes 294920 | tf_op jit(solution)/shard_map/ppermute | solution.py:396
  29.1 4.9 %collective-permute-start.11 = (bf16[192,256]{1,0:T(8,128)(2,1)S(1)}, bf16[192,256]{1,0:T(8,128)(2,1)S(1)}, u32[]{:S(2)}, u32[]{:S(2)}) collective-permute-start(bf16[192,256]{1,0:T(8,128)(2,1)S(1)} %get-tuple-element.59), channel_id=1, source_target_pairs={{0,4},{2,6},{4,0},{6,2},{1,5},{3,7},{5,1},{7,3},{8,12},{10,14},{12... | collective-permute-start | bytes 294920 | tf_op jit(solution)/shard_map/ppermute | solution.py:396
  29.2 8.6 %collective-permute-start.7 = (bf16[96,512]{1,0:T(8,128)(2,1)S(1)}, bf16[96,512]{1,0:T(8,128)(2,1)S(1)}, u32[]{:S(2)}, u32[]{:S(2)}) collective-permute-start(bf16[96,512]{1,0:T(8,128)(2,1)S(1)} %get-tuple-element.50), channel_id=1, source_target_pairs={{24,0},{16,8},{8,16},{0,24},{25,1},{17,9},{9,17},{1,25},{26,2},{18... | collective-permute-start | bytes 294920 | tf_op jit(solution)/shard_map/ppermute | solution.py:392
  30.7 7.1 %collective-permute-start.8 = (bf16[96,512]{1,0:T(8,128)(2,1)S(1)}, bf16[96,512]{1,0:T(8,128)(2,1)S(1)}, u32[]{:S(2)}, u32[]{:S(2)}) collective-permute-start(bf16[96,512]{1,0:T(8,128)(2,1)S(1)} %get-tuple-element.51), channel_id=1, source_target_pairs={{8,0},{0,8},{24,16},{16,24},{9,1},{1,9},{25,17},{17,25},{10,2},{2,... | collective-permute-start | bytes 294920 | tf_op jit(solution)/shard_map/ppermute | solution.py:392
  34.0 3.6 %copy-start.1 = (s32[1,360]{1,0:T(1,128)S(1)}, s32[1,360]{1,0:T(1,128)}, u32[]{:S(2)}) copy-start(s32[1,360]{1,0:T(1,128)} %copy-done) | copy-start | bytes 4324
  34.1 6.1 %collective-permute-start.12 = (bf16[96,256]{1,0:T(8,128)(2,1)S(1)}, bf16[96,256]{1,0:T(8,128)(2,1)S(1)}, u32[]{:S(2)}, u32[]{:S(2)}) collective-permute-start(bf16[96,256]{1,0:T(8,128)(2,1)S(1)} %get-tuple-element.60), channel_id=1, source_target_pairs={{16,0},{24,8},{0,16},{8,24},{17,1},{25,9},{1,17},{9,25},{18,2},{26... | collective-permute-start | bytes 147464 | tf_op jit(solution)/shard_map/ppermute | solution.py:392
  35.1 6.0 %collective-permute-start.13 = (bf16[96,256]{1,0:T(8,128)(2,1)S(1)}, bf16[96,256]{1,0:T(8,128)(2,1)S(1)}, u32[]{:S(2)}, u32[]{:S(2)}) collective-permute-start(bf16[96,256]{1,0:T(8,128)(2,1)S(1)} %get-tuple-element.61), channel_id=1, source_target_pairs={{24,0},{16,8},{8,16},{0,24},{25,1},{17,9},{9,17},{1,25},{26,2},{18... | collective-permute-start | bytes 147464 | tf_op jit(solution)/shard_map/ppermute | solution.py:392
  37.5 4.1 %collective-permute-start.14 = (bf16[96,256]{1,0:T(8,128)(2,1)S(1)}, bf16[96,256]{1,0:T(8,128)(2,1)S(1)}, u32[]{:S(2)}, u32[]{:S(2)}) collective-permute-start(bf16[96,256]{1,0:T(8,128)(2,1)S(1)} %get-tuple-element.62), channel_id=1, source_target_pairs={{8,0},{0,8},{24,16},{16,24},{9,1},{1,9},{25,17},{17,25},{10,2},{2,... | collective-permute-start | bytes 147464 | tf_op jit(solution)/shard_map/ppermute | solution.py:392
